TPU v7x, 32 devices: a whole 2x2x4 slice. The times are simulated.
32 devices in a mesh: wide: 16 (over z, y, core), narrow: 2 (over x).
Axes of the slice: x: 2, y: 2, z: 4, core: 2. Of those that a mesh axis runs over, the one named last changes fastest.
Arguments:
- tokens: bfloat16 [2, 8192, 768], P(None, 'wide'), may hold values from -6 to 6
- segments: int32 [2, 8192], P(None, 'wide'), may hold values from -1 to 7, as said below
- query_weight: bfloat16 [768, 768], P(None, 'narrow'), may hold values from -0.21875 to 0.21875
- key_weight: bfloat16 [768, 768], P(None, 'narrow'), may hold values from -0.21875 to 0.21875
- value_weight: bfloat16 [768, 768], P(None, 'narrow'), may hold values from -0.21875 to 0.21875
- output_weight: bfloat16 [768, 768], P('narrow'), may hold values from -0.875 to 0.875
- expand_weight: bfloat16 [768, 3072], P(None, 'narrow'), may hold values from -0.21875 to 0.21875
- reduce_weight: bfloat16 [3072, 768], P('narrow'), may hold values from -0.109375 to 0.109375
- heads_bias: float32 [3, 768], P(None, 'narrow'), may hold values from -1.8 to 1.8
- model_bias: float32 [6, 768], replicated, may hold values from -1.8 to 1.8
- hidden_bias: float32 [3072], P('narrow'), may hold values from -1.8 to 1.8
- mentor_query: bfloat16 [768, 768], P(None, 'narrow'), may hold values from -0.21875 to 0.21875
- mentor_key: bfloat16 [768, 768], P(None, 'narrow'), may hold values from -0.21875 to 0.21875
- mentor_value: bfloat16 [768, 768], P(None, 'narrow'), may hold values from -0.21875 to 0.21875
- mentor_output: bfloat16 [768, 768], P('narrow'), may hold values from -0.875 to 0.875
- mentor_expand: bfloat16 [768, 3072], P(None, 'narrow'), may hold values from -0.21875 to 0.21875
- mentor_reduce: bfloat16 [3072, 768], P('narrow'), may hold values from -0.109375 to 0.109375
- mentor_heads: float32 [3, 768], P(None, 'narrow'), may hold values from -1.8 to 1.8
- mentor_model: float32 [6, 768], replicated, may hold values from -1.8 to 1.8
- mentor_hidden: float32 [3072], P('narrow'), may hold values from -1.8 to 1.8
Outputs:
- student_out: bfloat16 [2, 8192, 768], P(None, 'wide')
- grad_tokens: float32 [2, 8192, 768], P(None, 'wide')
- grad_query: float32 [768, 768], P(None, 'narrow')
- grad_key: float32 [768, 768], P(None, 'narrow')
- grad_value: float32 [768, 768], P(None, 'narrow')
- grad_output: float32 [768, 768], P('narrow')
- grad_expand: float32 [768, 3072], P(None, 'narrow')
- grad_reduce: float32 [3072, 768], P('narrow')
- grad_heads: float32 [3, 768], P(None, 'narrow')
- grad_model: float32 [6, 768], replicated
- grad_hidden: float32 [3072], P('narrow')
Inputs may be any that keep to these rules, and one draw needn't show every extreme that they name: `segments`: within each device's 512 slots of a micro-batch, slots come in regions of 256; a live region holds examples of one length (64, 128 or 256) numbered 4 * region + place in order; padding regions (-1) follow the live ones and each device's first region is live; in every draw some device's slots hold no padding.
All inputs are finite; a program needn't handle non-finite values.
Results may differ from a plain program's by a relative error of at most 0.0078.
Values sent between devices are 32-bit elements; how exact they have to be, the bound alone decides.
No kernel may reach another device: no remote copies, remote signals or barrier semaphores. Data moves between devices by JAX's collectives and lax.ppermute only.
A program may use at most 192 MiB of HBM per device.

v0:
```python
import jax
import jax.numpy as jnp
from jax import lax
from jax.sharding import PartitionSpec as P

HEAD = 64


norm_eps = 1e-06
score_weight = 0.05
big_negative = -1e30


def matmul(left, right):
    return jnp.dot(left, right, preferred_element_type=jnp.float32)


def contract_rows(left, right):
    return lax.dot_general(
        left, right, (((0,), (0,)), ((), ())), preferred_element_type=jnp.float32
    )


def contract_cols(left, right):
    return lax.dot_general(
        left, right, (((1,), (1,)), ((), ())), preferred_element_type=jnp.float32
    )


def split_heads(values):
    return values.reshape(values.shape[0], values.shape[1] // HEAD, HEAD)


def layer_norm(values, gain, shift):
    centred = values - jnp.mean(values, axis=-1, keepdims=True)
    spread = jnp.mean(centred * centred, axis=-1, keepdims=True)
    return centred * lax.rsqrt(spread + norm_eps) * (1.0 + gain) + shift


def gelu_exact(values):
    return jax.nn.gelu(values, approximate=False)


def binarize(weight, axis):
    widened = weight.astype(jnp.float32)
    alpha = jnp.mean(jnp.abs(widened), axis=axis, keepdims=True)
    return (alpha * jnp.sign(widened)).astype(jnp.bfloat16)


def scores_of(query, keys):
    return jnp.einsum(
        "qhd,khd->hqk", split_heads(query), split_heads(keys), preferred_element_type=jnp.float32
    ) * HEAD ** (-0.5)


def front(inputs, params):
    query = (matmul(inputs, params[0]) + params[6][0]).astype(jnp.bfloat16)
    keys = (matmul(inputs, params[1]) + params[6][1]).astype(jnp.bfloat16)
    values = (matmul(inputs, params[2]) + params[6][2]).astype(jnp.bfloat16)
    return (query, keys, values)


def attend(query, keys, values, allowed):
    masked = jnp.where(allowed, scores_of(query, keys), big_negative)
    top = jnp.max(masked, axis=-1, keepdims=True)
    expo = jnp.exp(masked - top)
    total = jnp.sum(expo, axis=-1, keepdims=True)
    probs = (expo / total).astype(jnp.bfloat16)
    mixed = jnp.einsum(
        "hqk,khd->qhd", probs, split_heads(values), preferred_element_type=jnp.float32
    )
    return (mixed.reshape(query.shape).astype(jnp.bfloat16), top + jnp.log(total))


def micro_step(inputs, segment, student, teacher):
    rows = inputs.shape[0]
    resident = inputs.astype(jnp.float32)
    same_doc = segment[:, None] == segment[None, :]
    live_row = segment >= 0
    diagonal = jnp.arange(rows)[:, None] == jnp.arange(rows)[None, :]
    allowed = same_doc & (live_row[:, None] | diagonal)
    pairs = (same_doc & live_row[:, None]).astype(jnp.float32)
    query_s, keys_s, values_s = front(inputs, student)
    query_t, keys_t, values_t = front(inputs, teacher)
    mixed_s, lse_s = attend(query_s, keys_s, values_s, allowed)
    mixed_t, unused = attend(query_t, keys_t, values_t, allowed)
    attn_s, attn_t = lax.psum((matmul(mixed_s, student[3]), matmul(mixed_t, teacher[3])), "narrow")
    model_s = student[7]
    model_t = teacher[7]
    pre_s = resident + attn_s + model_s[0]
    first_s, first_back = jax.vjp(layer_norm, pre_s, model_s[2], model_s[3])
    first_t = layer_norm(resident + attn_t + model_t[0], model_t[2], model_t[3])
    first_low = first_s.astype(jnp.bfloat16)
    upward_s = matmul(first_low, student[4]) + student[8]
    active_s, gelu_back = jax.vjp(gelu_exact, upward_s)
    active_low = active_s.astype(jnp.bfloat16)
    active_t = gelu_exact(matmul(first_t.astype(jnp.bfloat16), teacher[4]) + teacher[8]).astype(
        jnp.bfloat16
    )
    down_s, down_t = lax.psum(
        (matmul(active_low, student[5]), matmul(active_t, teacher[5])), "narrow"
    )
    out_s, second_back = jax.vjp(layer_norm, first_s + down_s + model_s[1], model_s[4], model_s[5])
    out_t = layer_norm(first_t + down_t + model_t[1], model_t[4], model_t[5])
    d_out = jnp.where(live_row[:, None], out_s - out_t, 0.0)
    d_pre2, d_gain2, d_shift2 = second_back(d_out)
    d_down = d_pre2.astype(jnp.bfloat16)
    grad_reduce = contract_rows(active_low, d_down)
    d_active = contract_cols(d_down, student[5])
    d_upward = gelu_back(d_active)[0].astype(jnp.bfloat16)
    grad_expand = contract_rows(first_low, d_upward)
    d_first = lax.psum(contract_cols(d_upward, student[4]), "narrow") + d_pre2
    d_pre1, d_gain1, d_shift1 = first_back(d_first)
    d_attn = d_pre1.astype(jnp.bfloat16)
    grad_output = contract_rows(mixed_s, d_attn)
    d_mixed = contract_cols(d_attn, student[3]).astype(jnp.bfloat16)
    scores = scores_of(query_s, keys_s)
    probs = jnp.exp(jnp.where(allowed, scores, big_negative) - lse_s)
    heads_grad = split_heads(d_mixed)
    d_probs = jnp.einsum(
        "qhd,khd->hqk", heads_grad, split_heads(values_s), preferred_element_type=jnp.float32
    )
    d_values = jnp.einsum(
        "hqk,qhd->khd", probs.astype(jnp.bfloat16), heads_grad, preferred_element_type=jnp.float32
    )
    d_values = d_values.reshape(values_s.shape).astype(jnp.bfloat16)
    d_scores = probs * (d_probs - jnp.sum(probs * d_probs, axis=-1, keepdims=True))
    d_scores = d_scores + score_weight * pairs[None, :, :] * (scores - scores_of(query_t, keys_t))
    d_scores = d_scores.astype(jnp.bfloat16)
    d_query = jnp.einsum(
        "hqk,khd->qhd", d_scores, split_heads(keys_s), preferred_element_type=jnp.float32
    ) * HEAD ** (-0.5)
    d_query = d_query.reshape(query_s.shape).astype(jnp.bfloat16)
    d_keys = jnp.einsum(
        "hqk,qhd->khd", d_scores, split_heads(query_s), preferred_element_type=jnp.float32
    ) * HEAD ** (-0.5)
    d_keys = d_keys.reshape(keys_s.shape).astype(jnp.bfloat16)
    partial_in = (
        contract_cols(d_query, student[0])
        + contract_cols(d_keys, student[1])
        + contract_cols(d_values, student[2])
    )
    d_tokens = lax.psum(partial_in, "narrow") + d_pre1
    grad_query = contract_rows(inputs, d_query)
    grad_key = contract_rows(inputs, d_keys)
    grad_value = contract_rows(inputs, d_values)
    grad_heads = jnp.stack(
        [
            jnp.sum(d_query.astype(jnp.float32), axis=0),
            jnp.sum(d_keys.astype(jnp.float32), axis=0),
            jnp.sum(d_values.astype(jnp.float32), axis=0),
        ]
    )
    grad_model = jnp.stack(
        [
            jnp.sum(d_attn.astype(jnp.float32), axis=0),
            jnp.sum(d_down.astype(jnp.float32), axis=0),
            d_gain1,
            d_shift1,
            d_gain2,
            d_shift2,
        ]
    )
    grad_hidden = jnp.sum(d_upward.astype(jnp.float32), axis=0)
    grads = (
        grad_query,
        grad_key,
        grad_value,
        grad_output,
        grad_expand,
        grad_reduce,
        grad_heads,
        grad_model,
        grad_hidden,
    )
    return (out_s.astype(jnp.bfloat16), d_tokens, grads)


def on_device(
    tokens,
    segments,
    query_weight,
    key_weight,
    value_weight,
    output_weight,
    expand_weight,
    reduce_weight,
    heads_bias,
    model_bias,
    hidden_bias,
    mentor_query,
    mentor_key,
    mentor_value,
    mentor_output,
    mentor_expand,
    mentor_reduce,
    mentor_heads,
    mentor_model,
    mentor_hidden,
):
    student = (
        binarize(query_weight, 0),
        binarize(key_weight, 0),
        binarize(value_weight, 0),
        binarize(output_weight, 1),
        binarize(expand_weight, 0),
        binarize(reduce_weight, 1),
        heads_bias,
        model_bias,
        hidden_bias,
    )
    teacher = (
        mentor_query,
        mentor_key,
        mentor_value,
        mentor_output,
        mentor_expand,
        mentor_reduce,
        mentor_heads,
        mentor_model,
        mentor_hidden,
    )
    outputs = []
    d_rows = []
    totals = None
    for index in range(tokens.shape[0]):
        out_row, d_row, grads = micro_step(tokens[index], segments[index], student, teacher)
        if totals is None:
            totals = tuple(grads)
        else:
            totals = tuple(jax.tree.map(jnp.add, tuple(totals), tuple(grads)))
        outputs.append(out_row)
        d_rows.append(d_row)
    totals = lax.psum(
        (
            totals[0],
            totals[1],
            totals[2],
            totals[3],
            totals[4],
            totals[5],
            totals[6],
            totals[7],
            totals[8],
        ),
        "wide",
    )
    return (
        jnp.stack(outputs),
        jnp.stack(d_rows),
        totals[0],
        totals[1],
        totals[2],
        totals[3],
        totals[4],
        totals[5],
        totals[6],
        totals[7],
        totals[8],
    )


def solution(mesh):
    placed = (
        P(None, "wide", None),
        P(None, "wide"),
        P(None, "narrow"),
        P(None, "narrow"),
        P(None, "narrow"),
        P("narrow", None),
        P(None, "narrow"),
        P("narrow", None),
        P(None, "narrow"),
        P(),
        P("narrow"),
        P(None, "narrow"),
        P(None, "narrow"),
        P(None, "narrow"),
        P("narrow", None),
        P(None, "narrow"),
        P("narrow", None),
        P(None, "narrow"),
        P(),
        P("narrow"),
    )
    return jax.shard_map(
        on_device,
        mesh=mesh,
        in_specs=placed,
        out_specs=(
            P(None, "wide", None),
            P(None, "wide", None),
            P(None, "narrow"),
            P(None, "narrow"),
            P(None, "narrow"),
            P("narrow", None),
            P(None, "narrow"),
            P("narrow", None),
            P(None, "narrow"),
            P(),
            P("narrow"),
        ),
        check_vma=False,
    )
```

profile of v0, /device:TPU:0, one launch (start us, length us, event | category | flops | bytes accessed | tf_op | source)
XLA Modules:
  0.0 1028.9 jit_solution(8906816964118637664)
XLA Ops:
  39.6 6.1 fusion.424
  45.7 3.6 fusion.178
  51.1 6.1 fusion.425
  66.4 153.4 %all-reduce.20.cloned.1.call-done = (f32[512,768]{1,0:T(8,128)}, f32[512,768]{1,0:T(8,128)}, f32[512,768]{1,0:T(8,128)}, f32[512,768]{1,0:T(8,128)}) async-done(((f32[512,768]{1,0:T(8,128)}, f32[512,768]{1,0:T(8,128)}, f32[512,768]{1,0:T(8,128)}, f32[512,768]{1,0:T(8,128)}), (f32[512,768]{1,0:T(8,128)}, f32[512,768]{1,0:T(8,128)}, f32[512,768]{1,0:T(8,128)}, ...) | async-done | bytes 6291472 | tf_op jit(solution)/shard_map/psum | solution.py:87
  223.5 5.0 multiply_reduce_fusion.13
  228.6 12.6 %fusion.128 = f32[512,768]{1,0:T(8,128)} fusion(bf16[1536,768]{1,0:T(8,128)(2,1)S(1)} %copy-done, bf16[768,1536]{1,0:T(8,128)(2,1)} %param.35, f32[1536]{0:T(1024)S(1)} %copy-done.137, f32[768]{0:T(1024)S(1)} %get-tuple-element.40, f32[768]{0:T(1024)S(1)} %get-tuple-element.41, f32[512]{0:T(512)S(1)} %add_rsqrt_fusion.3, f32[512]{0:T(512)S(1)} %get-tuple-element.167, ...), kind=kOutput, calls=%fused_computation.236 | convolution fusion | flops 2470969344 | bytes 8670208 | tf_op jit(solution)/shard_map/dot_general | solution.py:15
  241.1 12.4 %fusion.127 = f32[512,768]{1,0:T(8,128)} fusion(bf16[1536,768]{1,0:T(8,128)(2,1)S(1)} %copy-done, bf16[768,1536]{1,0:T(8,128)(2,1)} %param.35, f32[1536]{0:T(1024)S(1)} %copy-done.137, f32[512]{0:T(512)S(1)} %add_rsqrt_fusion.1, f32[512]{0:T(512)S(1)} %get-tuple-element.166, f32[768]{0:T(1024)S(1)} %get-tuple-element.40, f32[768]{0:T(1024)S(1)} %get-tuple-element.41, ...), kind=kOutput, calls=%fused_computation.235 | convolution fusion | flops 2470969344 | bytes 8670208 | tf_op jit(solution)/shard_map/dot_general | solution.py:15
  257.7 14.1 %multiply_convert_fusion.1 = (bf16[512,1536]{1,0:T(8,128)(2,1)S(1)}, f32[512,1536]{1,0:T(8,128)}, f32[512,1536]{1,0:T(8,128)}) fusion(f32[1536]{0:T(1024)S(1)} %copy-done.138, bf16[768,1536]{1,0:T(8,128)(2,1)} %param.26, f32[1536]{0:T(1024)S(1)} %broadcast_multiply_fusion.1, f32[512,768]{1,0:T(8,128)S(1)} %copy-done.9, f32[768]{0:T(1024)S(1)} %get-tuple-element.46, ...), kind=kOutput, calls=%fused_computation.116 | convolution fusion | flops 1266548736 | bytes 11819008 | tf_op jit(solution)/shard_map/dot_general | solution.py:15
  271.9 12.1 %multiply_convert_fusion = (bf16[512,1536]{1,0:T(8,128)(2,1)S(1)}, f32[512,1536]{1,0:T(8,128)}, f32[512,1536]{1,0:T(8,128)}) fusion(f32[1536]{0:T(1024)S(1)} %copy-done.138, bf16[768,1536]{1,0:T(8,128)(2,1)S(1)} %copy-done.44, f32[1536]{0:T(1024)S(1)} %broadcast_multiply_fusion.1, f32[512,768]{1,0:T(8,128)S(1)} %copy-done.5, f32[512]{0:T(512)S(1)} %fusion.268, ...), kind=kOutput, calls=%fused_computation.103 | convolution fusion | flops 1266548736 | bytes 11819008 | tf_op jit(solution)/shard_map/dot_general | solution.py:15
  290.3 154.4 %all-reduce.18.cloned.1.call-done = (f32[512,768]{1,0:T(8,128)}, f32[512,768]{1,0:T(8,128)}, f32[512,768]{1,0:T(8,128)}, f32[512,768]{1,0:T(8,128)}) async-done(((f32[512,768]{1,0:T(8,128)}, f32[512,768]{1,0:T(8,128)}, f32[512,768]{1,0:T(8,128)}, f32[512,768]{1,0:T(8,128)}), (f32[512,768]{1,0:T(8,128)}, f32[512,768]{1,0:T(8,128)}, f32[512,768]{1,0:T(8,128)}, ...) | async-done | bytes 6291472 | tf_op jit(solution)/shard_map/psum | solution.py:100
  444.7 4.2 fusion.412
  451.5 5.3 multiply_reduce_fusion.4
  461.5 4.1 convert_reduce_fusion.1
  469.6 4.1 convert_reduce_fusion
  484.6 4.7 fusion.434
  489.3 3.6 fusion.437
  494.5 3.7 convolution_add_fusion
  498.2 65.8 %all-reduce.16.cloned.1.call-done = (f32[512,768]{1,0:T(8,128)}, f32[512,768]{1,0:T(8,128)}) async-done(((f32[512,768]{1,0:T(8,128)}, f32[512,768]{1,0:T(8,128)}), (f32[512,768]{1,0:T(8,128)}, f32[512,768]{1,0:T(8,128)})) %all-reduce.16.cloned.1.call-update) | async-done | bytes 3145744 | tf_op jit(solution)/shard_map/psum | solution.py:112
  564.1 5.0 multiply_reduce_fusion.5
  574.2 3.7 fusion.436
  580.4 13.8 %convert_reduce_fusion.10 = (f32[6,64]{1,0:T(8,128)S(1)}, bf16[6,64,512]{2,1,0:T(8,128)(2,1)}) fusion(bf16[512,6,64]{0,2,1:T(8,128)(2,1)S(1)} %bitcast.245, f32[6,512,512]{1,2,0:T(8,128)} %fusion.436, f32[6,512,512]{1,2,0:T(8,128)} %fusion.434, f32[6,512,512]{1,2,0:T(8,128)} %copy-done.13, f32[512,512]{0,1:T(8,128)} %fusion.195, ...), kind=kOutput, calls=%fused_computation.327 | convolution fusion | flops 224136320 | bytes 20985344 | tf_op jit(solution)/shard_map/hqk,qhd->khd/dot_general | solution.py:134
  594.2 13.7 %convert_reduce_fusion.11 = (f32[6,64]{1,0:T(8,128)S(1)}, bf16[6,64,512]{2,1,0:T(8,128)(2,1)}) fusion(bf16[512,6,64]{0,2,1:T(8,128)(2,1)S(1)} %bitcast.247, f32[6,512,512]{1,2,0:T(8,128)} %fusion.436, f32[6,512,512]{1,2,0:T(8,128)} %fusion.434, f32[6,512,512]{1,2,0:T(8,128)} %copy-done.13, f32[512,512]{0,1:T(8,128)} %fusion.195, ...), kind=kOutput, calls=%fused_computation.328 | convolution fusion | flops 224136320 | bytes 20985344 | tf_op jit(solution)/shard_map/hqk,khd->qhd/dot_general | solution.py:130
  610.5 3.7 fusion.439
  614.2 5.3 convert_reduce_fusion.6
  619.4 13.5 %convert_reduce_fusion.7 = (f32[6,64]{1,0:T(8,128)S(1)}, bf16[6,64,512]{2,1,0:T(8,128)(2,1)}) fusion(bf16[512,6,64]{0,2,1:T(8,128)(2,1)S(1)} %bitcast.241, f32[6,512,512]{1,2,0:T(8,128)} %fusion.439, f32[6,512,512]{1,2,0:T(8,128)} %fusion.437, f32[6,512,512]{1,2,0:T(8,128)} %copy-done.12, f32[512,512]{0,1:T(8,128)} %fusion.196, ...), kind=kOutput, calls=%fused_computation.324 | convolution fusion | flops 224136320 | bytes 20985344 | tf_op jit(solution)/shard_map/hqk,qhd->khd/dot_general | solution.py:134
  632.9 13.7 %convert_reduce_fusion.8 = (f32[6,64]{1,0:T(8,128)S(1)}, bf16[6,64,512]{2,1,0:T(8,128)(2,1)}) fusion(bf16[512,6,64]{0,2,1:T(8,128)(2,1)} %bitcast.243, f32[6,512,512]{1,2,0:T(8,128)} %fusion.439, f32[6,512,512]{1,2,0:T(8,128)} %fusion.437, f32[6,512,512]{1,2,0:T(8,128)} %copy-done.12, f32[512,512]{0,1:T(8,128)} %fusion.196, f32[6,512]{1,0:T(8,128)S(1)} %log_add_fusion, ...), kind=kOutput, calls=%fused_computation.325 | convolution fusion | flops 224136320 | bytes 20985344 | tf_op jit(solution)/shard_map/hqk,khd->qhd/dot_general | solution.py:130
  655.7 3.6 fusion.394
  659.4 3.9 convolution_add_fusion.1
  674.6 62.1 %all-reduce = (f32[3,384]{1,0:T(4,128)}, f32[6,768]{1,0:T(8,128)}, f32[1536]{0:T(1024)}) all-reduce(f32[3,384]{1,0:T(4,128)S(1)} %maximum_add_fusion, f32[6,768]{1,0:T(8,128)S(1)} %add.602, f32[1536]{0:T(1024)S(1)} %add.603), channel_id=1, replica_groups=mesh['wide'=16,'narrow'=2] {'wide'}, use_global_device_ids=true, to_apply=%region_64.65 | all-reduce | flops 7296 | bytes 58368 | tf_op jit(solution)/shard_map/psum | solution.py:234
  736.7 5.1 all-reduce.14.cloned.1.call-done
  746.3 261.3 %all-reduce.12.cloned.1.call-done = (f32[768,384]{0,1:T(8,128)}, f32[768,384]{0,1:T(8,128)}, f32[768,384]{0,1:T(8,128)}, f32[384,768]{1,0:T(8,128)}, f32[768,1536]{1,0:T(8,128)}, /*index=5*/f32[1536,768]{1,0:T(8,128)}) async-done(((f32[768,384]{0,1:T(8,128)}, f32[768,384]{0,1:T(8,128)}, f32[768,384]{0,1:T(8,128)}, f32[384,768]{1,0:T(8,128)}, f32[768,1536]{1,0:T(8,128)}, /*index=5*/f32[1536,768]{1,0:T(8,128)}), ...) | async-done | bytes 14155792 | tf_op jit(solution)/shard_map/psum | solution.py:234
  1014.2 5.5 copy.73
  (447 shorter events, 123.4 us)
Async XLA Ops:
  7.2 221.4 %copy-start = (bf16[1536,768]{1,0:T(8,128)(2,1)S(1)}, bf16[1536,768]{1,0:T(8,128)(2,1)}, u32[]{:S(2)}) copy-start(bf16[1536,768]{1,0:T(8,128)(2,1)} %param.36) | copy-start | bytes 7077892
  7.2 212.6 %all-reduce.20.cloned.1.call-start = ((), (), s32[]{:S(2)}) async-start(), calls=%async_computation.4 | async-start | bytes 12582912 | tf_op jit(solution)/shard_map/psum | solution.py:87
  12.2 19.6 %copy-start.68 = (bf16[384,512]{1,0:T(8,128)(2,1)}, bf16[384,512]{1,0:T(8,128)(2,1)S(1)}, u32[]{:S(2)}) copy-start(bf16[384,512]{1,0:T(8,128)(2,1)S(1)} %fusion.149) | copy-start | bytes 1179652
  13.6 18.2 %copy-start.70 = (bf16[384,512]{1,0:T(8,128)(2,1)}, bf16[384,512]{1,0:T(8,128)(2,1)S(1)}, u32[]{:S(2)}) copy-start(bf16[384,512]{1,0:T(8,128)(2,1)S(1)} %fusion.150) | copy-start | bytes 1179652
  15.1 19.3 %copy-start.75 = (bf16[384,512]{1,0:T(8,128)(2,1)}, bf16[384,512]{1,0:T(8,128)(2,1)S(1)}, u32[]{:S(2)}) copy-start(bf16[384,512]{1,0:T(8,128)(2,1)S(1)} %fusion.148) | copy-start | bytes 1179652
  23.1 16.5 %copy-start.39 = (pred[512,512]{0,1:T(8,128)(4,1)}, pred[512,512]{0,1:T(8,128)(4,1)S(1)}, u32[]{:S(2)}) copy-start(pred[512,512]{0,1:T(8,128)(4,1)S(1)} %compare_and_fusion.3) | copy-start | bytes 786436
  23.3 14.4 %copy-start.115 = (f32[384]{0:T(512)}, f32[384]{0:T(512)S(1)}, u32[]{:S(2)}) copy-start(f32[384]{0:T(512)S(1)} %broadcast_multiply_fusion.10) | copy-start | bytes 4612
  23.6 27.5 %copy-start.37 = (pred[512,512]{0,1:T(8,128)(4,1)}, pred[512,512]{0,1:T(8,128)(4,1)S(1)}, u32[]{:S(2)}) copy-start(pred[512,512]{0,1:T(8,128)(4,1)S(1)} %compare_and_fusion.1) | copy-start | bytes 786436
  62.6 382.0 %all-reduce.18.cloned.1.call-start = ((), (), s32[]{:S(2)}) async-start(), calls=%async_computation.3 | async-start | bytes 12582912 | tf_op jit(solution)/shard_map/psum | solution.py:100
  63.5 385.8 %copy-start.85 = (f32[768]{0:T(1024)}, f32[768]{0:T(1024)S(1)}, u32[]{:S(2)}) copy-start(f32[768]{0:T(1024)S(1)} %get-tuple-element.47) | copy-start | bytes 9220
  63.5 385.8 %copy-start.97 = (f32[768]{0:T(1024)}, f32[768]{0:T(1024)S(1)}, u32[]{:S(2)}) copy-start(f32[768]{0:T(1024)S(1)} %get-tuple-element.46) | copy-start | bytes 9220
  253.5 195.8 %copy-start.93 = (f32[512]{0:T(512)}, f32[512]{0:T(512)S(1)}, u32[]{:S(2)}) copy-start(f32[512]{0:T(512)S(1)} %broadcast_multiply_fusion.9) | copy-start | bytes 6148
  255.9 193.4 %copy-start.99 = (f32[512]{0:T(512)}, f32[512]{0:T(512)S(1)}, u32[]{:S(2)}) copy-start(f32[512]{0:T(512)S(1)} %fusion.266) | copy-start | bytes 6148
  256.0 193.4 %copy-start.89 = (f32[512]{0:T(512)}, f32[512]{0:T(512)S(1)}, u32[]{:S(2)}) copy-start(f32[512]{0:T(512)S(1)} %broadcast_multiply_fusion.7) | copy-start | bytes 6148
  257.7 14.2 %copy-start.105 = (f32[512]{0:T(512)}, f32[512]{0:T(512)S(1)}, u32[]{:S(2)}) copy-start(f32[512]{0:T(512)S(1)} %multiply_reduce_fusion.15) | copy-start | bytes 6148
  257.7 191.6 %copy-start.95 = (f32[512]{0:T(512)}, f32[512]{0:T(512)S(1)}, u32[]{:S(2)}) copy-start(f32[512]{0:T(512)S(1)} %fusion.268) | copy-start | bytes 6148
  257.7 14.2 %copy-start.5 = (f32[512,768]{1,0:T(8,128)S(1)}, f32[512,768]{1,0:T(8,128)}, u32[]{:S(2)}) copy-start(f32[512,768]{1,0:T(8,128)} %get-tuple-element.120) | copy-start | bytes 4718596
  257.7 14.2 %copy-start.44 = (bf16[768,1536]{1,0:T(8,128)(2,1)S(1)}, bf16[768,1536]{1,0:T(8,128)(2,1)}, u32[]{:S(2)}) copy-start(bf16[768,1536]{1,0:T(8,128)(2,1)} %param.26) | copy-start | bytes 7077892
  290.2 154.5 %copy-start.4 = (bf16[2,512,768]{2,1,0:T(8,128)(2,1)S(1)}, bf16[2,512,768]{2,1,0:T(8,128)(2,1)}, u32[]{:S(2)}) copy-start(bf16[2,512,768]{2,1,0:T(8,128)(2,1)} %param.20) | copy-start | bytes 4718596
  290.3 273.8 %all-reduce.16.cloned.1.call-start = ((), (), s32[]{:S(2)}) async-start(), calls=%async_computation.2 | async-start | bytes 6291456 | tf_op jit(solution)/shard_map/psum | solution.py:112
  478.0 263.8 %all-reduce.14.cloned.1.call-start = ((), (), s32[]{:S(2)}) async-start(), calls=%async_computation.1 | async-start | bytes 6291456 | tf_op jit(solution)/shard_map/psum | solution.py:143
  494.4 69.6 %copy-start.86 = (f32[768]{0:T(1024)S(1)}, f32[768]{0:T(1024)}, u32[]{:S(2)}) copy-start(f32[768]{0:T(1024)} %copy-done.85) | copy-start | bytes 9220
  494.4 69.6 %copy-start.90 = (f32[512]{0:T(512)S(1)}, f32[512]{0:T(512)}, u32[]{:S(2)}) copy-start(f32[512]{0:T(512)} %copy-done.89) | copy-start | bytes 6148
  494.5 69.6 %copy-start.94 = (f32[512]{0:T(512)S(1)}, f32[512]{0:T(512)}, u32[]{:S(2)}) copy-start(f32[512]{0:T(512)} %copy-done.93) | copy-start | bytes 6148
  494.5 69.6 %copy-start.96 = (f32[512]{0:T(512)S(1)}, f32[512]{0:T(512)}, u32[]{:S(2)}) copy-start(f32[512]{0:T(512)} %copy-done.95) | copy-start | bytes 6148
  494.5 69.6 %copy-start.100 = (f32[512]{0:T(512)S(1)}, f32[512]{0:T(512)}, u32[]{:S(2)}) copy-start(f32[512]{0:T(512)} %copy-done.99) | copy-start | bytes 6148
  494.5 69.6 %copy-start.108 = (f32[512]{0:T(512)S(1)}, f32[512]{0:T(512)}, u32[]{:S(2)}) copy-start(f32[512]{0:T(512)} %copy-done.107) | copy-start | bytes 6148
  494.5 69.6 %copy-start.110 = (f32[512]{0:T(512)S(1)}, f32[512]{0:T(512)}, u32[]{:S(2)}) copy-start(f32[512]{0:T(512)} %copy-done.109) | copy-start | bytes 6148
  632.9 15.5 %copy-start.25 = (bf16[768,384]{1,0:T(8,128)(2,1)S(1)}, bf16[768,384]{1,0:T(8,128)(2,1)}, u32[]{:S(2)}) copy-start(bf16[768,384]{1,0:T(8,128)(2,1)} %param.22) | copy-start | bytes 1769476
  632.9 15.5 %copy-start.112 = (f32[384]{0:T(512)S(1)}, f32[384]{0:T(512)}, u32[]{:S(2)}) copy-start(f32[384]{0:T(512)} %copy-done.111) | copy-start | bytes 4612
  655.6 351.9 %all-reduce.12.cloned.1.call-start = ((), (), s32[]{:S(2)}) async-start(), calls=%async_computation | async-start | bytes 28311552 | tf_op jit(solution)/shard_map/psum | solution.py:234
  673.9 70.0 %copy-start.16 = (f32[512,768]{1,0:T(8,128)S(1)}, f32[512,768]{1,0:T(8,128)}, u32[]{:S(2)}) copy-start(f32[512,768]{1,0:T(8,128)} %get-tuple-element.131) | copy-start | bytes 4718596
  (121 other events, 449.2 us)
Sparse Core Ops, SparseCore 0:
  62.8 156.9 all-reduce.19
  290.4 154.2 all-reduce.17
  478.1 85.9 all-reduce.15
  655.7 85.9 all-reduce.13
  747.3 260.2 all-reduce.11
where the time goes:
time: 1040 us; the launch traced here: 1030 us
  waiting for transfers between devices  640 us (62%)
  matrix products  226 us (22%)
  blocking collectives  62.1 us (6%)
  other arithmetic  55.2 us (5%)
  local copies, waits for them, and re-layouts  28.6 us (3%)
  between operations  16 us (2%)
    psum x1, waiting for transfers between devices, on_device(): lax.psum((totals[0], totals[1], totals[2], totals[3], totals[4], totals[5...  261 us
    psum x1, waiting for transfers between devices, micro_step(): lax.psum((matmul(active_low, student[5]), matmul(active_t, teacher[5])),...  154 us
    psum x1, waiting for transfers between devices, micro_step(): lax.psum((matmul(mixed_s, student[3]), matmul(mixed_t, teacher[3])), 'nar...  153 us
    dot_general x22, matrix products, matmul(): return jnp.dot(left, right, preferred_element_type=jnp.float32)  77.4 us
    psum x1, waiting for transfers between devices, micro_step(): d_first = lax.psum(contract_cols(d_upward, student[4]), 'narrow') + d_pre2  65.8 us
    psum x1, blocking collectives, on_device(): lax.psum((totals[0], totals[1], totals[2], totals[3], totals[4], totals[5...  62.1 us
    dot_general x2, matrix products, micro_step(): jnp.einsum('hqk,khd->qhd', d_scores, split_heads(keys_s), preferred_eleme...  27.4 us
    dot_general x2, matrix products, micro_step(): jnp.einsum('hqk,qhd->khd', d_scores, split_heads(query_s), preferred_elem...  27.3 us
  transfers between devices with their start and end apart: 5, of which 5 were waited for; matrix products, arithmetic and copies ran while one was open for 4% of the time, Pallas kernels for 0%

commit v1 on v0

v1 whole, which is shorter than its diff:
```python
import functools

import jax
import jax.numpy as jnp
from jax import lax
from jax.experimental import pallas as pl
from jax.experimental.pallas import tpu as pltpu
from jax.sharding import PartitionSpec as P

HEAD = 64
REGION = 256

norm_eps = 1e-06
score_weight = 0.05
big_negative = -1e30
f32 = jnp.float32
bf16 = jnp.bfloat16


def dot_nn(left, right):
    return jnp.dot(left, right, preferred_element_type=f32)


def dot_tn(left, right):
    return lax.dot_general(left, right, (((0,), (0,)), ((), ())), preferred_element_type=f32)


def dot_nt(left, right):
    return lax.dot_general(left, right, (((1,), (1,)), ((), ())), preferred_element_type=f32)


def layer_norm(values, gain, shift):
    centred = values - jnp.mean(values, axis=-1, keepdims=True)
    spread = jnp.mean(centred * centred, axis=-1, keepdims=True)
    return centred * lax.rsqrt(spread + norm_eps) * (1.0 + gain) + shift


def binarize(weight, axis):
    widened = weight.astype(f32)
    alpha = jnp.mean(jnp.abs(widened), axis=axis, keepdims=True)
    return (alpha * jnp.sign(widened)).astype(bf16)


def half_masks():
    lane = lax.broadcasted_iota(jnp.int32, (1, 2 * HEAD), 1)
    low = jnp.where(lane < HEAD, 1.0, 0.0).astype(bf16)
    return (low, (1.0 - low.astype(f32)).astype(bf16))


def region_masks(row_ref, col_ref):
    across = row_ref[0]
    down = col_ref[...]
    same = down == across
    live = down >= 0
    size = down.shape[0]
    diagonal = lax.broadcasted_iota(jnp.int32, (size, size), 0) == lax.broadcasted_iota(
        jnp.int32, (size, size), 1
    )
    pairs = same & live
    return pairs, pairs | diagonal


def probabilities(scores, allowed):
    masked = jnp.where(allowed, scores, big_negative)
    top = jnp.max(masked, axis=-1, keepdims=True)
    expo = jnp.exp(masked - top)
    total = jnp.sum(expo, axis=-1, keepdims=True)
    return expo * (1.0 / total)


def attend_kernel(width, qkv_ref, row_ref, col_ref, out_ref):
    pairs, allowed = region_masks(row_ref, col_ref)
    masks = half_masks()
    scale = HEAD ** (-0.5)
    for net in range(2):
        base = net * 3 * width
        for at in range(0, width, 2 * HEAD):
            query = qkv_ref[:, base + at : base + at + 2 * HEAD]
            keys = qkv_ref[:, base + width + at : base + width + at + 2 * HEAD]
            values = qkv_ref[:, base + 2 * width + at : base + 2 * width + at + 2 * HEAD]
            probs = [
                probabilities(dot_nt(query * mask, keys) * scale, allowed).astype(bf16)
                for mask in masks
            ]
            stacked = jnp.concatenate([values * mask for mask in masks], axis=0)
            mixed = dot_nn(jnp.concatenate(probs, axis=1), stacked)
            out_ref[:, net * width + at : net * width + at + 2 * HEAD] = mixed.astype(bf16)


def attend(qkv, seg_row, seg_col):
    rows, columns = qkv.shape
    width = columns // 6
    regions = rows // REGION
    return pl.pallas_call(
        functools.partial(attend_kernel, width),
        grid=(regions,),
        in_specs=[
            pl.BlockSpec((REGION, columns), lambda i: (i, 0)),
            pl.BlockSpec((1, 1, REGION), lambda i: (i, 0, 0)),
            pl.BlockSpec((REGION, 1), lambda i: (i, 0)),
        ],
        out_specs=pl.BlockSpec((REGION, 2 * width), lambda i: (i, 0)),
        out_shape=jax.ShapeDtypeStruct((rows, 2 * width), bf16),
        compiler_params=pltpu.CompilerParams(vmem_limit_bytes=32 * 2**20),
        cost_estimate=pl.CostEstimate(
            flops=8 * rows * REGION * width, bytes_accessed=8 * rows * columns, transcendentals=0
        ),
        name="attend",
    )(qkv, seg_row, seg_col)


def attend_back_kernel(width, own_ref, oth_ref, grad_ref, row_ref, col_ref, out_ref):
    pairs, allowed = region_masks(row_ref, col_ref)
    weight = jnp.where(pairs, score_weight, 0.0)
    masks = half_masks()
    scale = HEAD ** (-0.5)
    step = 2 * HEAD
    for part, qkv_ref in enumerate((own_ref, oth_ref)):
        for at in range(0, width, step):
            query, keys, values, query_t, keys_t = (
                qkv_ref[:, k * width + at : k * width + at + step] for k in range(5)
            )
            grad = grad_ref[:, part * width + at : part * width + at + step]
            probs = []
            slopes = []
            for mask in masks:
                scores = dot_nt(query * mask, keys) * scale
                prob = probabilities(scores, allowed)
                gap = scores - dot_nt(query_t * mask, keys_t) * scale
                d_prob = dot_nt(grad * mask, values)
                mean = jnp.sum(prob * d_prob, axis=-1, keepdims=True)
                slope = prob * (d_prob - mean) + weight * gap
                probs.append(prob.astype(bf16))
                slopes.append(slope.astype(bf16))

            def both(array):
                return jnp.concatenate([array * mask for mask in masks], axis=0)

            d_query = dot_nn(jnp.concatenate(slopes, axis=1), both(keys)) * scale
            d_keys = dot_tn(jnp.concatenate(slopes, axis=0), both(query)) * scale
            d_values = dot_tn(jnp.concatenate(probs, axis=0), both(grad))
            for k, result in enumerate((d_query, d_keys, d_values)):
                start = part * 3 * width + k * width + at
                out_ref[:, start : start + step] = result.astype(bf16)


def attend_back(qkv_own, qkv_oth, grad, seg_row, seg_col):
    rows, columns = qkv_own.shape
    width = columns // 6
    regions = rows // REGION
    return pl.pallas_call(
        functools.partial(attend_back_kernel, width),
        grid=(regions,),
        in_specs=[
            pl.BlockSpec((REGION, columns), lambda i: (i, 0)),
            pl.BlockSpec((REGION, columns), lambda i: (i, 0)),
            pl.BlockSpec((REGION, 2 * width), lambda i: (i, 0)),
            pl.BlockSpec((1, 1, REGION), lambda i: (i, 0, 0)),
            pl.BlockSpec((REGION, 1), lambda i: (i, 0)),
        ],
        out_specs=pl.BlockSpec((REGION, 6 * width), lambda i: (i, 0)),
        out_shape=jax.ShapeDtypeStruct((rows, 6 * width), bf16),
        compiler_params=pltpu.CompilerParams(vmem_limit_bytes=48 * 2**20),
        cost_estimate=pl.CostEstimate(
            flops=28 * rows * REGION * width, bytes_accessed=16 * rows * columns, transcendentals=0
        ),
        name="attend_back",
    )(qkv_own, qkv_oth, grad, seg_row, seg_col)


def assemble_kernel(count, where_ref, *refs):
    out_ref = refs[-1]
    step = pl.program_id(0)
    for k, ref in enumerate(refs[:-1]):

        @pl.when(step // count == k)
        def _(ref=ref):
            out_ref[...] = ref[...].astype(out_ref.dtype)


def assemble(pieces, where, count, dtype=bf16):
    rows = pieces[0].shape[0] // count
    columns = pieces[0].shape[1]
    total = count * len(pieces)
    specs = [
        pl.BlockSpec((rows, columns), lambda i, w, k=k: (jnp.clip(i - count * k, 0, count - 1), 0))
        for k in range(len(pieces))
    ]
    return pl.pallas_call(
        functools.partial(assemble_kernel, count),
        grid_spec=pltpu.PrefetchScalarGridSpec(
            num_scalar_prefetch=1,
            grid=(total,),
            in_specs=specs,
            out_specs=pl.BlockSpec((rows, columns), lambda i, w: (jnp.bitwise_xor(i, w[0]), 0)),
        ),
        out_shape=jax.ShapeDtypeStruct((total * rows, columns), dtype),
        compiler_params=pltpu.CompilerParams(vmem_limit_bytes=40 * 2**20),
        cost_estimate=pl.CostEstimate(
            flops=0, bytes_accessed=6 * total * rows * columns, transcendentals=0
        ),
        name="assemble",
    )(where.reshape(1).astype(jnp.int32), *pieces)


def on_device(
    n_wide,
    tokens,
    segments,
    query_weight,
    key_weight,
    value_weight,
    output_weight,
    expand_weight,
    reduce_weight,
    heads_bias,
    model_s,
    hidden_bias,
    mentor_query,
    mentor_key,
    mentor_value,
    mentor_output,
    mentor_expand,
    mentor_reduce,
    mentor_heads,
    model_t,
    mentor_hidden,
):
    n_bits = n_wide.bit_length() - 1
    side = lax.axis_index("narrow")
    place = lax.axis_index("wide")
    bits = [(place >> b) & 1 for b in range(n_bits)]

    def swap(array, bit):
        if bit == "x":
            return lax.ppermute(array, "narrow", [(0, 1), (1, 0)])
        return lax.ppermute(array, "wide", [(i, i ^ (1 << bit)) for i in range(n_wide)])

    w_qkv = jnp.concatenate(
        [
            binarize(query_weight, 0),
            binarize(key_weight, 0),
            binarize(value_weight, 0),
            mentor_query,
            mentor_key,
            mentor_value,
        ],
        axis=1,
    )
    w_out = jnp.concatenate([binarize(output_weight, 1), mentor_output], axis=1)
    w_up = jnp.concatenate([binarize(expand_weight, 0), mentor_expand], axis=1)
    w_down = jnp.concatenate([binarize(reduce_weight, 1), mentor_reduce], axis=1)
    width = query_weight.shape[1]
    hidden = expand_weight.shape[1]
    dim = query_weight.shape[0]

    biases = jnp.concatenate(
        [heads_bias.reshape(-1), mentor_heads.reshape(-1), hidden_bias, mentor_hidden]
    )
    biases_oth = swap(biases.reshape(-1, 128), "x").reshape(-1)

    def fetch(weight, first, second):
        rows = weight.shape[0] // 8
        index = bits[0] * 4 + bits[second] * 2 + bits[first]
        piece = lax.dynamic_slice_in_dim(weight, index * rows, rows, 0).astype(f32)
        piece = lax.optimization_barrier(piece)
        zero = swap(piece, "x")
        pair = jnp.concatenate([zero, swap(zero, first)], axis=0)
        pair_b = swap(pair, second)
        return assemble([pair, pair_b, swap(pair, 0), swap(pair_b, 0)], index, 2)

    def fetch_direct(weight):
        rows = weight.shape[0] // 2
        piece = lax.dynamic_slice_in_dim(weight, bits[0] * rows, rows, 0).astype(f32)
        piece = lax.optimization_barrier(piece)
        mine = swap(piece, "x")
        return assemble([mine, swap(mine, 0)], bits[0] * 2 , 2)

    v_qkv = fetch(w_qkv, 1, 2)
    v_out = fetch(w_out, 2, 1)
    v_up = fetch(w_up, 1, 2)
    cut = w_down.shape[0] * 2 // 3
    v_down_a = fetch(w_down[:cut], 2, 1)
    v_down_b = fetch_direct(w_down[cut:])

    x = lax.dynamic_index_in_dim(tokens, side, 0, keepdims=False)
    segment = lax.dynamic_index_in_dim(segments, side, 0, keepdims=False)
    rows = x.shape[0]
    live = (segment >= 0)[:, None]
    seg_row = segment.reshape(rows // REGION, 1, REGION)
    seg_col = segment.reshape(rows, 1)
    resident = x.astype(f32)

    heads_end = 6 * width
    qkv_own = (dot_nn(x, w_qkv) + biases[:heads_end]).astype(bf16)
    qkv_oth = (dot_nn(x, v_qkv) + biases_oth[:heads_end]).astype(bf16)
    mixed_own = attend(qkv_own, seg_row, seg_col)
    mixed_oth = attend(qkv_oth, seg_row, seg_col)

    def net_parts(own, oth, net, size):
        return own[:, net * size : (net + 1) * size], oth[:, net * size : (net + 1) * size]

    def first_norm_in(net, model):
        m_own, m_oth = net_parts(mixed_own, mixed_oth, net, width)
        o_own, o_oth = net_parts(w_out, v_out, net, dim)
        return resident + (dot_nn(m_own, o_own) + dot_nn(m_oth, o_oth)) + model[0]

    pre_s = first_norm_in(0, model_s)
    pre_t = first_norm_in(1, model_t)
    first_s, first_back = jax.vjp(layer_norm, pre_s, model_s[2], model_s[3])
    first_t = layer_norm(pre_t, model_t[2], model_t[3])
    low_s = first_s.astype(bf16)
    low_t = first_t.astype(bf16)

    def cdf_of(up):
        return 0.5 * lax.erfc(-up * 0.5**0.5)

    def forward_up(weight, bias):
        up_s = dot_nn(low_s, weight[:, :hidden]) + bias[heads_end : heads_end + hidden]
        up_t = dot_nn(low_t, weight[:, hidden:]) + bias[heads_end + hidden :]
        cdf = cdf_of(up_s)
        slope = cdf + up_s * jnp.exp(-0.5 * up_s * up_s) * (2.0 * jnp.pi) ** -0.5
        return (up_s * cdf).astype(bf16), slope, (up_t * cdf_of(up_t)).astype(bf16)

    act_s_own, slope_own, act_t_own = forward_up(w_up, biases)
    act_s_oth, slope_oth, act_t_oth = forward_up(v_up, biases_oth)

    def down(own, oth, net):
        lo, hi = net * dim, (net + 1) * dim
        return (
            dot_nn(own, w_down[:, lo:hi])
            + dot_nn(oth[:, :cut], v_down_a[:, lo:hi])
            + dot_nn(oth[:, cut:], v_down_b[:, lo:hi])
        )

    down_s = down(act_s_own, act_s_oth, 0)
    down_t = down(act_t_own, act_t_oth, 1)
    out_s, second_back = jax.vjp(layer_norm, first_s + down_s + model_s[1], model_s[4], model_s[5])
    out_t = layer_norm(first_t + down_t + model_t[1], model_t[4], model_t[5])

    d_out = jnp.where(live, out_s - out_t, 0.0)
    d_pre2, d_gain2, d_shift2 = second_back(d_out)
    d_down = d_pre2.astype(bf16)

    act_s = jnp.concatenate([act_s_own, act_s_oth], axis=1)
    grad_reduce = dot_tn(act_s, d_down).reshape(2, hidden, dim)
    d_up_own = (dot_nt(d_down, w_down[:, :dim]) * slope_own).astype(bf16)
    d_act_oth = jnp.concatenate(
        [dot_nt(d_down, v_down_a[:, :dim]), dot_nt(d_down, v_down_b[:, :dim])], axis=1
    )
    d_up_oth = (d_act_oth * slope_oth).astype(bf16)
    d_up = jnp.concatenate([d_up_own, d_up_oth], axis=1)
    grad_expand = dot_tn(low_s, d_up)
    d_first = dot_nt(d_up_own, w_up[:, :hidden]) + dot_nt(d_up_oth, v_up[:, :hidden]) + d_pre2
    d_pre1, d_gain1, d_shift1 = first_back(d_first)
    d_attn = d_pre1.astype(bf16)
    mixed_s = jnp.concatenate([mixed_own[:, :width], mixed_oth[:, :width]], axis=1)
    grad_output = dot_tn(mixed_s, d_attn).reshape(2, width, dim)
    d_mixed = jnp.concatenate(
        [dot_nt(d_attn, w_out[:, :dim]), dot_nt(d_attn, v_out[:, :dim])], axis=1
    ).astype(bf16)
    d_qkv = attend_back(qkv_own, qkv_oth, d_mixed, seg_row, seg_col)
    grad_qkv = dot_tn(x, d_qkv)
    d_tokens = (
        dot_nt(d_qkv[:, : 3 * width], w_qkv[:, : 3 * width])
        + dot_nt(d_qkv[:, 3 * width :], v_qkv[:, : 3 * width])
        + d_pre1
    )

    def cut_rows(array, bit, mine):
        size = array.shape[-2] // 2
        start = (bits[bit] if mine else 1 - bits[bit]) * size
        return lax.dynamic_slice_in_dim(array, start, size, array.ndim - 2)

    def total(grad, order):
        def cut_one(array, name, mine):
            if name != "x":
                return cut_rows(array, name, mine)
            if array.ndim == 3:
                return array[0 if mine else 1]
            size = array.shape[-1] // 2
            return array[:, :size] if mine else array[:, size:]

        terms = [grad]
        for name in order:
            send = functools.reduce(jnp.add, [cut_one(t, name, False) for t in terms])
            got = swap(send, name)
            terms = [cut_one(t, name, True) for t in terms] + [got]
        block = functools.reduce(jnp.add, terms)
        for extra in range(4, n_bits):
            block = block + swap(block, extra)
        for name in [n for n in reversed(order) if n != "x"]:
            got = swap(block, name)
            first = bits[name] == 0
            block = jnp.where(
                first,
                jnp.concatenate([block, got], axis=0),
                jnp.concatenate([got, block], axis=0),
            )
        return block

    out_reduce = total(grad_reduce, (0, "x", 1, 2, 3))
    out_expand = total(grad_expand, (0, 1, 2, "x", 3))
    out_output = total(grad_output, (0, "x", 2, 1, 3))
    out_qkv = total(grad_qkv, (0, "x", 2, 1, 3))

    sum_qkv = jnp.sum(d_qkv.astype(f32), axis=0)
    sum_up = jnp.sum(d_up.astype(f32), axis=0)
    sums_model = jnp.concatenate(
        [
            jnp.sum(d_attn.astype(f32), axis=0),
            jnp.sum(d_down.astype(f32), axis=0),
            d_gain1,
            d_shift1,
            d_gain2,
            d_shift2,
        ]
    )
    mine = jnp.concatenate([sum_qkv[: 3 * width], sum_up[:hidden], sums_model])
    theirs = jnp.concatenate([sum_qkv[3 * width :], sum_up[hidden:], sums_model])
    small = mine.reshape(-1, 128) + swap(theirs.reshape(-1, 128), "x")
    for b in range(n_bits):
        small = small + swap(small, b)
    small = small.reshape(-1)
    out_heads = small[: 3 * width].reshape(3, width)
    out_hidden = small[3 * width : 3 * width + hidden]
    out_model = small[3 * width + hidden :].reshape(6, dim)

    def both_batches(array, dtype):
        return assemble([array, swap(array, "x")], side * 4, 4, dtype).reshape(2, rows, dim)

    student_out = both_batches(out_s, bf16)
    grad_tokens = both_batches(d_tokens, f32)
    return (
        student_out,
        grad_tokens,
        out_qkv[:, :width],
        out_qkv[:, width : 2 * width],
        out_qkv[:, 2 * width :],
        out_output,
        out_expand,
        out_reduce,
        out_heads,
        out_model,
        out_hidden,
    )


def solution(mesh):
    cols = P(None, "narrow")
    rows = P("narrow", None)
    net = (cols, cols, cols, rows, cols, rows, cols, P(), P("narrow"))
    data = P(None, "wide", None)
    return jax.shard_map(
        functools.partial(on_device, mesh.shape["wide"]),
        mesh=mesh,
        in_specs=(data, P(None, "wide")) + net + net,
        out_specs=(data, data) + net,
        check_vma=False,
    )
```

time: 1040 us -> 703 us (0.68)
  waiting for transfers between devices: 640 us -> 358 us
  matrix products: 226 us -> 74 us
  blocking collectives: 62.1 us -> 0 us
  starting transfers between devices: 0.78 us -> 55 us
  Pallas kernels: 0 us -> 47.9 us
  other arithmetic: 55.2 us -> 94 us
  local copies, waits for them, and re-layouts: 28.6 us -> 61.4 us
  between operations: 16 us -> 2.48 us
    psum x5 -> x0, waiting for transfers between devices: 640 us -> none  [the longest x1 261 us: on_device(): lax.psum((totals[0], totals[1], totals[2], totals[3], totals[4], totals[5...]
    ppermute x0 -> x66, waiting for transfers between devices: none -> 358 us  [the longest x53 216 us: swap(): lax.ppermute(array, 'wide', [(i, i ^ 1 << bit) for i in range(n_wide)])]
    dot_general x62 -> x28, matrix products: 214 us -> 74 us  [the longest x15 54.1 us: dot_nn(): return jnp.dot(left, right, preferred_element_type=f32)]
    psum x1 -> x0, blocking collectives: 62.1 us -> none  [on_device(): lax.psum((totals[0], totals[1], totals[2], totals[3], totals[4], totals[5...]
    ppermute x0 -> x66, starting transfers between devices: none -> 55 us  [the longest x53 42.8 us: swap(): lax.ppermute(array, 'wide', [(i, i ^ 1 << bit) for i in range(n_wide)])]
    pallas_call x0 -> x10, Pallas kernels: none -> 47.9 us  [the longest x7 25 us: assemble(): pl.pallas_call(functools.partial(assemble_kernel, count), grid_spec=pltpu...]
    select_n x0 -> x16, other arithmetic: none -> 25.8 us  [total(): jnp.where(first, jnp.concatenate([block, got], axis=0), jnp.concatenate([...]
    add x5 -> x21, other arithmetic: 2.1 us -> 27.5 us  [the longest x12 21.1 us: total(): send = functools.reduce(jnp.add, [cut_one(t, name, False) for t in terms])]
  transfers between devices with their start and end apart: 5 -> 66, of which waited for: 5 -> 23; matrix products, arithmetic and copies ran while one was open for 4% -> 22% of each run, Pallas kernels for 0% -> 6%
where the time goes in v1:
time: 703 us; the launch traced here: 693 us
  waiting for transfers between devices  358 us (51%)
  other arithmetic  94 us (13%)
  matrix products  74 us (11%)
  local copies, waits for them, and re-layouts  61.4 us (9%)
  starting transfers between devices  55 us (8%)
  Pallas kernels  47.9 us (7%)
    ppermute x53, waiting for transfers between devices, swap(): lax.ppermute(array, 'wide', [(i, i ^ 1 << bit) for i in range(n_wide)])  216 us
    ppermute x13, waiting for transfers between devices, swap(): return lax.ppermute(array, 'narrow', [(0, 1), (1, 0)])  142 us
    dot_general x15, matrix products, dot_nn(): return jnp.dot(left, right, preferred_element_type=f32)  54.1 us
    ppermute x53, starting transfers between devices, swap(): lax.ppermute(array, 'wide', [(i, i ^ 1 << bit) for i in range(n_wide)])  42.8 us
    unnamed x195, local copies, waits for them, and re-layouts  39.7 us
    select_n x16, other arithmetic, total(): jnp.where(first, jnp.concatenate([block, got], axis=0), jnp.concatenate([...  25.8 us
    pallas_call x7, Pallas kernels, assemble(): pl.pallas_call(functools.partial(assemble_kernel, count), grid_spec=pltpu...  25 us
    add x12, other arithmetic, total(): send = functools.reduce(jnp.add, [cut_one(t, name, False) for t in terms])  21.1 us
  transfers between devices with their start and end apart: 66, of which 23 were waited for; matrix products, arithmetic and copies ran while one was open for 22% of the time, Pallas kernels for 6%

profile of v1, /device:TPU:0, one launch (start us, length us, event | category | flops | bytes accessed | tf_op | source)
XLA Modules:
  0.0 693.2 jit_solution(8869910058840931675)
XLA Ops:
  41.5 47.0 %collective-permute-done = f32[96,2304]{1,0:T(8,128)} collective-permute-done((f32[96,2304]{1,0:T(8,128)}, f32[96,2304]{1,0:T(8,128)}, u32[]{:S(2)}, u32[]{:S(2)}) %collective-permute-start) | collective-permute-done | bytes 884768 | tf_op jit(solution)/shard_map/ppermute | solution.py:236
  97.5 14.9 %collective-permute-done.11 = f32[96,3072]{1,0:T(8,128)S(1)} collective-permute-done((f32[96,3072]{1,0:T(8,128)}, f32[96,3072]{1,0:T(8,128)S(1)}, u32[]{:S(2)}, u32[]{:S(2)}) %collective-permute-start.11) | collective-permute-done | bytes 1179680 | tf_op jit(solution)/shard_map/ppermute | solution.py:236
  119.5 9.2 %collective-permute-done.8.refs_1_ = f32[96,1536]{1,0:T(8,128)S(1)} collective-permute-done((f32[96,1536]{1,0:T(8,128)S(1)}, f32[96,1536]{1,0:T(8,128)S(1)}, u32[]{:S(2)}, u32[]{:S(2)}) %collective-permute-start.8) | collective-permute-done | bytes 589856 | tf_op jit(solution)/shard_map/ppermute | solution.py:237
  130.0 24.0 %collective-permute-done.12 = f32[96,3072]{1,0:T(8,128)S(1)} collective-permute-done((f32[96,3072]{1,0:T(8,128)S(1)}, f32[96,3072]{1,0:T(8,128)S(1)}, u32[]{:S(2)}, u32[]{:S(2)}) %collective-permute-start.12) | collective-permute-done | bytes 1179680 | tf_op jit(solution)/shard_map/ppermute | solution.py:237
  158.3 26.9 %collective-permute-done.18.refs_1_ = f32[256,1536]{1,0:T(8,128)} collective-permute-done((f32[256,1536]{1,0:T(8,128)}, f32[256,1536]{1,0:T(8,128)}, u32[]{:S(2)}, u32[]{:S(2)}) %collective-permute-start.18) | collective-permute-done | bytes 1572896 | tf_op jit(solution)/shard_map/ppermute | solution.py:237
  190.0 5.4 attend.2
  200.8 9.1 %collective-permute-done.13.refs_1_ = f32[192,3072]{1,0:T(8,128)} collective-permute-done((f32[192,3072]{1,0:T(8,128)}, f32[192,3072]{1,0:T(8,128)}, u32[]{:S(2)}, u32[]{:S(2)}) %collective-permute-start.13) | collective-permute-done | bytes 2359328 | tf_op jit(solution)/shard_map/ppermute | solution.py:237
  220.5 5.1 attend.3
  229.5 9.7 %multiply_convert_fusion.1 = (bf16[512,1536]{1,0:T(8,128)(2,1)S(1)}, f32[512,1536]{1,0:T(8,128)}, f32[512,1536]{1,0:T(8,128)}) fusion(f32[1536]{0:T(1024)S(1)} %copy-done.82, bf16[768,1536]{1,0:T(8,128)(2,1)S(1)} %copy-done.37, f32[512,768]{1,0:T(8,128)S(1)} %get-tuple-element.81, f32[768]{0:T(1024)S(1)} %get-tuple-element.25, ...), kind=kOutput, calls=%fused_computation.109 | convolution fusion | flops 1261830144 | bytes 11812864 | tf_op jit(solution)/shard_map/dot_general | solution.py:21
  241.8 12.7 %fusion.93 = f32[512,768]{1,0:T(8,128)} fusion(bf16[1536,768]{1,0:T(8,128)(2,1)} %param.36, bf16[768,1536]{1,0:T(8,128)(2,1)} %param.35, f32[1536]{0:T(1024)S(1)} %copy-done.83, f32[512,768]{1,0:T(8,128)} %copy-done.34, f32[768]{0:T(1024)S(1)} %get-tuple-element.19, f32[768]{0:T(1024)S(1)} %get-tuple-element.20, f32[512]{0:T(512)S(1)} %add_rsqrt_fusion.1, ...), kind=kOutput, calls=%fused_computation.188 | convolution fusion | flops 2469789696 | bytes 7880704 | tf_op jit(solution)/shard_map/dot_general | solution.py:21
  254.5 7.2 %assemble.9 = bf16[768,3072]{1,0:T(8,128)(2,1)S(1)} custom-call(s32[1]{0:T(128)} %bitcast.4.where_ref, f32[192,3072]{1,0:T(8,128)} %constant_dynamic-update-slice_fusion.10.refs_0_, f32[192,3072]{1,0:T(8,128)} %collective-permute-done.13.refs_1_, f32[192,3072]{1,0:T(8,128)} %collective-permute-done.14.refs_2_, f32[192,3072]{1,0:T(8,128)} %collective-permute-done.15.refs_3_), custom_call_target="tpu_custom_call" | custom-call | bytes 14155776 | tf_op jit(solution)/shard_map/assemble/pallas_call | solution.py:189
  261.7 8.0 %fusion.19 = bf16[512,1536]{1,0:T(8,128)(2,1)S(1)} fusion(bf16[768,3072]{1,0:T(8,128)(2,1)S(1)} %assemble.9, f32[1536]{0:T(1024)S(1)} %get-tuple-element.62, f32[512,768]{1,0:T(8,128)S(1)} %copy-done.35, f32[768]{0:T(1024)S(1)} %get-tuple-element.19, f32[768]{0:T(1024)S(1)} %get-tuple-element.20, f32[512]{0:T(512)S(1)} %add_rsqrt_fusion.1, ...), kind=kOutput, calls=%fused_computation.45 | convolution fusion | flops 1261830144 | bytes 5525504 | tf_op jit(solution)/shard_map/dot_general | solution.py:21
  272.6 8.4 %multiply_convert_fusion = (bf16[512,1536]{1,0:T(8,128)(2,1)S(1)}, f32[512,1536]{1,0:T(8,128)S(1)}, f32[512,1536]{1,0:T(8,128)S(1)}) fusion(f32[1536]{0:T(1024)S(1)} %get-tuple-element.63, bf16[768,3072]{1,0:T(8,128)(2,1)S(1)} %assemble.9, f32[512,768]{1,0:T(8,128)S(1)} %copy-done.24, f32[768]{0:T(1024)S(1)} %get-tuple-element.25, ...), kind=kOutput, calls=%fused_computation.95 | convolution fusion | flops 1261830144 | bytes 11816960 | tf_op jit(solution)/shard_map/dot_general | solution.py:21
  308.4 12.4 %attend_back.1 = bf16[512,2304]{1,0:T(8,128)(2,1)S(1)} custom-call(bf16[512,2304]{1,0:T(8,128)(2,1)S(1)} %copy-done.1, bf16[512,2304]{1,0:T(8,128)(2,1)} %copy-done.2, bf16[512,768]{1,0:T(8,128)(2,1)S(1)} %pad_maximum_fusion.2.grad_ref, s32[2,1,256]{2,1,0:T(1,128)S(1)} %bitcast.119, s32[512,1]{1,0:T(8,128)S(1)} %copy.34.col_ref), custom_call_target="tpu_custom_call" | custom-call | flops 1409286144 | bytes 18874368 | tf_op jit(solution)/shard_map/attend_back/pallas_call | solution.py:151
  347.1 5.8 fusion.238
  359.7 25.1 %collective-permute-done.26 = f32[384,1152]{1,0:T(8,128)S(1)} collective-permute-done((f32[384,1152]{1,0:T(8,128)S(1)}, f32[384,1152]{1,0:T(8,128)S(1)}, u32[]{:S(2)}, u32[]{:S(2)}) %collective-permute-start.26) | collective-permute-done | bytes 1769504 | tf_op jit(solution)/shard_map/ppermute | solution.py:236
  404.7 43.2 %collective-permute-done.61 = f32[57,128]{1,0:T(8,128)} collective-permute-done((f32[57,128]{1,0:T(8,128)}, f32[57,128]{1,0:T(8,128)}, u32[]{:S(2)}, u32[]{:S(2)}) %collective-permute-start.61) | collective-permute-done | bytes 29216 | tf_op jit(solution)/shard_map/ppermute | solution.py:236
  463.9 28.3 %collective-permute-done.28 = f32[96,1152]{1,0:T(8,128)S(1)} collective-permute-done((f32[96,1152]{1,0:T(8,128)S(1)}, f32[96,1152]{1,0:T(8,128)S(1)}, u32[]{:S(2)}, u32[]{:S(2)}) %collective-permute-start.28) | collective-permute-done | bytes 442400 | tf_op jit(solution)/shard_map/ppermute | solution.py:237
  499.6 5.6 collective-permute-done.29
  506.8 16.9 %collective-permute-done.55 = f32[192,768]{1,0:T(8,128)S(1)} collective-permute-done((f32[192,768]{1,0:T(8,128)S(1)}, f32[192,768]{1,0:T(8,128)S(1)}, u32[]{:S(2)}, u32[]{:S(2)}) %collective-permute-start.55) | collective-permute-done | bytes 589856 | tf_op jit(solution)/shard_map/ppermute | solution.py:237
  529.2 10.6 %collective-permute-done.30 = f32[48,1152]{1,0:T(8,128)S(1)} collective-permute-done((f32[48,1152]{1,0:T(8,128)S(1)}, f32[48,1152]{1,0:T(8,128)S(1)}, u32[]{:S(2)}, u32[]{:S(2)}) %collective-permute-start.30) | collective-permute-done | bytes 221216 | tf_op jit(solution)/shard_map/ppermute | solution.py:237
  540.6 5.6 collective-permute-done.56
  547.5 11.3 %collective-permute-done.48 = f32[48,1536]{1,0:T(8,128)S(1)} collective-permute-done((f32[48,1536]{1,0:T(8,128)S(1)}, f32[48,1536]{1,0:T(8,128)S(1)}, u32[]{:S(2)}, u32[]{:S(2)}) %collective-permute-start.48) | collective-permute-done | bytes 294944 | tf_op jit(solution)/shard_map/ppermute | solution.py:237
  567.8 11.5 %collective-permute-done.49 = f32[96,1536]{1,0:T(8,128)S(1)} collective-permute-done((f32[96,1536]{1,0:T(8,128)S(1)}, f32[96,1536]{1,0:T(8,128)S(1)}, u32[]{:S(2)}, u32[]{:S(2)}) %collective-permute-start.49) | collective-permute-done | bytes 589856 | tf_op jit(solution)/shard_map/ppermute | solution.py:237
  581.8 12.4 %collective-permute-done.58 = f32[192,768]{1,0:T(8,128)S(1)} collective-permute-done((f32[192,768]{1,0:T(8,128)S(1)}, f32[192,768]{1,0:T(8,128)S(1)}, u32[]{:S(2)}, u32[]{:S(2)}) %collective-permute-start.58) | collective-permute-done | bytes 589856 | tf_op jit(solution)/shard_map/ppermute | solution.py:237
  597.0 10.4 %collective-permute-done.39 = f32[24,768]{1,0:T(8,128)S(1)} collective-permute-done((f32[24,768]{1,0:T(8,128)S(1)}, f32[24,768]{1,0:T(8,128)S(1)}, u32[]{:S(2)}, u32[]{:S(2)}) %collective-permute-start.39) | collective-permute-done | bytes 73760 | tf_op jit(solution)/shard_map/ppermute | solution.py:237
  607.9 5.2 collective-permute-done.32
  620.3 15.5 %collective-permute-done.40 = f32[48,768]{1,0:T(8,128)S(1)} collective-permute-done((f32[48,768]{1,0:T(8,128)S(1)}, f32[48,768]{1,0:T(8,128)S(1)}, u32[]{:S(2)}, u32[]{:S(2)}) %collective-permute-start.40) | collective-permute-done | bytes 147488 | tf_op jit(solution)/shard_map/ppermute | solution.py:237
  637.5 7.8 %collective-permute-done.41 = f32[96,768]{1,0:T(8,128)S(1)} collective-permute-done((f32[96,768]{1,0:T(8,128)S(1)}, f32[96,768]{1,0:T(8,128)S(1)}, u32[]{:S(2)}, u32[]{:S(2)}) %collective-permute-start.41) | collective-permute-done | bytes 294944 | tf_op jit(solution)/shard_map/ppermute | solution.py:237
  654.3 11.8 %collective-permute-done.23.refs_1_ = f32[512,768]{1,0:T(8,128)S(1)} collective-permute-done((f32[512,768]{1,0:T(8,128)}, f32[512,768]{1,0:T(8,128)S(1)}, u32[]{:S(2)}, u32[]{:S(2)}) %collective-permute-start.23) | collective-permute-done | bytes 1572896 | tf_op jit(solution)/shard_map/ppermute | solution.py:236
  679.2 6.9 maximum_select_fusion
  686.2 6.5 maximum_select_fusion.1
  (455 shorter events, 250.2 us)
Async XLA Ops:
  15.0 98.9 %collective-permute-start.21 = (f32[256,1536]{1,0:T(8,128)}, f32[256,1536]{1,0:T(8,128)S(1)}, u32[]{:S(2)}, u32[]{:S(2)}) collective-permute-start(f32[256,1536]{1,0:T(8,128)} %fusion.116), channel_id=1, source_target_pairs={{0,1},{1,0},{2,3},{3,2},{4,5},{5,4},{6,7},{7,6},{8,9},{9,8},{10,11... | collective-permute-start | bytes 4718600 | tf_op jit(solution)/shard_map/ppermute | solution.py:236
  22.6 69.1 %collective-permute-start.16 = (f32[128,1536]{1,0:T(8,128)}, f32[128,1536]{1,0:T(8,128)}, u32[]{:S(2)}, u32[]{:S(2)}) collective-permute-start(f32[128,1536]{1,0:T(8,128)} %fusion.148), channel_id=1, source_target_pairs={{0,1},{1,0},{2,3},{3,2},{4,5},{5,4},{6,7},{7,6},{8,9},{9,8},{10,11... | collective-permute-start | bytes 2359304 | tf_op jit(solution)/shard_map/ppermute | solution.py:236
  33.8 54.7 %collective-permute-start = (f32[96,2304]{1,0:T(8,128)}, f32[96,2304]{1,0:T(8,128)}, u32[]{:S(2)}, u32[]{:S(2)}) collective-permute-start(f32[96,2304]{1,0:T(8,128)} %dynamic-slice_convert_fusion), channel_id=1, source_target_pairs={{0,1},{1,0},{2,3},{3,2},{4,5},{5,4},{6,7},{7,6},{8,9},{9,8},{10,11... | collective-permute-start | bytes 2654216 | tf_op jit(solution)/shard_map/ppermute | solution.py:236
  37.9 74.5 %collective-permute-start.11 = (f32[96,3072]{1,0:T(8,128)}, f32[96,3072]{1,0:T(8,128)S(1)}, u32[]{:S(2)}, u32[]{:S(2)}) collective-permute-start(f32[96,3072]{1,0:T(8,128)} %fusion.135), channel_id=1, source_target_pairs={{0,1},{1,0},{2,3},{3,2},{4,5},{5,4},{6,7},{7,6},{8,9},{9,8},{10,11... | collective-permute-start | bytes 3538952 | tf_op jit(solution)/shard_map/ppermute | solution.py:236
  39.8 51.1 %collective-permute-start.7 = (f32[48,1536]{1,0:T(8,128)}, f32[48,1536]{1,0:T(8,128)S(1)}, u32[]{:S(2)}, u32[]{:S(2)}) collective-permute-start(f32[48,1536]{1,0:T(8,128)} %collective-permute-done.6), channel_id=1, source_target_pairs={{0,8},{2,10},{4,12},{6,14},{8,0},{10,2},{12,4},{14,6},{16,24},{18,... | collective-permute-start | bytes 884744 | tf_op jit(solution)/shard_map/ppermute | solution.py:237
  114.0 40.0 %collective-permute-start.12 = (f32[96,3072]{1,0:T(8,128)S(1)}, f32[96,3072]{1,0:T(8,128)S(1)}, u32[]{:S(2)}, u32[]{:S(2)}) collective-permute-start(f32[96,3072]{1,0:T(8,128)S(1)} %collective-permute-done.11), channel_id=1, source_target_pairs={{0,4},{2,6},{4,0},{6,2},{8,12},{10,14},{12,8},{14,10},{16,20},{18,... | collective-permute-start | bytes 3538952 | tf_op jit(solution)/shard_map/ppermute | solution.py:237
  114.5 43.5 %collective-permute-start.22 = (f32[256,1536]{1,0:T(8,128)S(1)}, f32[256,1536]{1,0:T(8,128)}, u32[]{:S(2)}, u32[]{:S(2)}) collective-permute-start(f32[256,1536]{1,0:T(8,128)S(1)} %collective-permute-done.21.refs_0_), channel_id=1, source_target_pairs={{0,2},{2,0},{4,6},{6,4},{8,10},{10,8},{12,14},{14,12},{16,18},{18,... | collective-permute-start | bytes 4718600 | tf_op jit(solution)/shard_map/ppermute | solution.py:237
  115.5 69.7 %collective-permute-start.2 = (f32[192,2304]{1,0:T(8,128)}, f32[192,2304]{1,0:T(8,128)}, u32[]{:S(2)}, u32[]{:S(2)}) collective-permute-start(f32[192,2304]{1,0:T(8,128)} %constant_dynamic-update-slice_fusion.6.refs_0_), channel_id=1, source_target_pairs={{0,8},{2,10},{4,12},{6,14},{8,0},{10,2},{12,4},{14,6},{16,24},{18,... | collective-permute-start | bytes 5308424 | tf_op jit(solution)/shard_map/ppermute | solution.py:237
  118.0 67.2 %collective-permute-start.18 = (f32[256,1536]{1,0:T(8,128)}, f32[256,1536]{1,0:T(8,128)}, u32[]{:S(2)}, u32[]{:S(2)}) collective-permute-start(f32[256,1536]{1,0:T(8,128)} %constant_dynamic-update-slice_fusion.12.refs_0_), channel_id=1, source_target_pairs={{0,4},{2,6},{4,0},{6,2},{8,12},{10,14},{12,8},{14,10},{16,20},{18,... | collective-permute-start | bytes 4718600 | tf_op jit(solution)/shard_map/ppermute | solution.py:237
  155.9 54.0 %collective-permute-start.13 = (f32[192,3072]{1,0:T(8,128)}, f32[192,3072]{1,0:T(8,128)}, u32[]{:S(2)}, u32[]{:S(2)}) collective-permute-start(f32[192,3072]{1,0:T(8,128)} %constant_dynamic-update-slice_fusion.10.refs_0_), channel_id=1, source_target_pairs={{0,8},{2,10},{4,12},{6,14},{8,0},{10,2},{12,4},{14,6},{16,24},{18,... | collective-permute-start | bytes 7077896 | tf_op jit(solution)/shard_map/ppermute | solution.py:237
  157.7 43.0 %collective-permute-start.19 = (f32[256,1536]{1,0:T(8,128)}, f32[256,1536]{1,0:T(8,128)S(1)}, u32[]{:S(2)}, u32[]{:S(2)}) collective-permute-start(f32[256,1536]{1,0:T(8,128)} %constant_dynamic-update-slice_fusion.12.refs_0_), channel_id=1, source_target_pairs={{0,2},{2,0},{4,6},{6,4},{8,10},{10,8},{12,14},{14,12},{16,18},{18,... | collective-permute-start | bytes 4718600 | tf_op jit(solution)/shard_map/ppermute | solution.py:237
  158.0 56.9 %collective-permute-start.3 = (f32[192,2304]{1,0:T(8,128)}, f32[192,2304]{1,0:T(8,128)S(1)}, u32[]{:S(2)}, u32[]{:S(2)}) collective-permute-start(f32[192,2304]{1,0:T(8,128)} %constant_dynamic-update-slice_fusion.6.refs_0_), channel_id=1, source_target_pairs={{0,2},{2,0},{4,6},{6,4},{8,10},{10,8},{12,14},{14,12},{16,18},{18,... | collective-permute-start | bytes 5308424 | tf_op jit(solution)/shard_map/ppermute | solution.py:237
  200.8 53.7 %collective-permute-start.14 = (f32[192,3072]{1,0:T(8,128)}, f32[192,3072]{1,0:T(8,128)}, u32[]{:S(2)}, u32[]{:S(2)}) collective-permute-start(f32[192,3072]{1,0:T(8,128)} %constant_dynamic-update-slice_fusion.10.refs_0_), channel_id=1, source_target_pairs={{0,2},{2,0},{4,6},{6,4},{8,10},{10,8},{12,14},{14,12},{16,18},{18,... | collective-permute-start | bytes 7077896 | tf_op jit(solution)/shard_map/ppermute | solution.py:237
  209.9 44.6 %collective-permute-start.15 = (f32[192,3072]{1,0:T(8,128)}, f32[192,3072]{1,0:T(8,128)}, u32[]{:S(2)}, u32[]{:S(2)}) collective-permute-start(f32[192,3072]{1,0:T(8,128)} %collective-permute-done.13.refs_1_), channel_id=1, source_target_pairs={{0,2},{2,0},{4,6},{6,4},{8,10},{10,8},{12,14},{14,12},{16,18},{18,... | collective-permute-start | bytes 7077896 | tf_op jit(solution)/shard_map/ppermute | solution.py:237
  338.8 53.6 %collective-permute-start.44 = (f32[192,3072]{1,0:T(8,128)S(1)}, f32[192,3072]{1,0:T(8,128)S(1)}, u32[]{:S(2)}, u32[]{:S(2)}) collective-permute-start(f32[192,3072]{1,0:T(8,128)S(1)} %dynamic-slice_add_fusion), channel_id=1, source_target_pairs={{0,4},{2,6},{4,0},{6,2},{8,12},{10,14},{12,8},{14,10},{16,20},{18,... | collective-permute-start | bytes 7077896 | tf_op jit(solution)/shard_map/ppermute | solution.py:237
  343.2 41.5 %collective-permute-start.26 = (f32[384,1152]{1,0:T(8,128)S(1)}, f32[384,1152]{1,0:T(8,128)S(1)}, u32[]{:S(2)}, u32[]{:S(2)}) collective-permute-start(f32[384,1152]{1,0:T(8,128)S(1)} %get-tuple-element.57), channel_id=1, source_target_pairs={{0,1},{1,0},{2,3},{3,2},{4,5},{5,4},{6,7},{7,6},{8,9},{9,8},{10,11... | collective-permute-start | bytes 5308424 | tf_op jit(solution)/shard_map/ppermute | solution.py:236
  344.8 53.0 %collective-permute-start.34 = (f32[2,192,768]{2,1,0:T(8,128)S(1)}, f32[2,192,768]{2,1,0:T(8,128)S(1)}, u32[]{:S(2)}, u32[]{:S(2)}) collective-permute-start(f32[2,192,768]{2,1,0:T(8,128)S(1)} %constant_dynamic-slice_fusion.2), channel_id=1, source_target_pairs={{0,2},{2,0},{4,6},{6,4},{8,10},{10,8},{12,14},{14,12},{16,18},{18,... | collective-permute-start | bytes 3538952 | tf_op jit(solution)/shard_map/ppermute | solution.py:237
  352.8 98.7 %collective-permute-start.53 = (f32[768,768]{1,0:T(8,128)}, f32[768,768]{1,0:T(8,128)}, u32[]{:S(2)}, u32[]{:S(2)}) collective-permute-start(f32[768,768]{1,0:T(8,128)} %get-tuple-element.52), channel_id=1, source_target_pairs={{0,1},{1,0},{2,3},{3,2},{4,5},{5,4},{6,7},{7,6},{8,9},{9,8},{10,11... | collective-permute-start | bytes 7077896 | tf_op jit(solution)/shard_map/ppermute | solution.py:236
  387.6 66.9 %collective-permute-start.27 = (f32[192,1152]{1,0:T(8,128)}, f32[192,1152]{1,0:T(8,128)}, u32[]{:S(2)}, u32[]{:S(2)}) collective-permute-start(f32[192,1152]{1,0:T(8,128)} %fusion.114), channel_id=1, source_target_pairs={{0,8},{2,10},{4,12},{6,14},{8,0},{10,2},{12,4},{14,6},{16,24},{18,... | collective-permute-start | bytes 2654216 | tf_op jit(solution)/shard_map/ppermute | solution.py:237
  396.2 61.2 %collective-permute-start.45 = (f32[96,3072]{1,0:T(8,128)}, f32[96,3072]{1,0:T(8,128)}, u32[]{:S(2)}, u32[]{:S(2)}) collective-permute-start(f32[96,3072]{1,0:T(8,128)} %dynamic-slice_add_fusion.2), channel_id=1, source_target_pairs={{0,8},{2,10},{4,12},{6,14},{8,0},{10,2},{12,4},{14,6},{16,24},{18,... | collective-permute-start | bytes 3538952 | tf_op jit(solution)/shard_map/ppermute | solution.py:237
  398.7 50.0 %collective-permute-start.35 = (f32[192,768]{1,0:T(8,128)}, f32[192,768]{1,0:T(8,128)S(1)}, u32[]{:S(2)}, u32[]{:S(2)}) collective-permute-start(f32[192,768]{1,0:T(8,128)} %get-tuple-element.61), channel_id=1, source_target_pairs={{0,1},{1,0},{2,3},{3,2},{4,5},{5,4},{6,7},{7,6},{8,9},{9,8},{10,11... | collective-permute-start | bytes 1769480 | tf_op jit(solution)/shard_map/ppermute | solution.py:236
  403.2 44.7 %collective-permute-start.61 = (f32[57,128]{1,0:T(8,128)}, f32[57,128]{1,0:T(8,128)}, u32[]{:S(2)}, u32[]{:S(2)}) collective-permute-start(f32[57,128]{1,0:T(8,128)} %bitcast.134), channel_id=1, source_target_pairs={{0,1},{1,0},{2,3},{3,2},{4,5},{5,4},{6,7},{7,6},{8,9},{9,8},{10,11... | collective-permute-start | bytes 87560 | tf_op jit(solution)/shard_map/ppermute | solution.py:236
  453.8 42.2 %collective-permute-start.54 = (f32[384,768]{1,0:T(8,128)S(1)}, f32[384,768]{1,0:T(8,128)S(1)}, u32[]{:S(2)}, u32[]{:S(2)}) collective-permute-start(f32[384,768]{1,0:T(8,128)S(1)} %fusion.109), channel_id=1, source_target_pairs={{0,4},{2,6},{4,0},{6,2},{8,12},{10,14},{12,8},{14,10},{16,20},{18,... | collective-permute-start | bytes 3538952 | tf_op jit(solution)/shard_map/ppermute | solution.py:237
  460.8 100.3 %collective-permute-start.63 = (f32[57,128]{1,0:T(8,128)S(1)}, f32[57,128]{1,0:T(8,128)S(1)}, u32[]{:S(2)}, u32[]{:S(2)}) collective-permute-start(f32[57,128]{1,0:T(8,128)S(1)} %fusion.274), channel_id=1, source_target_pairs={{0,4},{2,6},{4,0},{6,2},{8,12},{10,14},{12,8},{14,10},{16,20},{18,... | collective-permute-start | bytes 87560 | tf_op jit(solution)/shard_map/ppermute | solution.py:237
  462.4 99.9 %collective-permute-start.37 = (f32[48,768]{1,0:T(8,128)S(1)}, f32[48,768]{1,0:T(8,128)S(1)}, u32[]{:S(2)}, u32[]{:S(2)}) collective-permute-start(f32[48,768]{1,0:T(8,128)S(1)} %fusion.175), channel_id=1, source_target_pairs={{0,4},{2,6},{4,0},{6,2},{8,12},{10,14},{12,8},{14,10},{16,20},{18,... | collective-permute-start | bytes 442376 | tf_op jit(solution)/shard_map/ppermute | solution.py:237
  567.7 45.4 %collective-permute-start.32 = (f32[192,1152]{1,0:T(8,128)S(1)}, f32[192,1152]{1,0:T(8,128)S(1)}, u32[]{:S(2)}, u32[]{:S(2)}) collective-permute-start(f32[192,1152]{1,0:T(8,128)S(1)} %maximum_select_fusion.9), channel_id=1, source_target_pairs={{0,8},{2,10},{4,12},{6,14},{8,0},{10,2},{12,4},{14,6},{16,24},{18,... | collective-permute-start | bytes 2654216 | tf_op jit(solution)/shard_map/ppermute | solution.py:237
  594.4 41.4 %collective-permute-start.59 = (f32[384,768]{1,0:T(8,128)S(1)}, f32[384,768]{1,0:T(8,128)S(1)}, u32[]{:S(2)}, u32[]{:S(2)}) collective-permute-start(f32[384,768]{1,0:T(8,128)S(1)} %maximum_select_fusion.8), channel_id=1, source_target_pairs={{0,4},{2,6},{4,0},{6,2},{8,12},{10,14},{12,8},{14,10},{16,20},{18,... | collective-permute-start | bytes 3538952 | tf_op jit(solution)/shard_map/ppermute | solution.py:237
  596.3 49.8 %collective-permute-start.24 = (f32[512,768]{1,0:T(8,128)S(1)}, f32[512,768]{1,0:T(8,128)S(1)}, u32[]{:S(2)}, u32[]{:S(2)}) collective-permute-start(f32[512,768]{1,0:T(8,128)S(1)} %add_add_fusion.2.refs_0_), channel_id=1, source_target_pairs={{0,1},{1,0},{2,3},{3,2},{4,5},{5,4},{6,7},{7,6},{8,9},{9,8},{10,11... | collective-permute-start | bytes 4718600 | tf_op jit(solution)/shard_map/ppermute | solution.py:236
  607.3 58.7 %collective-permute-start.23 = (f32[512,768]{1,0:T(8,128)}, f32[512,768]{1,0:T(8,128)S(1)}, u32[]{:S(2)}, u32[]{:S(2)}) collective-permute-start(f32[512,768]{1,0:T(8,128)} %get-tuple-element.38.refs_0_), channel_id=1, source_target_pairs={{0,1},{1,0},{2,3},{3,2},{4,5},{5,4},{6,7},{7,6},{8,9},{9,8},{10,11... | collective-permute-start | bytes 4718600 | tf_op jit(solution)/shard_map/ppermute | solution.py:236
  618.6 55.0 %collective-permute-start.33 = (f32[384,1152]{1,0:T(8,128)}, f32[384,1152]{1,0:T(8,128)}, u32[]{:S(2)}, u32[]{:S(2)}) collective-permute-start(f32[384,1152]{1,0:T(8,128)} %maximum_select_fusion.5), channel_id=1, source_target_pairs={{0,2},{2,0},{4,6},{6,4},{8,10},{10,8},{12,14},{14,12},{16,18},{18,... | collective-permute-start | bytes 5308424 | tf_op jit(solution)/shard_map/ppermute | solution.py:237
  635.7 43.5 %collective-permute-start.51 = (f32[384,1536]{1,0:T(8,128)}, f32[384,1536]{1,0:T(8,128)}, u32[]{:S(2)}, u32[]{:S(2)}) collective-permute-start(f32[384,1536]{1,0:T(8,128)} %maximum_select_fusion.3), channel_id=1, source_target_pairs={{0,2},{2,0},{4,6},{6,4},{8,10},{10,8},{12,14},{14,12},{16,18},{18,... | collective-permute-start | bytes 7077896 | tf_op jit(solution)/shard_map/ppermute | solution.py:237
  645.3 40.9 %collective-permute-start.60 = (f32[768,768]{1,0:T(8,128)}, f32[768,768]{1,0:T(8,128)}, u32[]{:S(2)}, u32[]{:S(2)}) collective-permute-start(f32[768,768]{1,0:T(8,128)} %maximum_select_fusion.4), channel_id=1, source_target_pairs={{0,2},{2,0},{4,6},{6,4},{8,10},{10,8},{12,14},{14,12},{16,18},{18,... | collective-permute-start | bytes 7077896 | tf_op jit(solution)/shard_map/ppermute | solution.py:237
  (127 other events, 1591.5 us)

commit v2 on v0

v2 whole, which is shorter than its diff:
```python
import functools
import types

import jax
import jax.numpy as jnp
from jax import lax
from jax.experimental import pallas as pl
from jax.experimental.pallas import tpu as pltpu
from jax.sharding import PartitionSpec as P

HEAD = 64
REGION = 256

norm_eps = 1e-06
score_weight = 0.05
big_negative = -1e30
f32 = jnp.float32
bf16 = jnp.bfloat16


def dot_nn(left, right):
    return jnp.dot(left, right, preferred_element_type=f32)


def dot_tn(left, right):
    return lax.dot_general(left, right, (((0,), (0,)), ((), ())), preferred_element_type=f32)


def dot_nt(left, right):
    return lax.dot_general(left, right, (((1,), (1,)), ((), ())), preferred_element_type=f32)


MIB = 2**20
STRIP = 384
C, Y, ZL, ZH, SIDE = range(5)


def shape(dims, dtype=f32):
    return jax.ShapeDtypeStruct(dims, dtype)


def vmem(dims, dtype=f32):
    return pltpu.VMEM(dims, dtype)


TOKEN = (8, 128)


def invoke(kernel, name, bits, arrays, specs, outs, out_specs, dep, limit, grid, scratch=(), into=None):
    single = not isinstance(outs, (list, tuple))
    outs = [outs] if single else list(outs)
    out_specs = [out_specs] if single else list(out_specs)
    count = len(arrays)
    after = [in_hbm(token) for token in dep] + ([] if into is None else [in_hbm(into)])
    first = count + len(after)
    end = first + len(outs)

    def body(bits_ref, *refs):
        kernel(bits_ref, refs[:count], refs[first:end] + refs[end + 1 :])

    anywhere = pl.BlockSpec(memory_space=pl.ANY)
    in_specs = list(specs) + [anywhere] * len(after)
    form = dict(
        in_specs=in_specs, out_specs=out_specs + [anywhere], scratch_shapes=scratch
    )
    if grid is None:
        form["in_specs"] = [pl.BlockSpec(memory_space=pltpu.SMEM)] + in_specs
    else:
        form = dict(
            grid_spec=pltpu.PrefetchScalarGridSpec(num_scalar_prefetch=1, grid=grid, **form)
        )
    *results, token = pl.pallas_call(
        body,
        out_shape=outs + [pltpu.HBM(TOKEN, f32)],
        input_output_aliases={} if into is None else {first: 0},
        compiler_params=pltpu.CompilerParams(vmem_limit_bytes=limit * MIB),
        cost_estimate=pl.CostEstimate(flops=0, bytes_accessed=0, transcendentals=0),
        name=name,
        **form,
    )(bits, *arrays, *after)
    dep[:] = [token]
    return results[0] if single else results


def call(kernel, name, bits, arrays, specs, outs, out_specs, grid, dep, limit=20, scratch=(), into=None):
    return invoke(
        kernel, name, bits, arrays, specs, outs, out_specs, dep, limit, grid, scratch, into
    )


def whole_call(kernel, name, bits, arrays, outs, dep, limit=16, hold=True):
    if hold:
        arrays = [pin(a) for a in arrays]
    count = len(arrays)
    return invoke(
        kernel, name, bits, arrays, [IN_VMEM] * count, outs, [IN_VMEM] * len(outs), dep, limit, None
    )


def pin(array):
    return pltpu.with_memory_space_constraint(array, pltpu.VMEM)


def in_hbm(array):
    return pltpu.with_memory_space_constraint(array, pltpu.HBM)


IN_VMEM = pl.BlockSpec(memory_space=pltpu.VMEM)


def place_of(bits_ref, names):
    index = 0
    for name in names:
        index = index * 2 + bits_ref[name]
    return index


def fixed(dims):
    return pl.BlockSpec(dims, lambda *a: (0,) * len(dims))


def normalize(values):
    centred = values - jnp.mean(values, axis=-1, keepdims=True)
    spread = jnp.mean(centred * centred, axis=-1, keepdims=True)
    scale = lax.rsqrt(spread + norm_eps)
    return centred * scale, scale


def norm_back(grad, unit, scale, gain):
    inner = grad * (1.0 + gain)
    return scale * (
        inner
        - jnp.mean(inner, axis=-1, keepdims=True)
        - unit * jnp.mean(inner * unit, axis=-1, keepdims=True)
    )


def cdf_of(up):
    return 0.5 + 0.5 * lax.erf(up * 0.5**0.5)


def sign_of(wide, axis):
    alpha = jnp.mean(jnp.abs(wide), axis=axis, keepdims=True)
    return (jnp.where(wide > 0, alpha, jnp.where(wide < 0, -alpha, 0.0))).astype(bf16)


def binarize(weight, axis, bits, dep):
    def kernel(bits_ref, ins, outs):
        outs[0][...] = sign_of(ins[0][...].astype(f32), axis)

    rows, columns = weight.shape
    if axis == 0:
        spec = pl.BlockSpec((rows, STRIP), lambda i, b: (0, i))
        steps = columns // STRIP
    else:
        spec = pl.BlockSpec((STRIP, columns), lambda i, b: (i, 0))
        steps = rows // STRIP
    return call(
        kernel,
        "binarize",
        bits,
        [weight],
        [spec],
        shape(weight.shape, bf16),
        spec,
        (steps,),
        dep,
    )


def binarize_pack(weights, axes, names, bits, dep):
    parts = 2 ** len(names)

    def kernel(bits_ref, ins, outs):
        part = place_of(bits_ref, names)
        at = 0
        for ref, axis, out in zip(ins, axes, outs):
            result = sign_of(ref[...].astype(f32), axis)
            out[...] = result
            rows, columns = ref.shape[0] // parts, ref.shape[1]
            mine = out[pl.ds(part * rows, rows), :].astype(f32)
            for left in range(0, columns, STRIP):
                outs[-1][at : at + rows, :] = mine[:, left : left + STRIP]
                at += rows

    total = sum(w.size for w in weights) // parts // STRIP
    return whole_call(
        kernel,
        "binarize_pack",
        bits,
        weights,
        [shape(w.shape, bf16) for w in weights] + [vmem((total, STRIP))],
        dep,
        hold=False,
    )


def pack(weights, names, bits, dep):
    parts = 2 ** len(names)

    def kernel(bits_ref, ins, outs):
        at = 0
        for ref in ins:
            rows, columns = ref.shape
            for left in range(0, columns, STRIP):
                outs[0][at : at + rows, :] = ref[:, left : left + STRIP].astype(f32)
                at += rows

    specs = [
        pl.BlockSpec((w.shape[0] // parts, w.shape[1]), lambda i, b: (place_of(b, names), 0))
        for w in weights
    ]
    total = sum(w.size for w in weights) // parts // STRIP
    return call(
        kernel,
        "pack",
        bits,
        [in_hbm(w) for w in weights],
        specs,
        [vmem((total, STRIP))],
        [IN_VMEM],
        (1,),
        dep,
    )[0]


def pack_tile(weight, row_names, column_names, bits, dep):
    def kernel(bits_ref, ins, outs):
        at = pl.multiple_of(pl.program_id(0) * tall, 8)
        outs[0][pl.ds(at, tall), :] = ins[0][...].astype(f32)

    dims = (weight.shape[0] >> len(row_names), weight.shape[1] >> len(column_names))
    steps = max(1, dims[0] // 384)
    tall = dims[0] // steps
    return call(
        kernel,
        "pack_tile",
        bits,
        [weight],
        [
            pl.BlockSpec(
                (tall, dims[1]),
                lambda i, b: (place_of(b, row_names) * steps + i, place_of(b, column_names)),
            )
        ],
        [vmem(dims)],
        [IN_VMEM],
        (steps,),
        dep,
    )[0]


def touch(array, bits, dep):
    count = len(dep)

    def body(bits_ref, *refs):
        pass

    anywhere = pl.BlockSpec(memory_space=pl.ANY)
    result, token = pl.pallas_call(
        body,
        in_specs=[pl.BlockSpec(memory_space=pltpu.SMEM)] + [anywhere] * (1 + count),
        out_specs=[anywhere] * 2,
        out_shape=[shape(array.shape, array.dtype), pltpu.HBM(TOKEN, f32)],
        input_output_aliases={1: 0},
        compiler_params=pltpu.CompilerParams(vmem_limit_bytes=MIB),
        cost_estimate=pl.CostEstimate(flops=0, bytes_accessed=0, transcendentals=0),
        name="touch",
    )(bits, array, *map(in_hbm, dep))
    dep[:] = [token]
    return result


def join(first, second, bits, dep):
    rows, columns = first.shape

    def kernel(bits_ref, ins, outs):
        for k in range(2):
            outs[0][k * rows : (k + 1) * rows, :] = ins[k][...]

    return whole_call(kernel, "join", bits, [first, second], [vmem((2 * rows, columns))], dep)[0]


def half_masks():
    lane = lax.broadcasted_iota(jnp.int32, (1, 2 * HEAD), 1)
    low = jnp.where(lane < HEAD, 1.0, 0.0).astype(bf16)
    return (low, (1.0 - low.astype(f32)).astype(bf16))


def region_masks(row_ref, col_ref):
    across = row_ref[0]
    down = col_ref[...]
    same = down == across
    live = down >= 0
    size = down.shape[0]
    diagonal = lax.broadcasted_iota(jnp.int32, (size, size), 0) == lax.broadcasted_iota(
        jnp.int32, (size, size), 1
    )
    pairs = same & live
    return pairs, pairs | diagonal


def probabilities(scores, allowed):
    masked = jnp.where(allowed, scores, big_negative)
    top = jnp.max(masked, axis=-1, keepdims=True)
    expo = jnp.exp(masked - top)
    total = jnp.sum(expo, axis=-1, keepdims=True)
    return expo * (1.0 / total)


def attention(parts, allowed, masks, scale, write):
    width = parts[0].shape[1]
    for at in range(0, width, 2 * HEAD):
        query, keys, values = (part[:, at : at + 2 * HEAD] for part in parts)
        probs = [
            probabilities(dot_nt(query * mask, keys) * scale, allowed).astype(bf16) for mask in masks
        ]
        stacked = jnp.concatenate([values * mask for mask in masks], axis=0)
        write(at, dot_nn(jnp.concatenate(probs, axis=1), stacked).astype(bf16))


def attend_own(x, weights, biases, seg_row, seg_col, bits, dep):
    rows, dim = x.shape
    width = weights[0].shape[1]

    def kernel(bits_ref, ins, outs):
        x_ref, bias_ref, row_ref, col_ref = ins[:4]
        tokens = x_ref[...]
        pairs, allowed = region_masks(row_ref, col_ref)
        masks = half_masks()
        for net in range(2):
            parts = []
            for k in range(3):
                row = 3 * net + k
                part = dot_nn(tokens, ins[4 + row][...]) + bias_ref[row : row + 1, :]
                parts.append(part.astype(bf16))
                if row < 5:
                    outs[0][:, row * width : (row + 1) * width] = parts[k]

            def write(at, mixed, net=net):
                outs[1 + net][:, at : at + 2 * HEAD] = mixed

            attention(parts, allowed, masks, HEAD ** (-0.5), write)

    def block(columns):
        return pl.BlockSpec((REGION, columns), lambda i, b: (i, 0))

    return call(
        kernel,
        "attend_own",
        bits,
        [x, biases, seg_row, seg_col, *weights],
        [
            block(dim),
            fixed(biases.shape),
            pl.BlockSpec((1, 1, REGION), lambda i, b: (i, 0, 0)),
            block(1),
        ]
        + [fixed(w.shape) for w in weights],
        [shape((rows, 5 * width), bf16), shape((rows, width), bf16), shape((rows, width), bf16)],
        [block(5 * width), block(width), block(width)],
        (rows // REGION,),
        dep,
    )


def attend_other(
    x, pieces, names, biases, seg_row, seg_col, mixed, output, model, student, bits, dep
):
    rows, dim = x.shape
    width = mixed.shape[1]
    parts = 2 ** len(names)
    half_parts = parts // 2
    tall = dim // parts
    short = width // parts
    per_part = 3 * tall + 2 * short
    first_row = 0 if student else 3
    kept = 3 if student else 2

    def kernel(bits_ref, ins, outs):
        x_ref, bias_ref, row_ref, col_ref, mine_ref, theirs_ref, mixed_ref, out_ref, model_ref = ins
        qkv_ref, low_ref, first_ref = outs[:3]
        weight_refs = outs[5:9] if student else outs[3:7]
        part = place_of(bits_ref, names)

        @pl.when(pl.program_id(0) == 0)
        def _():
            for k in range(parts):
                ref = (mine_ref, theirs_ref)[k // half_parts]
                base = (k % half_parts) * per_part
                where = jnp.bitwise_xor(part, k)
                for m in range(3):
                    weight_refs[m][pl.ds(pl.multiple_of(where * tall, 16), tall), :] = ref[
                        base + m * tall : base + (m + 1) * tall, :
                    ].astype(bf16)
                for m in range(2):
                    at = base + 3 * tall + m * short
                    weight_refs[3][
                        pl.ds(pl.multiple_of(where * short, 16), short), m * STRIP : (m + 1) * STRIP
                    ] = ref[at : at + short, :].astype(bf16)

        tokens = x_ref[...]
        pairs, allowed = region_masks(row_ref, col_ref)
        masks = half_masks()
        parts_qkv = []
        for k in range(3):
            row = first_row + k
            part_k = dot_nn(tokens, weight_refs[k][...]) + bias_ref[row : row + 1, :]
            parts_qkv.append(part_k.astype(bf16))
            if k < kept:
                qkv_ref[:, k * width : (k + 1) * width] = parts_qkv[k]
        tiles = []
        attention(parts_qkv, allowed, masks, HEAD ** (-0.5), lambda at, tile: tiles.append(tile))
        mine = jnp.concatenate(tiles, axis=1)
        pre = (
            tokens.astype(f32)
            + (dot_nn(mixed_ref[...], out_ref[...]) + dot_nn(mine, weight_refs[3][...]))
            + model_ref[0:1, :]
        )
        unit, scale = normalize(pre)
        first = unit * (1.0 + model_ref[2:3, :]) + model_ref[3:4, :]
        low_ref[...] = first.astype(bf16)
        first_ref[...] = first
        if student:
            outs[3][...] = mine
            outs[4][...] = pre

    def block(columns):
        return pl.BlockSpec((REGION, columns), lambda i, b: (i, 0))

    weights = [shape((dim, width), bf16)] * 3 + [shape((width, dim), bf16)]
    outs = [shape((rows, kept * width), bf16), shape((rows, dim), bf16), shape((rows, dim))]
    out_specs = [block(kept * width), block(dim), block(dim)]
    if student:
        outs += [shape((rows, width), bf16), shape((rows, dim)), *weights]
        out_specs += [block(width), block(dim)] + [fixed(w.shape) for w in weights]
    return call(
        kernel,
        "attend_other",
        bits,
        [x, biases, seg_row, seg_col, *map(pin, pieces), mixed, output, model],
        [
            block(dim),
            fixed(biases.shape),
            pl.BlockSpec((1, 1, REGION), lambda i, b: (i, 0, 0)),
            block(1),
            IN_VMEM,
            IN_VMEM,
            block(width),
            fixed(output.shape),
            fixed(model.shape),
        ],
        outs,
        out_specs,
        (rows // REGION,),
        dep,
        limit=24,
        scratch=[] if student else [pltpu.VMEM(w.shape, bf16) for w in weights],
    )


def activate(up, outs, student):
    cdf = cdf_of(up)
    outs[0][...] = (up * cdf).astype(bf16)
    if student:
        bell = jnp.exp(-0.5 * up * up) * (2.0 * jnp.pi) ** -0.5
        outs[1][...] = (cdf + up * bell).astype(bf16)


def up_own(low, weight, biases, first_row, student, bits, dep):
    tokens, dim = low.shape
    hidden = weight.shape[1]

    def kernel(bits_ref, ins, outs):
        j = pl.program_id(0)
        up = dot_nn(ins[0][...], ins[1][...]) + ins[2][pl.ds(first_row + j, 1), :]
        activate(up, outs, student)

    count = 2 if student else 1
    return call(
        kernel,
        "up_own",
        bits,
        [low, weight, biases],
        [fixed(low.shape), pl.BlockSpec((dim, STRIP), lambda j, b: (0, j)), fixed(biases.shape)],
        [shape((tokens, hidden), bf16)] * count,
        [pl.BlockSpec((tokens, STRIP), lambda j, b: (0, j))] * count,
        (hidden // STRIP,),
        dep,
    )


def up_other(low, mine, theirs, names, biases, first_row, student, bits, dep):
    tokens, dim = low.shape
    steps = mine.shape[0] // STRIP
    half = dim // 2

    def kernel(bits_ref, ins, outs):
        low_ref, tile_m, tile_o, bias_ref = ins
        j = jnp.bitwise_xor(pl.program_id(0), place_of(bits_ref, names))
        at = pl.ds(pl.multiple_of(pl.program_id(0) * half, 8), half)
        weight_ref = outs[2] if student else outs[1]
        core = bits_ref[C]
        weight_ref[pl.ds(pl.multiple_of(core * half, 16), half), :] = tile_m[at, :].astype(bf16)
        weight_ref[pl.ds(pl.multiple_of((1 - core) * half, 16), half), :] = tile_o[at, :].astype(bf16)
        up = dot_nn(low_ref[...], weight_ref[...]) + bias_ref[pl.ds(first_row + j, 1), :]
        activate(up, outs, student)

    def column(j, b):
        return (0, jnp.bitwise_xor(j, place_of(b, names)))

    outs = [shape((tokens, steps * STRIP), bf16)]
    out_specs = [pl.BlockSpec((tokens, STRIP), column)]
    if student:
        outs += [outs[0], shape((dim, steps * STRIP), bf16)]
        out_specs += [out_specs[0], pl.BlockSpec((dim, STRIP), column)]
    return call(
        kernel,
        "up_other",
        bits,
        [low, pin(mine), pin(theirs), biases],
        [fixed(low.shape), IN_VMEM, IN_VMEM, fixed(biases.shape)],
        outs,
        out_specs,
        (steps,),
        dep,
        limit=16,
        scratch=[] if student else [pltpu.VMEM((dim, STRIP), bf16)],
    )


def down_own(acts, weights, firsts, models, bits, dep):
    tokens, hidden = acts[0].shape
    dim = weights[0].shape[1]

    def kernel(bits_ref, ins, outs):
        for net in range(2):
            act, weight, first, model = ins[4 * net : 4 * net + 4]
            outs[net][...] = first[...] + model[1:2, :] + dot_nn(act[...], weight[...])

    def block(columns):
        return pl.BlockSpec((REGION, columns), lambda i, b: (i, 0))

    arrays = []
    specs = []
    for net in range(2):
        arrays += [acts[net], weights[net], firsts[net], models[net]]
        specs += [block(hidden), fixed((hidden, dim)), block(dim), fixed(models[net].shape)]
    return call(
        kernel,
        "down_own",
        bits,
        arrays,
        specs,
        [shape((tokens, dim))] * 2,
        [block(dim)] * 2,
        (tokens // REGION,),
        dep,
        limit=24,
    )


def down_other(acts, student_tiles, teacher_tiles, names, partials, models, seg_col, bits, dep):
    tokens, hidden = acts[0].shape
    dim = partials[0].shape[1]
    half = dim // 2
    steps = hidden // STRIP

    def kernel(bits_ref, ins, outs):
        act_s, act_t, s_mine, s_other, t_mine, t_other, part_s, part_t, model_s, model_t, seg = ins
        out_ref, pre_ref, down_ref, sums_ref, weight_ref, low_ref, teacher_ref = outs
        step = pl.program_id(0)
        first_core = bits_ref[C] == 0

        @pl.when(step == 0)
        def _():
            place = place_of(bits_ref, names)
            for k in range(steps):
                rows = slice(k * STRIP, (k + 1) * STRIP)
                where = pl.ds(pl.multiple_of(jnp.bitwise_xor(place, k) * STRIP, 16), STRIP)
                tile, other = s_mine[rows, :].astype(bf16), s_other[rows, :].astype(bf16)
                weight_ref[where, :half] = jnp.where(first_core, tile, other)
                weight_ref[where, half:] = jnp.where(first_core, other, tile)
                tile, other = t_mine[rows, :].astype(bf16), t_other[rows, :].astype(bf16)
                teacher_ref[rows, :half] = jnp.where(first_core, tile, other)
                teacher_ref[rows, half:] = jnp.where(first_core, other, tile)

        unit_s, scale_s = normalize(part_s[...] + dot_nn(act_s[...], weight_ref[...]))
        unit_t, _ = normalize(part_t[...] + dot_nn(act_t[...], teacher_ref[...]))
        gain = model_s[4:5, :]
        out_s = unit_s * (1.0 + gain) + model_s[5:6, :]
        out_t = unit_t * (1.0 + model_t[4:5, :]) + model_t[5:6, :]
        out_ref[...] = out_s
        low_ref[0] = out_s.astype(bf16)
        grad = jnp.where(seg[...] >= 0, out_s - out_t, 0.0)
        d_pre = norm_back(grad, unit_s, scale_s, gain)
        pre_ref[...] = d_pre
        low = d_pre.astype(bf16)
        down_ref[...] = low
        add_sums(sums_ref, (grad * unit_s, grad, low.astype(f32)), step)

    def block(columns):
        return pl.BlockSpec((REGION, columns), lambda i, b: (i, 0))

    return call(
        kernel,
        "down_other",
        bits,
        [*acts, *map(pin, student_tiles), *map(pin, teacher_tiles), *partials, *models, seg_col],
        [block(hidden)] * 2
        + [IN_VMEM] * 4
        + [block(dim)] * 2
        + [fixed(m.shape) for m in models]
        + [block(1)],
        [
            shape((tokens, dim)),
            shape((tokens, dim)),
            shape((tokens, dim), bf16),
            shape((8, dim)),
            shape((hidden, dim), bf16),
            pltpu.HBM((2, tokens, dim), bf16),
        ],
        [
            block(dim),
            block(dim),
            block(dim),
            fixed((8, dim)),
            fixed((hidden, dim)),
            pl.BlockSpec((1, REGION, dim), lambda i, b: (b[SIDE], i, 0)),
        ],
        (tokens // REGION,),
        dep,
        limit=28,
        scratch=[pltpu.VMEM((hidden, dim), bf16)],
    )


def up_back(d_down, weights, slopes, bits, dep):
    tokens, dim = d_down.shape
    hidden = weights[0].shape[0]

    def kernel(bits_ref, ins, outs):
        rows = []
        for half in range(2):
            grad = dot_nt(ins[0][...], ins[1 + half][...])
            low = (grad * ins[3 + half][...].astype(f32)).astype(bf16)
            outs[half][...] = low
            rows.append(jnp.sum(low.astype(f32), axis=0, keepdims=True))
        outs[2][...] = jnp.concatenate(rows + [jnp.zeros((6, STRIP), f32)], axis=0)

    block = pl.BlockSpec((tokens, STRIP), lambda j, b: (0, j))
    return call(
        kernel,
        "up_back",
        bits,
        [d_down, *weights, *slopes],
        [fixed(d_down.shape)] + [pl.BlockSpec((STRIP, dim), lambda j, b: (j, 0))] * 2 + [block] * 2,
        [shape((tokens, hidden), bf16)] * 2 + [shape((8, hidden))],
        [block, block, pl.BlockSpec((8, STRIP), lambda j, b: (0, j))],
        (hidden // STRIP,),
        dep,
    )


def add_sums(ref, arrays, step):
    rows = [jnp.sum(v, axis=0, keepdims=True) for v in arrays]
    rows.append(jnp.zeros((8 - len(rows), rows[0].shape[1]), f32))
    new = jnp.concatenate(rows, axis=0)
    ref[...] = jnp.where(step == 0, new, ref[...] + new)


def first_back(d_ups, weights, d_pre2, pre, model, outputs, bits, dep):
    tokens, hidden = d_ups[0].shape
    dim = d_pre2.shape[1]
    width = outputs[0].shape[0]

    def kernel(bits_ref, ins, outs):
        d_own, d_oth, w_own, w_oth, d_pre2_ref, pre_ref, model_ref, o_own, o_oth = ins
        grad = d_pre2_ref[...] + (dot_nt(d_own[...], w_own[...]) + dot_nt(d_oth[...], w_oth[...]))
        unit, scale = normalize(pre_ref[...])
        d_pre = norm_back(grad, unit, scale, model_ref[2:3, :])
        outs[0][...] = d_pre
        low = d_pre.astype(bf16)
        outs[1][...] = low
        outs[2][...] = dot_nt(low, o_own[...]).astype(bf16)
        outs[3][...] = dot_nt(low, o_oth[...]).astype(bf16)
        add_sums(outs[4], (grad * unit, grad, low.astype(f32)), pl.program_id(0))

    def block(columns):
        return pl.BlockSpec((REGION, columns), lambda i, b: (i, 0))

    return call(
        kernel,
        "first_back",
        bits,
        [*d_ups, *weights, d_pre2, pre, model, *outputs],
        [block(hidden)] * 2
        + [fixed(w.shape) for w in weights]
        + [block(dim)] * 2
        + [fixed(model.shape)]
        + [fixed(o.shape) for o in outputs],
        [
            shape((tokens, dim)),
            shape((tokens, dim), bf16),
            shape((tokens, width), bf16),
            shape((tokens, width), bf16),
            shape((8, dim)),
        ],
        [block(dim), block(dim), block(width), block(width), fixed((8, dim))],
        (tokens // REGION,),
        dep,
        limit=28,
    )


def token_grad(d_pre, terms, bits, dep):
    tokens, dim = d_pre.shape

    def kernel(bits_ref, ins, outs):
        total = ins[0][...]
        for k in range(len(terms)):
            total = total + dot_nt(ins[1 + 2 * k][...], ins[2 + 2 * k][...])
        outs[0][...] = total
        outs[1][0] = total

    arrays = [d_pre]
    specs = [pl.BlockSpec((REGION, dim), lambda i, b: (i, 0))]
    for grad, at, weight in terms:
        arrays += [grad, weight]
        specs += [
            pl.BlockSpec((REGION, weight.shape[1]), lambda i, b, at=at: (i, at)),
            fixed(weight.shape),
        ]
    return call(
        kernel,
        "token_grad",
        bits,
        arrays,
        specs,
        [shape((tokens, dim)), pltpu.HBM((2, tokens, dim), f32)],
        [specs[0], pl.BlockSpec((1, REGION, dim), lambda i, b: (b[SIDE], i, 0))],
        (tokens // REGION,),
        dep,
    )


def attend_back(qkv, grads, seg_row, seg_col, bits, dep):
    rows, columns = qkv[0].shape
    width = columns // 5
    step = 2 * HEAD

    def kernel(bits_ref, ins, outs):
        pairs, allowed = region_masks(ins[5], ins[6])
        weight = jnp.where(pairs, score_weight, 0.0)
        masks = half_masks()
        scale = HEAD ** (-0.5)

        @pl.when(pl.program_id(0) == 0)
        def _():
            outs[4][...] = jnp.zeros_like(outs[4])

        for part in range(2):
            for at in range(0, width, step):
                places = [(0, k) for k in range(5)] if part == 0 else [(1, 0), (1, 1), (1, 2), (2, 0), (2, 1)]
                query, keys, values, query_t, keys_t = (
                    ins[r][:, k * width + at : k * width + at + step] for r, k in places
                )
                grad = ins[3 + part][:, at : at + step]
                probs = []
                slopes = []
                for mask in masks:
                    scores = dot_nt(query * mask, keys) * scale
                    prob = probabilities(scores, allowed)
                    gap = scores - dot_nt(query_t * mask, keys_t) * scale
                    d_prob = dot_nt(grad * mask, values)
                    mean = jnp.sum(prob * d_prob, axis=-1, keepdims=True)
                    slope = prob * (d_prob - mean) + weight * gap
                    probs.append(prob.astype(bf16))
                    slopes.append(slope.astype(bf16))

                def both(array):
                    return jnp.concatenate([array * mask for mask in masks], axis=0)

                d_query = dot_nn(jnp.concatenate(slopes, axis=1), both(keys)) * scale
                d_keys = dot_tn(jnp.concatenate(slopes, axis=0), both(query)) * scale
                d_values = dot_tn(jnp.concatenate(probs, axis=0), both(grad))
                for k, result in enumerate((d_query, d_keys, d_values)):
                    low = result.astype(bf16)
                    if k < 2:
                        outs[part][:, k * width + at : k * width + at + step] = low
                    else:
                        outs[2 + part][:, at : at + step] = low
                    outs[4][part : part + 1, k * width + at : k * width + at + step] += jnp.sum(
                        low.astype(f32), axis=0, keepdims=True
                    )

    def block(columns):
        return pl.BlockSpec((REGION, columns), lambda i, b: (i, 0))

    return call(
        kernel,
        "attend_back",
        bits,
        [*qkv, *grads, seg_row, seg_col],
        [
            block(columns),
            block(3 * width),
            block(2 * width),
            block(width),
            block(width),
            pl.BlockSpec((1, 1, REGION), lambda i, b: (i, 0, 0)),
            block(1),
        ],
        [shape((rows, 2 * width), bf16)] * 2
        + [shape((rows, width), bf16)] * 2
        + [shape((8, 3 * width))],
        [block(2 * width)] * 2 + [block(width)] * 2 + [fixed((8, 3 * width))],
        (rows // REGION,),
        dep,
    )


def outer(groups, bits, dep, start=0, size=None, block=384):
    size = size or groups[0][0][0].shape[1]
    tall = size // 2
    steps = tall // block
    tokens = groups[0][0][0].shape[0]
    arrays = []
    specs = []
    for lhs, rhs, at, columns in groups:
        for half in range(2):

            def left(p, h, i, b, half=half, lhs=lhs):
                core = jnp.where(p == 0, 1 - b[C], b[C])
                where = start // block + core * steps + i
                return (0, where if lhs[0] is lhs[1] else jnp.where(h == half, where, start // block))

            arrays += [lhs[half], rhs[half]]
            specs += [
                pl.BlockSpec((tokens, block), left),
                pl.BlockSpec((tokens, columns), lambda p, h, i, b, at=at: (0, at)),
            ]
    wide = sum(g[3] for g in groups)

    def kernel(bits_ref, ins, outs):
        for phase in range(2):
            for half in range(2):

                @pl.when((pl.program_id(0) == phase) & (pl.program_id(1) == half))
                def _(phase=phase, half=half):
                    at = 0
                    row = pl.multiple_of(pl.program_id(2) * block, 8)
                    for k, group in enumerate(groups):
                        lhs, rhs = ins[4 * k + 2 * half], ins[4 * k + 2 * half + 1]
                        outs[phase][half, pl.ds(row, block), at : at + group[3]] = dot_tn(
                            lhs[...], rhs[...]
                        )
                        at += group[3]

    out = vmem((2, tall, wide))
    return call(
        kernel, "outer", bits, arrays, specs, [out, out], [IN_VMEM, IN_VMEM], (2, 2, steps), dep, limit=16
    )


def split(first, second, name, bits, dep, limit=16):
    halves, rows, columns = first.shape
    out = vmem((1, rows, columns)) if name == "x" else vmem((halves, rows // 2, columns))

    def kernel(bits_ref, ins, outs):
        for k in range(2):
            if name == "x":
                where = (pl.ds(1 - k, 1), slice(None))
            else:
                bit = bits_ref[name]
                start = (1 - bit if k == 0 else bit) * (rows // 2)
                where = (slice(None), pl.ds(pl.multiple_of(start, 8), rows // 2))
            outs[k][...] = ins[0][where] + ins[1][where]

    return whole_call(kernel, "split", bits, [first, second], [out, out], dep, limit)


def add(first, second, bits, dep):
    def kernel(bits_ref, ins, outs):
        outs[0][...] = ins[0][...] + ins[1][...]

    return whole_call(kernel, "add", bits, [first, second], [vmem(first.shape)], dep)[0]


def merge(mine, theirs, name, bits, dep):
    one, rows, columns = mine.shape

    def kernel(bits_ref, ins, outs):
        bit = bits_ref[name]
        for k in range(2):
            start = (bit if k == 0 else 1 - bit) * rows
            outs[0][:, pl.ds(pl.multiple_of(start, 8), rows)] = ins[k][...]

    return whole_call(kernel, "merge", bits, [mine, theirs], [vmem((1, 2 * rows, columns))], dep)[0]


def finish(pieces, cuts, outs, bits, dep, into=None):
    def kernel(bits_ref, ins, refs):
        results, sems = refs[:-1], refs[-1]
        copies = []
        for k, (piece, source, out, target) in enumerate(cuts):
            copy = pltpu.make_async_copy(
                ins[piece].at[source], results[out].at[target(bits_ref)], sems.at[k]
            )
            copy.start()
            copies.append(copy)
        for copy in copies:
            copy.wait()

    return invoke(
        kernel,
        "finish",
        bits,
        [*map(pin, pieces)],
        [IN_VMEM] * len(pieces),
        [pltpu.HBM(o.shape, o.dtype) for o in outs],
        [pl.BlockSpec(memory_space=pl.ANY)] * len(outs),
        dep,
        8,
        None,
        [pltpu.SemaphoreType.DMA((len(cuts),))],
        into,
    )


def flip(array, bits, dep):
    def kernel(bits_ref, ins, outs):
        outs[0][...] = ins[0][0].T

    one, rows, columns = array.shape
    return whole_call(kernel, "flip", bits, [array], [vmem((columns, rows))], dep)[0]


def put_rows(array, bits, dep, into):
    two, rows, dim = into.shape
    tall = rows // 4

    def kernel(bits_ref, ins, outs):
        at = pl.ds(pl.multiple_of(pl.program_id(0) * tall, 8), tall)
        outs[-1][0] = ins[0][at, :].astype(into.dtype)

    return call(
        kernel,
        "place",
        bits,
        [pin(array)],
        [IN_VMEM],
        [pltpu.HBM(into.shape, into.dtype)],
        [pl.BlockSpec((1, tall, dim), lambda i, b: (1 - b[SIDE], i, 0))],
        (4,),
        dep,
        into=into,
    )[0]


def collect(sums, other, bits, dep):
    wide = sum(s.shape[1] for s in sums)

    def kernel(bits_ref, ins, outs):
        at = 0
        for k, ref in enumerate(ins):
            columns = ref.shape[1]
            if other and k < 2:
                both = jnp.concatenate([ref[1:2, :], ref[0:1, :], ref[2:, :]], axis=0)
            else:
                both = ref[...]
            outs[0][:, at : at + columns] = both
            at += columns

    return whole_call(kernel, "collect", bits, sums, [vmem((8, wide))], dep)[0]


R0, R1, E0, E1, QK, VO, SUMS = range(7)
(
    DO_B0,
    DO_B1,
    DO_BIN_A,
    DO_BIN_E,
    DO_BIN_R,
    DO_ATT_O,
    DO_KBT,
    DO_KBS,
    DO_UP_OT,
    DO_UP_OS,
    DO_UP_XT,
    DO_UP_XS,
    DO_DN_O,
    DO_KD,
    DO_S,
    DO_TT,
    DO_SF,
    DO_TF,
    DO_DU,
    DO_DH1,
    DO_ATT,
    DO_TOK,
    DO_O_R0,
    DO_O_R1,
    DO_O_E0,
    DO_O_E1,
    DO_O_QK,
    DO_O_VO,
) = range(28)
OUTERS = (DO_O_R0, DO_O_R1, DO_O_E0, DO_O_E1, DO_O_QK, DO_O_VO)
CHUNK_STEP, FETCH_STEP = 50, 60
PATHS = {
    R0: ("x", Y, ZL, ZH),
    R1: ("x", Y, ZL, ZH),
    E0: (Y, ZL, "x", ZH),
    E1: (ZL, "x", ZH, Y),
    QK: ("x", Y, ZL, ZH),
    VO: (ZL, Y, "x", ZH),
}
FETCH = ((Y,), (Y, ZL), (Y, ZL), (Y, ZL), (ZL, Y))
ORDER = (
    FETCH_STEP + 3, DO_B0, DO_BIN_A, DO_B1, DO_BIN_E, DO_BIN_R, FETCH_STEP + 2, FETCH_STEP + 3,
    FETCH_STEP + 5, FETCH_STEP + 6, FETCH_STEP + 1, FETCH_STEP + 2, FETCH_STEP + 3, DO_ATT_O,
    FETCH_STEP + 2, FETCH_STEP + 1, FETCH_STEP + 3, FETCH_STEP + 4, FETCH_STEP + 5,
    FETCH_STEP + 4, FETCH_STEP + 1, FETCH_STEP + 2, FETCH_STEP + 3, FETCH_STEP + 1, DO_KBT,
    FETCH_STEP + 4, FETCH_STEP + 2, FETCH_STEP + 5, DO_KBS, DO_UP_OT, DO_UP_XT, DO_UP_OS,
    DO_DN_O, FETCH_STEP + 4, FETCH_STEP + 5, FETCH_STEP + 6, FETCH_STEP + 4, DO_UP_XS,
    FETCH_STEP + 5, FETCH_STEP + 6, DO_KD, DO_DU, DO_O_R0, DO_O_E1, CHUNK_STEP + R0,
    CHUNK_STEP + E1, DO_O_E0, CHUNK_STEP + E0, DO_O_R1, CHUNK_STEP + R1, CHUNK_STEP + E1,
    CHUNK_STEP + R0, DO_DH1, DO_ATT, DO_O_VO, CHUNK_STEP + VO, DO_O_QK, CHUNK_STEP + R0,
    CHUNK_STEP + E1, CHUNK_STEP + QK, CHUNK_STEP + VO, CHUNK_STEP + R1, DO_TOK,
    CHUNK_STEP + QK, CHUNK_STEP + E0, CHUNK_STEP + R0, CHUNK_STEP + E1, CHUNK_STEP + E1,
    CHUNK_STEP + R0, CHUNK_STEP + VO, CHUNK_STEP + E0, CHUNK_STEP + R0, CHUNK_STEP + E1,
    CHUNK_STEP + R1, DO_S, CHUNK_STEP + E0, CHUNK_STEP + QK, DO_TT, CHUNK_STEP + E1,
    CHUNK_STEP + VO, CHUNK_STEP + E0, CHUNK_STEP + SUMS, CHUNK_STEP + VO, CHUNK_STEP + R0,
    CHUNK_STEP + SUMS, CHUNK_STEP + E0, CHUNK_STEP + R1, CHUNK_STEP + SUMS, CHUNK_STEP + E1,
    CHUNK_STEP + QK, CHUNK_STEP + R1, CHUNK_STEP + SUMS, CHUNK_STEP + VO, CHUNK_STEP + R0,
    CHUNK_STEP + QK, CHUNK_STEP + R1, CHUNK_STEP + E0, CHUNK_STEP + VO, CHUNK_STEP + R1,
    CHUNK_STEP + QK, CHUNK_STEP + SUMS, DO_TF, CHUNK_STEP + QK, CHUNK_STEP + E0,
    CHUNK_STEP + R1, DO_SF, CHUNK_STEP + E1, CHUNK_STEP + E0, CHUNK_STEP + R0,
    CHUNK_STEP + SUMS, CHUNK_STEP + R1, CHUNK_STEP + QK, CHUNK_STEP + VO, CHUNK_STEP + QK,
    CHUNK_STEP + VO,
)


def on_device(n_wide, tokens, segments, *params):
    (w_q, w_k, w_v, w_o, w_e, w_r, heads_s, model_s, hidden_s) = params[:9]
    (t_q, t_k, t_v, t_o, t_e, t_r, heads_t, model_t, hidden_t) = params[9:]
    n_bits = n_wide.bit_length() - 1
    side = lax.axis_index("narrow")
    place = lax.axis_index("wide")
    bits = jnp.stack([(place >> b) & 1 for b in range(4)] + [side]).astype(jnp.int32)
    dim, width = w_q.shape
    hidden = w_e.shape[1]

    def swap(array, bit):
        if bit == "x":
            return lax.ppermute(array, "narrow", [(0, 1), (1, 0)])
        return lax.ppermute(array, "wide", [(i, i ^ (1 << bit)) for i in range(n_wide)])

    x = lax.dynamic_index_in_dim(tokens, side, 0, keepdims=False)
    segment = lax.dynamic_index_in_dim(segments, side, 0, keepdims=False)
    rows = x.shape[0]
    seg_row = segment.reshape(rows // REGION, 1, REGION)
    seg_col = segment.reshape(rows, 1)
    biases = jnp.concatenate(
        [heads_s, heads_t, hidden_s.reshape(-1, width), hidden_t.reshape(-1, width)]
    )
    blocks = hidden // width
    models = (model_s, model_t)
    half = hidden // 2

    v = types.SimpleNamespace()
    fetched = {}
    last = []

    def fetch(key, made, path):
        held = swap(made(), "x")
        yield
        held = touch(held, bits, last)
        for name in path:
            got = swap(held, name)
            yield
            held = join(held, got, bits, last)
        got = swap(held, C)
        yield
        fetched[key] = (held, touch(got, bits, last))
        yield

    def fetch_direct(key, made):
        zero = swap(made(), "x")
        yield
        zero = touch(zero, bits, last)
        got = swap(zero, C)
        yield
        fetched[key] = (zero, touch(got, bits, last))
        yield

    def reduce_chunk(made, path):
        send, keep = made
        got = swap(touch(send, bits, last), C)
        yield
        for name in path[:-1]:
            send, keep = split(keep, got, name, bits, last)
            got = swap(send, name)
            yield
        block = add(keep, got, bits, last)
        got = swap(block, path[-1])
        yield
        for extra in range(4, n_bits):
            block = block + got
            got = swap(block, extra)
        block = add(block, got, bits, last)
        back = [name for name in reversed(path[:-1]) if name != "x"] + [C]
        for name in back[:-1]:
            got = swap(block, name)
            yield
            block = merge(block, got, name, bits, last)
        got = swap(block, C)
        yield
        yield (block, got)

    def small_sums():
        sums = [v.sums_qkv, v.sums_up, v.sums1, v.sums2]
        total = collect(sums, False, bits, last)
        got = swap(collect(sums, True, bits, last), "x")
        yield
        for b in range(4):
            total = add(total, got, bits, last)
            got = swap(total, b)
            yield
        total = add(total, got, bits, last)
        for b in range(4, n_bits):
            total = total + swap(total, b)
        yield total

    tall = dim // 2
    steps = {}
    fetching = {}
    outs = types.SimpleNamespace(reduce=None, expand=None)

    def names_of(k):
        return (C, *reversed(FETCH[k - 1]))

    def start_fetch(k):
        names = names_of(k)
        makers = {
            1: lambda: pack([t_q, t_k, t_v, t_o], names, bits, last),
            2: lambda: touch(v.b_pack, bits, last),
            3: lambda: pack_tile(t_e, (C,), names[1:], bits, last),
            4: lambda: pack_tile(v.b_e, (C,), names[1:], bits, last),
            5: lambda: pack_tile(v.b_r, names[1:], (C,), bits, last),
        }
        return fetch(k, makers[k], FETCH[k - 1])

    def do(name):
        if name == DO_B0:
            v.biases_oth = swap(touch(biases, bits, last), "x")
        elif name == DO_B1:
            v.biases_oth = touch(v.biases_oth, bits, last)
        elif name == DO_BIN_A:
            *v.b, v.b_pack = binarize_pack(
                [w_q, w_k, w_v, w_o], (0, 0, 0, 1), names_of(2), bits, last
            )
        elif name == DO_BIN_E:
            v.b_e = binarize(w_e, 0, bits, last)
        elif name == DO_BIN_R:
            v.b_r = binarize(w_r, 1, bits, last)
        elif name == DO_ATT_O:
            b = v.b
            v.qkv_own, *v.mixed_own = attend_own(
                x,
                (b[0], b[1], b[2], in_hbm(t_q), in_hbm(t_k), in_hbm(t_v)),
                biases,
                seg_row,
                seg_col,
                bits,
                last,
            )
        elif name == DO_KBT:
            v.qk_t, v.low_t, v.first_t = attend_other(
                x,
                fetched[1],
                names_of(1),
                v.biases_oth,
                seg_row,
                seg_col,
                v.mixed_own[1],
                t_o,
                model_t,
                False,
                bits,
                last,
            )
        elif name == DO_KBS:
            v.qkv_oth, v.low_s, v.first_s, v.mixed_oth, v.pre_s, *v.o = attend_other(
                x,
                fetched[2],
                names_of(2),
                v.biases_oth,
                seg_row,
                seg_col,
                v.mixed_own[0],
                v.b[3],
                model_s,
                True,
                bits,
                last,
            )
        elif name == DO_UP_OT:
            (v.act_t_own,) = up_own(v.low_t, t_e, biases, 6 + blocks, False, bits, last)
        elif name == DO_UP_OS:
            v.act_s_own, v.slope_own = up_own(
                v.low_s, v.b_e, biases, 6, True, bits, last
            )
        elif name == DO_UP_XT:
            (v.act_t_oth,) = up_other(
                v.low_t, *fetched[3], names_of(3)[1:], v.biases_oth, 6 + blocks, False, bits, last
            )
        elif name == DO_UP_XS:
            v.act_s_oth, v.slope_oth, v.o_e = up_other(
                v.low_s, *fetched[4], names_of(4)[1:], v.biases_oth, 6, True, bits, last
            )
        elif name == DO_DN_O:
            v.partials = down_own(
                (v.act_s_own, v.act_t_own),
                (v.b_r, t_r),
                (v.first_s, v.first_t),
                models,
                bits,
                last,
            )
        elif name == DO_KD:
            v.out_s, v.d_pre2, v.d_down, v.sums2, v.o_r, v.out_low = down_other(
                (v.act_s_oth, v.act_t_oth),
                fetched[5],
                fetched[6],
                names_of(5)[1:],
                v.partials,
                models,
                seg_col,
                bits,
                last,
            )
        elif name == DO_S:
            v.out_other = swap(touch(v.out_s, bits, last), "x")
        elif name == DO_TT:
            v.tok_other = swap(touch(v.d_tokens, bits, last), "x")
        elif name in (DO_SF, DO_TF):
            if name == DO_SF:
                outs.low = put_rows(v.out_other, bits, last, v.out_low)
            else:
                outs.tok = put_rows(v.tok_other, bits, last, v.out_tok)
        elif name == DO_DU:
            v.d_up_own, v.d_up_oth, v.sums_up = up_back(
                v.d_down,
                (v.b_r, v.o_r),
                (v.slope_own, v.slope_oth),
                bits,
                last,
            )
        elif name == DO_DH1:
            v.d_pre1, v.d_attn, *v.d_mixed, v.sums1 = first_back(
                (v.d_up_own, v.d_up_oth),
                (v.b_e, v.o_e),
                v.d_pre2,
                v.pre_s,
                model_s,
                (v.b[3], v.o[3]),
                bits,
                last,
            )
        elif name == DO_ATT:
            *v.dqk, v.dv_own, v.dv_oth, v.sums_qkv = attend_back(
                (v.qkv_own, v.qkv_oth, v.qk_t), v.d_mixed, seg_row, seg_col, bits, last
            )
        elif name == DO_TOK:
            terms = []
            for d_qk, d_v, weights in (
                (v.dqk[0], v.dv_own, v.b),
                (v.dqk[1], v.dv_oth, v.o),
            ):
                terms += [(d_qk, 0, weights[0]), (d_qk, 1, weights[1]), (d_v, 0, weights[2])]
            v.d_tokens, v.out_tok = token_grad(v.d_pre1, terms, bits, last)
        elif name in OUTERS:
            chunk = OUTERS.index(name)
            part = chunk % 2
            if chunk in (R0, R1):
                acts = (v.act_s_own, v.act_s_oth)
                made = outer([(acts, (v.d_down,) * 2, 0, dim)], bits, last, half * part, half)
            elif chunk in (E0, E1):
                d_ups = (v.d_up_own, v.d_up_oth)
                made = outer([((v.low_s,) * 2, d_ups, part, half)], bits, last)
            elif chunk == QK:
                made = outer([((x, x), v.dqk, 0, 2 * width)], bits, last)
            else:
                mixed = (v.mixed_own[0], v.mixed_oth)
                made = outer(
                    [
                        ((x, x), (v.dv_own, v.dv_oth), 0, width),
                        ((v.d_attn,) * 2, mixed, 0, width),
                    ],
                    bits,
                    last,
                )
            steps[chunk] = reduce_chunk(made, PATHS[chunk])
        elif name >= FETCH_STEP:
            k = name - FETCH_STEP
            if k not in fetching:
                fetching[k] = (
                    fetch_direct(6, lambda: pack_tile(t_r, (), (C,), bits, last))
                    if k == 6
                    else start_fetch(k)
                )
            next(fetching[k])
        else:
            chunk = name - CHUNK_STEP
            if chunk == SUMS and chunk not in steps:
                steps[chunk] = small_sums()
            pieces = next(steps[chunk])
            if pieces is None:
                return
            if chunk == SUMS:
                outs.sums = pieces
                return

            def rows_of(k, b):
                place = b[C] if k == 0 else 1 - b[C]
                return pl.ds(pl.multiple_of(place * tall, 8), tall)

            everything = (0, slice(None), slice(None))
            if chunk in (R0, R1):
                base = (chunk % 2) * dim

                def target(k):
                    def at(b):
                        place = b[C] if k == 0 else 1 - b[C]
                        return (pl.ds(pl.multiple_of(base + place * tall, 8), tall), slice(None))

                    return at

                cuts = [(k, everything, 0, target(k)) for k in range(2)]
                (outs.reduce,) = finish(
                    pieces, cuts, [shape((hidden, dim))], bits, last, outs.reduce
                )
            elif chunk in (E0, E1):
                left = (chunk % 2) * half
                cuts = [
                    (k, everything, 0, lambda b, k=k: (rows_of(k, b), pl.ds(left, half)))
                    for k in range(2)
                ]
                (outs.expand,) = finish(
                    pieces, cuts, [shape((dim, hidden))], bits, last, outs.expand
                )
            else:
                cuts = []
                if chunk == VO:
                    pieces = [*pieces]
                    for k in range(2):
                        pieces.append(flip(pieces[k][:, :, width:], bits, last))
                        cuts.append(
                            (2 + k, (slice(None), slice(None)), 1, lambda b, k=k: (slice(None), rows_of(k, b)))
                        )
                for j in range(1 if chunk == VO else 2):
                    source = (0, slice(None), pl.ds(j * width, width))
                    cuts += [
                        (k, source, j, lambda b, k=k: (rows_of(k, b), slice(None))) for k in range(2)
                    ]
                dims = [(dim, width), (width, dim) if chunk == VO else (dim, width)]
                pair = finish(pieces, cuts, [shape(d) for d in dims], bits, last)
                if chunk == VO:
                    outs.value, outs.output = pair
                else:
                    outs.query, outs.key = pair

    for name in ORDER:
        do(name)
    small = outs.sums
    n_qkv, n_up = 3 * width, hidden
    out_heads = small[0, :n_qkv].reshape(3, width)
    out_hidden = small[0, n_qkv : n_qkv + n_up]
    first, second = (small[:3, n_qkv + n_up + k * dim :][:, :dim] for k in range(2))
    out_model = jnp.stack([first[2], second[2], first[0], first[1], second[0], second[1]])
    return (
        outs.low,
        outs.tok,
        outs.query,
        outs.key,
        outs.value,
        outs.output,
        outs.expand,
        outs.reduce,
        out_heads,
        out_model,
        out_hidden,
    )


def solution(mesh):
    cols = P(None, "narrow")
    rows = P("narrow", None)
    net = (cols, cols, cols, rows, cols, rows, cols, P(), P("narrow"))
    data = P(None, "wide", None)
    return jax.shard_map(
        functools.partial(on_device, mesh.shape["wide"]),
        mesh=mesh,
        in_specs=(data, P(None, "wide")) + net + net,
        out_specs=(data, data) + net,
        check_vma=False,
    )
```

time: 1040 us -> 442 us (0.42)
  waiting for transfers between devices: 640 us -> 147 us
  matrix products: 226 us -> 0 us
  Pallas kernels: 0 us -> 190 us
  starting transfers between devices: 0.78 us -> 68 us
  blocking collectives: 62.1 us -> 0 us
  other arithmetic: 55.2 us -> 0.64 us
  between operations: 16 us -> 2.78 us
    psum x5 -> x0, waiting for transfers between devices: 640 us -> none  [the longest x1 261 us: on_device(): lax.psum((totals[0], totals[1], totals[2], totals[3], totals[4], totals[5...]
    dot_general x62 -> x0, matrix products: 214 us -> none  [the longest x22 77.4 us: matmul(): return jnp.dot(left, right, preferred_element_type=jnp.float32)]
    pallas_call x0 -> x118, Pallas kernels: none -> 190 us  [the longest x95 177 us: invoke(): pl.pallas_call(body, out_shape=outs + [pltpu.HBM(TOKEN, f32)], input_outp...]
    ppermute x0 -> x77, waiting for transfers between devices: none -> 147 us  [the longest x61 102 us: swap(): lax.ppermute(array, 'wide', [(i, i ^ 1 << bit) for i in range(n_wide)])]
    ppermute x0 -> x77, starting transfers between devices: none -> 68 us  [the longest x61 46.5 us: swap(): lax.ppermute(array, 'wide', [(i, i ^ 1 << bit) for i in range(n_wide)])]
    psum x1 -> x0, blocking collectives: 62.1 us -> none  [on_device(): lax.psum((totals[0], totals[1], totals[2], totals[3], totals[4], totals[5...]
    reduce_sum x26 -> x0, other arithmetic: 42.7 us -> none  [the longest x5 11.8 us: layer_norm(): centred = values - jnp.mean(values, axis=-1, keepdims=True)]
    sub x2 -> x0, matrix products: 12.3 us -> none  [attend(): expo = jnp.exp(masked - top)]
  transfers between devices with their start and end apart: 5 -> 77, of which waited for: 5 -> 33; matrix products, arithmetic and copies ran while one was open for 4% -> 0% of each run, Pallas kernels for 0% -> 37%
where the time goes in v2:
time: 442 us; the launch traced here: 438 us
  Pallas kernels  190 us (43%)
  waiting for transfers between devices  147 us (33%)
  starting transfers between devices  68 us (15%)
  local copies, waits for them, and re-layouts  30.5 us (7%)
    pallas_call x95, Pallas kernels, invoke(): pl.pallas_call(body, out_shape=outs + [pltpu.HBM(TOKEN, f32)], input_outp...  177 us
    ppermute x61, waiting for transfers between devices, swap(): lax.ppermute(array, 'wide', [(i, i ^ 1 << bit) for i in range(n_wide)])  102 us
    ppermute x61, starting transfers between devices, swap(): lax.ppermute(array, 'wide', [(i, i ^ 1 << bit) for i in range(n_wide)])  46.5 us
    ppermute x16, waiting for transfers between devices, swap(): return lax.ppermute(array, 'narrow', [(0, 1), (1, 0)])  44.9 us
    unnamed x157, local copies, waits for them, and re-layouts  28.8 us
    ppermute x16, starting transfers between devices, swap(): return lax.ppermute(array, 'narrow', [(0, 1), (1, 0)])  21.5 us
    pallas_call x23, Pallas kernels, touch(): pl.pallas_call(body, in_specs=[pl.BlockSpec(memory_space=pltpu.SMEM)] + [...  12.4 us
  transfers between devices with their start and end apart: 77, of which 33 were waited for; matrix products, arithmetic and copies ran while one was open for 0% of the time, Pallas kernels for 37%

profile of v2, /device:TPU:0, one launch (start us, length us, event | category | flops | bytes accessed | tf_op | source)
XLA Modules:
  0.0 438.3 jit_solution(15335862365735420738)
XLA Ops:
  15.5 5.5 %collective-permute-done.refs_0_ = f32[14,384]{1,0:T(8,128)S(1)} collective-permute-done((f32[14,384]{1,0:T(8,128)S(1)}, f32[14,384]{1,0:T(8,128)S(1)}, u32[]{:S(2)}, u32[]{:S(2)}) %collective-permute-start) | collective-permute-done | bytes 21536 | tf_op jit(solution)/shard_map/ppermute | solution.py:1057
  39.2 5.4 %collective-permute-done.1.refs_0_ = f32[384,384]{1,0:T(8,128)} collective-permute-done((f32[384,384]{1,0:T(8,128)S(1)}, f32[384,384]{1,0:T(8,128)}, u32[]{:S(2)}, u32[]{:S(2)}) %collective-permute-start.1) | collective-permute-done | bytes 589856 | tf_op jit(solution)/shard_map/ppermute | solution.py:1057
  53.2 9.6 %attend_own.1 = (bf16[512,1920]{1,0:T(8,128)(2,1)S(1)}, bf16[512,384]{1,0:T(8,128)(2,1)S(1)}, bf16[512,384]{1,0:T(8,128)(2,1)S(1)}, f32[8,128]{1,0:T(8,128)}) custom-call(s32[5]{0:T(128)S(1)} %stack.27.bits_ref, bf16[512,768]{1,0:T(8,128)(2,1)S(1)} %dynamic-slice_bitcast_fusion.refs_0_.refs_2_, f32[14,384]{1,0:T(8,128)S(1)} %pad_maximum_fusion.refs_1_.refs_2_, ...), custom_call_target="tpu_custom_call" | custom-call | tf_op jit(solution)/shard_map/attend_own/pallas_call | solution.py:72
  78.2 9.9 %collective-permute-done.10.refs_0_ = f32[384,384]{1,0:T(8,128)S(1)} collective-permute-done((f32[384,384]{1,0:T(8,128)S(1)}, f32[384,384]{1,0:T(8,128)S(1)}, u32[]{:S(2)}, u32[]{:S(2)}) %collective-permute-start.10) | collective-permute-done | bytes 589856 | tf_op jit(solution)/shard_map/ppermute | solution.py:1057
  88.6 8.8 %collective-permute-done.9.refs_0_ = f32[384,384]{1,0:T(8,128)S(1)} collective-permute-done((f32[384,384]{1,0:T(8,128)S(1)}, f32[384,384]{1,0:T(8,128)S(1)}, u32[]{:S(2)}, u32[]{:S(2)}) %collective-permute-start.9) | collective-permute-done | bytes 589856 | tf_op jit(solution)/shard_map/ppermute | solution.py:1057
  104.4 6.6 %attend_other.2 = (bf16[512,768]{1,0:T(8,128)(2,1)S(1)}, bf16[512,768]{1,0:T(8,128)(2,1)S(1)}, f32[512,768]{1,0:T(8,128)S(1)}, f32[8,128]{1,0:T(8,128)}) custom-call(s32[5]{0:T(128)S(1)} %stack.27.bits_ref, bf16[512,768]{1,0:T(8,128)(2,1)S(1)} %dynamic-slice_bitcast_fusion.refs_0_.refs_2_, f32[14,384]{1,0:T(8,128)S(1)} %get-tuple-element.312.refs_1_.refs_3_, ...), custom_call_target="tpu_custom_call" | custom-call | tf_op jit(solution)/shard_map/attend_other/pallas_call | solution.py:72
  111.0 5.5 %collective-permute-done.12.refs_1_ = f32[384,384]{1,0:T(8,128)S(1)} collective-permute-done((f32[384,384]{1,0:T(8,128)S(1)}, f32[384,384]{1,0:T(8,128)S(1)}, u32[]{:S(2)}, u32[]{:S(2)}) %collective-permute-start.12) | collective-permute-done | bytes 589856 | tf_op jit(solution)/shard_map/ppermute | solution.py:1058
  120.2 7.2 %attend_other.3 = (bf16[512,1152]{1,0:T(8,128)(2,1)S(1)}, bf16[512,768]{1,0:T(8,128)(2,1)S(1)}, f32[512,768]{1,0:T(8,128)S(1)}, bf16[512,384]{1,0:T(8,128)(2,1)S...) custom-call(s32[5]{0:T(128)S(1)} %stack.27.bits_ref, ...), custom_call_target="tpu_custom_call" | custom-call | tf_op jit(solution)/shard_map/attend_other/pallas_call | solution.py:72
  135.3 4.4 %up_own.3 = (bf16[512,1536]{1,0:T(8,128)(2,1)S(1)}, bf16[512,1536]{1,0:T(8,128)(2,1)S(1)}, f32[8,128]{1,0:T(8,128)}) custom-call(s32[5]{0:T(128)S(1)} %stack.27.bits_ref, bf16[512,768]{1,0:T(8,128)(2,1)S(1)} %get-tuple-element.364.refs_0_.refs_2_, bf16[768,1536]{1,0:T(8,128)(2,1)S(1)} %copy-done.3, f32[14,384]{1,0:T(8,128)S(1)} %pad_maximum_fusion.refs_1_.refs_2_, ...), custom_call_target="tpu_custom_call" | custom-call | tf_op jit(solution)/shard_map/up_own/pallas_call | solution.py:72
  148.1 5.3 %collective-permute-done.18.refs_0_ = f32[1536,384]{1,0:T(8,128)S(1)} collective-permute-done((f32[1536,384]{1,0:T(8,128)}, f32[1536,384]{1,0:T(8,128)S(1)}, u32[]{:S(2)}, u32[]{:S(2)}) %collective-permute-start.18) | collective-permute-done | bytes 2359328 | tf_op jit(solution)/shard_map/ppermute | solution.py:1057
  154.6 4.7 %up_other.3 = (bf16[512,1536]{1,0:T(8,128)(2,1)S(1)}, bf16[512,1536]{1,0:T(8,128)(2,1)S(1)}, bf16[768,1536]{1,0:T(8,128)(2,1)S(1)}, f32[8,128]{1,0:T(8,128)}) custom-call(s32[5]{0:T(128)S(1)} %stack.27.bits_ref, bf16[512,768]{1,0:T(8,128)(2,1)S(1)} %get-tuple-element.364.refs_0_.refs_2_, f32[1536,384]{1,0:T(8,128)S(1)} %get-tuple-element.377.refs_1_, ...), custom_call_target="tpu_custom_call" | custom-call | tf_op jit(solution)/shard_map/up_other/pallas_call | solution.py:72
  165.7 6.3 %down_other.1 = (f32[512,768]{1,0:T(8,128)S(1)}, f32[512,768]{1,0:T(8,128)S(1)}, bf16[512,768]{1,0:T(8,128)(2,1)S(1)}, f32[8,768]{1,0:T(8,128)S(1)}, bf16[1536,7...) custom-call(s32[5]{0:T(128)S(1)} %stack.27.bits_ref, ...), custom_call_target="tpu_custom_call" | custom-call | tf_op jit(solution)/shard_map/down_other/pallas_call | solution.py:72
  174.5 5.2 %up_back.1 = (bf16[512,1536]{1,0:T(8,128)(2,1)S(1)}, bf16[512,1536]{1,0:T(8,128)(2,1)S(1)}, f32[8,1536]{1,0:T(8,128)S(1)}, f32[8,128]{1,0:T(8,128)}) custom-call(s32[5]{0:T(128)S(1)} %stack.27.bits_ref, bf16[512,768]{1,0:T(8,128)(2,1)S(1)} %get-tuple-element.397.refs_0_.refs_1_.refs_3_, bf16[1536,768]{1,0:T(8,128)(2,1)S(1)} %copy-done.5, ...), custom_call_target="tpu_custom_call" | custom-call | tf_op jit(solution)/shard_map/up_back/pallas_call | solution.py:72
  192.9 4.5 %outer.9 = (f32[2,384,768]{2,1,0:T(8,128)}, f32[2,384,768]{2,1,0:T(8,128)S(1)}, f32[8,128]{1,0:T(8,128)}) custom-call(s32[5]{0:T(128)S(1)} %stack.27.bits_ref, bf16[512,1536]{1,0:T(8,128)(2,1)S(1)} %get-tuple-element.371.refs_0_, bf16[512,768]{1,0:T(8,128)(2,1)S(1)} %get-tuple-element.397.refs_0_.refs_1_.refs_3_, ...), custom_call_target="tpu_custom_call" | custom-call | tf_op jit(solution)/shard_map/outer/pallas_call | solution.py:72
  203.6 6.4 %first_back.1 = (f32[512,768]{1,0:T(8,128)S(1)}, bf16[512,768]{1,0:T(8,128)(2,1)S(1)}, bf16[512,384]{1,0:T(8,128)(2,1)S(1)}, bf16[512,384]{1,0:T(8,128)(2,1)S(1)...) custom-call(s32[5]{0:T(128)S(1)} %stack.27.bits_ref, bf16[512,1536]{1,0:T(8,128)(2,1)S(1)} %get-tuple-element.402.refs_1_.refs_0_, ...), custom_call_target="tpu_custom_call" | custom-call | tf_op jit(solution)/shard_map/first_back/pallas_call | solution.py:72
  210.1 11.9 %attend_back.1 = (bf16[512,768]{1,0:T(8,128)(2,1)S(1)}, bf16[512,768]{1,0:T(8,128)(2,1)S(1)}, bf16[512,384]{1,0:T(8,128)(2,1)S(1)}, bf16[512,384]{1,0:T(8,128)(2...) custom-call(s32[5]{0:T(128)S(1)} %stack.27.bits_ref, bf16[512,1920]{1,0:T(8,128)(2,1)S(1)} %copy-done.36, ...), custom_call_target="tpu_custom_call" | custom-call | tf_op jit(solution)/shard_map/attend_back/pallas_call | solution.py:72
  240.7 4.7 %token_grad.1 = (f32[512,768]{1,0:T(8,128)S(1)}, f32[2,512,768]{2,1,0:T(8,128)}, f32[8,128]{1,0:T(8,128)}) custom-call(s32[5]{0:T(128)S(1)} %stack.27.bits_ref, f32[512,768]{1,0:T(8,128)S(1)} %get-tuple-element.467.refs_0_, bf16[512,768]{1,0:T(8,128)(2,1)S(1)} %get-tuple-element.444.refs_1_.refs_3_, bf16[768,384]{1,0:T(8,128)(2,1)S(1)} %copy-done.17, ...), custom_call_target="tpu_custom_call" | custom-call | tf_op jit(solution)/shard_map/token_grad/pallas_call | solution.py:72
  256.9 13.7 %collective-permute-done.33.refs_1_ = f32[1,96,768]{2,1,0:T(8,128)S(1)} collective-permute-done((f32[1,96,768]{2,1,0:T(8,128)S(1)}, f32[1,96,768]{2,1,0:T(8,128)S(1)}, u32[]{:S(2)}, u32[]{:S(2)}) %collective-permute-start.33) | collective-permute-done | bytes 294944 | tf_op jit(solution)/shard_map/ppermute | solution.py:1058
  270.6 4.1 collective-permute-start.35
  275.3 5.6 %collective-permute-done.35.refs_1_ = f32[1,96,768]{2,1,0:T(8,128)S(1)} collective-permute-done((f32[1,96,768]{2,1,0:T(8,128)S(1)}, f32[1,96,768]{2,1,0:T(8,128)S(1)}, u32[]{:S(2)}, u32[]{:S(2)}) %collective-permute-start.35) | collective-permute-done | bytes 294944 | tf_op jit(solution)/shard_map/ppermute | solution.py:1058
  286.1 10.1 %collective-permute-done.36.refs_1_ = f32[1,96,768]{2,1,0:T(8,128)S(1)} collective-permute-done((f32[1,96,768]{2,1,0:T(8,128)S(1)}, f32[1,96,768]{2,1,0:T(8,128)S(1)}, u32[]{:S(2)}, u32[]{:S(2)}) %collective-permute-start.36) | collective-permute-done | bytes 294944 | tf_op jit(solution)/shard_map/ppermute | solution.py:1058
  300.1 3.9 collective-permute-done.41.refs_1_
  304.6 3.9 collective-permute-start.42
  330.3 3.9 collective-permute-done.46.refs_1_
  336.1 3.6 collective-permute-start.50
  340.9 3.6 collective-permute-done.51.refs_1_
  345.2 7.3 %collective-permute-done.50.refs_1_ = f32[1,96,768]{2,1,0:T(8,128)S(1)} collective-permute-done((f32[1,96,768]{2,1,0:T(8,128)S(1)}, f32[1,96,768]{2,1,0:T(8,128)S(1)}, u32[]{:S(2)}, u32[]{:S(2)}) %collective-permute-start.50) | collective-permute-done | bytes 294944 | tf_op jit(solution)/shard_map/ppermute | solution.py:1058
  355.9 5.0 %collective-permute-done.58.refs_1_ = f32[8,4224]{1,0:T(8,128)S(1)} collective-permute-done((f32[8,4224]{1,0:T(8,128)S(1)}, f32[8,4224]{1,0:T(8,128)S(1)}, u32[]{:S(2)}, u32[]{:S(2)}) %collective-permute-start.58) | collective-permute-done | bytes 135200 | tf_op jit(solution)/shard_map/ppermute | solution.py:1058
  376.9 6.1 %collective-permute-done.59.refs_1_ = f32[1,96,768]{2,1,0:T(8,128)S(1)} collective-permute-done((f32[1,96,768]{2,1,0:T(8,128)S(1)}, f32[1,96,768]{2,1,0:T(8,128)S(1)}, u32[]{:S(2)}, u32[]{:S(2)}) %collective-permute-start.59) | collective-permute-done | bytes 294944 | tf_op jit(solution)/shard_map/ppermute | solution.py:1058
  384.1 5.9 %collective-permute-done.67.refs_1_ = f32[8,4224]{1,0:T(8,128)S(1)} collective-permute-done((f32[8,4224]{1,0:T(8,128)S(1)}, f32[8,4224]{1,0:T(8,128)S(1)}, u32[]{:S(2)}, u32[]{:S(2)}) %collective-permute-start.67) | collective-permute-done | bytes 135200 | tf_op jit(solution)/shard_map/ppermute | solution.py:1058
  393.6 6.5 %collective-permute-done.65.refs_1_ = f32[1,96,768]{2,1,0:T(8,128)S(1)} collective-permute-done((f32[1,96,768]{2,1,0:T(8,128)S(1)}, f32[1,96,768]{2,1,0:T(8,128)S(1)}, u32[]{:S(2)}, u32[]{:S(2)}) %collective-permute-start.65) | collective-permute-done | bytes 294944 | tf_op jit(solution)/shard_map/ppermute | solution.py:1058
  416.0 5.5 %collective-permute-done.70.refs_1_ = f32[8,4224]{1,0:T(8,128)S(1)} collective-permute-done((f32[8,4224]{1,0:T(8,128)S(1)}, f32[8,4224]{1,0:T(8,128)S(1)}, u32[]{:S(2)}, u32[]{:S(2)}) %collective-permute-start.70) | collective-permute-done | bytes 135200 | tf_op jit(solution)/shard_map/ppermute | solution.py:1058
  (413 shorter events, 235.0 us)
Async XLA Ops:
  4.0 26.0 %collective-permute-start.2 = (f32[384,384]{1,0:T(8,128)}, f32[384,384]{1,0:T(8,128)}, u32[]{:S(2)}, u32[]{:S(2)}) collective-permute-start(f32[384,384]{1,0:T(8,128)} %get-tuple-element.319), channel_id=1, source_target_pairs={{0,1},{1,0},{2,3},{3,2},{4,5},{5,4},{6,7},{7,6},{8,9},{9,8},{10,11... | collective-permute-start | bytes 1769480 | tf_op jit(solution)/shard_map/ppermute | solution.py:1057
  38.6 29.5 %collective-permute-start.6 = (f32[768,384]{1,0:T(8,128)}, f32[768,384]{1,0:T(8,128)S(1)}, u32[]{:S(2)}, u32[]{:S(2)}) collective-permute-start(f32[768,384]{1,0:T(8,128)} %get-tuple-element.334), channel_id=1, source_target_pairs={{0,1},{1,0},{2,3},{3,2},{4,5},{5,4},{6,7},{7,6},{8,9},{9,8},{10,11... | collective-permute-start | bytes 3538952 | tf_op jit(solution)/shard_map/ppermute | solution.py:1057
  47.3 28.0 %collective-permute-start.8 = (f32[768,384]{1,0:T(8,128)}, f32[768,384]{1,0:T(8,128)}, u32[]{:S(2)}, u32[]{:S(2)}) collective-permute-start(f32[768,384]{1,0:T(8,128)} %get-tuple-element.338.refs_0_), channel_id=1, source_target_pairs={{0,8},{2,10},{4,12},{6,14},{8,0},{10,2},{12,4},{14,6},{16,24},{18,... | collective-permute-start | bytes 3538952 | tf_op jit(solution)/shard_map/ppermute | solution.py:1058
  68.7 29.2 %collective-permute-start.7 = (f32[768,384]{1,0:T(8,128)S(1)}, f32[768,384]{1,0:T(8,128)S(1)}, u32[]{:S(2)}, u32[]{:S(2)}) collective-permute-start(f32[768,384]{1,0:T(8,128)S(1)} %get-tuple-element.336.refs_0_), channel_id=1, source_target_pairs={{0,4},{2,6},{4,0},{6,2},{8,12},{10,14},{12,8},{14,10},{16,20},{18,... | collective-permute-start | bytes 3538952 | tf_op jit(solution)/shard_map/ppermute | solution.py:1058
  70.2 28.5 %collective-permute-start.5 = (f32[768,384]{1,0:T(8,128)S(1)}, f32[768,384]{1,0:T(8,128)S(1)}, u32[]{:S(2)}, u32[]{:S(2)}) collective-permute-start(f32[768,384]{1,0:T(8,128)S(1)} %get-tuple-element.333.refs_0_), channel_id=1, source_target_pairs={{0,8},{2,10},{4,12},{6,14},{8,0},{10,2},{12,4},{14,6},{16,24},{18,... | collective-permute-start | bytes 3538952 | tf_op jit(solution)/shard_map/ppermute | solution.py:1058
  77.8 19.6 %collective-permute-start.9 = (f32[384,384]{1,0:T(8,128)S(1)}, f32[384,384]{1,0:T(8,128)S(1)}, u32[]{:S(2)}, u32[]{:S(2)}) collective-permute-start(f32[384,384]{1,0:T(8,128)S(1)} %get-tuple-element.341), channel_id=1, source_target_pairs={{0,1},{1,0},{2,3},{3,2},{4,5},{5,4},{6,7},{7,6},{8,9},{9,8},{10,11... | collective-permute-start | bytes 1769480 | tf_op jit(solution)/shard_map/ppermute | solution.py:1057
  78.2 23.8 %collective-permute-start.14 = (f32[1536,384]{1,0:T(8,128)S(1)}, f32[1536,384]{1,0:T(8,128)S(1)}, u32[]{:S(2)}, u32[]{:S(2)}) collective-permute-start(f32[1536,384]{1,0:T(8,128)S(1)} %get-tuple-element.350.refs_1_), channel_id=1, source_target_pairs={{0,2},{2,0},{4,6},{6,4},{8,10},{10,8},{12,14},{14,12},{16,18},{18,... | collective-permute-start | bytes 7077896 | tf_op jit(solution)/shard_map/ppermute | solution.py:1058
  99.4 18.2 %collective-permute-start.11 = (f32[1536,384]{1,0:T(8,128)S(1)}, f32[1536,384]{1,0:T(8,128)S(1)}, u32[]{:S(2)}, u32[]{:S(2)}) collective-permute-start(f32[1536,384]{1,0:T(8,128)S(1)} %get-tuple-element.347.refs_4_), channel_id=1, source_target_pairs={{0,2},{2,0},{4,6},{6,4},{8,10},{10,8},{12,14},{14,12},{16,18},{18,... | collective-permute-start | bytes 7077896 | tf_op jit(solution)/shard_map/ppermute | solution.py:1058
  100.0 53.4 %collective-permute-start.18 = (f32[1536,384]{1,0:T(8,128)}, f32[1536,384]{1,0:T(8,128)S(1)}, u32[]{:S(2)}, u32[]{:S(2)}) collective-permute-start(f32[1536,384]{1,0:T(8,128)} %get-tuple-element.378), channel_id=1, source_target_pairs={{0,1},{1,0},{2,3},{3,2},{4,5},{5,4},{6,7},{7,6},{8,9},{9,8},{10,11... | collective-permute-start | bytes 7077896 | tf_op jit(solution)/shard_map/ppermute | solution.py:1057
  117.1 27.3 %collective-permute-start.16 = (f32[768,384]{1,0:T(8,128)S(1)}, f32[768,384]{1,0:T(8,128)S(1)}, u32[]{:S(2)}, u32[]{:S(2)}) collective-permute-start(f32[768,384]{1,0:T(8,128)S(1)} %get-tuple-element.365.refs_0_), channel_id=1, source_target_pairs={{0,8},{2,10},{4,12},{6,14},{8,0},{10,2},{12,4},{14,6},{16,24},{18,... | collective-permute-start | bytes 3538952 | tf_op jit(solution)/shard_map/ppermute | solution.py:1058
  118.8 26.7 %collective-permute-start.19 = (f32[768,384]{1,0:T(8,128)S(1)}, f32[768,384]{1,0:T(8,128)}, u32[]{:S(2)}, u32[]{:S(2)}) collective-permute-start(f32[768,384]{1,0:T(8,128)S(1)} %get-tuple-element.379.refs_0_), channel_id=1, source_target_pairs={{0,4},{2,6},{4,0},{6,2},{8,12},{10,14},{12,8},{14,10},{16,20},{18,... | collective-permute-start | bytes 3538952 | tf_op jit(solution)/shard_map/ppermute | solution.py:1058
  201.6 28.6 %collective-permute-start.27 = (f32[1,384,768]{2,1,0:T(8,128)}, f32[1,384,768]{2,1,0:T(8,128)}, u32[]{:S(2)}, u32[]{:S(2)}) collective-permute-start(f32[1,384,768]{2,1,0:T(8,128)} %get-tuple-element.451), channel_id=1, source_target_pairs={{0,1},{1,0},{2,3},{3,2},{4,5},{5,4},{6,7},{7,6},{8,9},{9,8},{10,11... | collective-permute-start | bytes 3538952 | tf_op jit(solution)/shard_map/ppermute | solution.py:1057
  203.1 28.6 %collective-permute-start.26 = (f32[2,192,768]{2,1,0:T(8,128)}, f32[2,192,768]{2,1,0:T(8,128)S(1)}, u32[]{:S(2)}, u32[]{:S(2)}) collective-permute-start(f32[2,192,768]{2,1,0:T(8,128)} %get-tuple-element.449), channel_id=1, source_target_pairs={{0,8},{2,10},{4,12},{6,14},{8,0},{10,2},{12,4},{14,6},{16,24},{18,... | collective-permute-start | bytes 3538952 | tf_op jit(solution)/shard_map/ppermute | solution.py:1058
  238.0 44.6 %collective-permute-start.38 = (f32[2,192,768]{2,1,0:T(8,128)S(1)}, f32[2,192,768]{2,1,0:T(8,128)S(1)}, u32[]{:S(2)}, u32[]{:S(2)}) collective-permute-start(f32[2,192,768]{2,1,0:T(8,128)S(1)} %get-tuple-element.487), channel_id=1, source_target_pairs={{0,8},{2,10},{4,12},{6,14},{8,0},{10,2},{12,4},{14,6},{16,24},{18,... | collective-permute-start | bytes 3538952 | tf_op jit(solution)/shard_map/ppermute | solution.py:1058
  247.2 36.2 %collective-permute-start.37 = (f32[2,192,768]{2,1,0:T(8,128)S(1)}, f32[2,192,768]{2,1,0:T(8,128)S(1)}, u32[]{:S(2)}, u32[]{:S(2)}) collective-permute-start(f32[2,192,768]{2,1,0:T(8,128)S(1)} %get-tuple-element.485), channel_id=1, source_target_pairs={{0,4},{2,6},{4,0},{6,2},{8,12},{10,14},{12,8},{14,10},{16,20},{18,... | collective-permute-start | bytes 3538952 | tf_op jit(solution)/shard_map/ppermute | solution.py:1058
  252.2 18.4 %collective-permute-start.33 = (f32[1,96,768]{2,1,0:T(8,128)S(1)}, f32[1,96,768]{2,1,0:T(8,128)S(1)}, u32[]{:S(2)}, u32[]{:S(2)}) collective-permute-start(f32[1,96,768]{2,1,0:T(8,128)S(1)} %get-tuple-element.477), channel_id=1, source_target_pairs={{0,16},{2,18},{4,20},{6,22},{8,24},{10,26},{12,28},{14,30},{16,0},... | collective-permute-start | bytes 884744 | tf_op jit(solution)/shard_map/ppermute | solution.py:1058
  254.9 44.0 %collective-permute-start.28 = (f32[1,384,768]{2,1,0:T(8,128)S(1)}, f32[1,384,768]{2,1,0:T(8,128)S(1)}, u32[]{:S(2)}, u32[]{:S(2)}) collective-permute-start(f32[1,384,768]{2,1,0:T(8,128)S(1)} %get-tuple-element.458), channel_id=1, source_target_pairs={{0,1},{1,0},{2,3},{3,2},{4,5},{5,4},{6,7},{7,6},{8,9},{9,8},{10,11... | collective-permute-start | bytes 3538952 | tf_op jit(solution)/shard_map/ppermute | solution.py:1057
  256.3 52.7 %collective-permute-start.45 = (f32[1,384,768]{2,1,0:T(8,128)S(1)}, f32[1,384,768]{2,1,0:T(8,128)S(1)}, u32[]{:S(2)}, u32[]{:S(2)}) collective-permute-start(f32[1,384,768]{2,1,0:T(8,128)S(1)} %get-tuple-element.507), channel_id=1, source_target_pairs={{0,1},{1,0},{2,3},{3,2},{4,5},{5,4},{6,7},{7,6},{8,9},{9,8},{10,11... | collective-permute-start | bytes 3538952 | tf_op jit(solution)/shard_map/ppermute | solution.py:1057
  284.0 20.0 %collective-permute-start.41 = (f32[2,96,768]{2,1,0:T(8,128)S(1)}, f32[2,96,768]{2,1,0:T(8,128)S(1)}, u32[]{:S(2)}, u32[]{:S(2)}) collective-permute-start(f32[2,96,768]{2,1,0:T(8,128)S(1)} %get-tuple-element.498), channel_id=1, source_target_pairs={{0,8},{2,10},{4,12},{6,14},{8,0},{10,2},{12,4},{14,6},{16,24},{18,... | collective-permute-start | bytes 1769480 | tf_op jit(solution)/shard_map/ppermute | solution.py:1058
  296.2 18.0 %collective-permute-start.43 = (f32[2,96,768]{2,1,0:T(8,128)S(1)}, f32[2,96,768]{2,1,0:T(8,128)S(1)}, u32[]{:S(2)}, u32[]{:S(2)}) collective-permute-start(f32[2,96,768]{2,1,0:T(8,128)S(1)} %get-tuple-element.503), channel_id=1, source_target_pairs={{0,4},{2,6},{4,0},{6,2},{8,12},{10,14},{12,8},{14,10},{16,20},{18,... | collective-permute-start | bytes 1769480 | tf_op jit(solution)/shard_map/ppermute | solution.py:1058
  315.6 19.2 %collective-permute-start.40 = (f32[1,192,768]{2,1,0:T(8,128)S(1)}, f32[1,192,768]{2,1,0:T(8,128)S(1)}, u32[]{:S(2)}, u32[]{:S(2)}) collective-permute-start(f32[1,192,768]{2,1,0:T(8,128)S(1)} %get-tuple-element.496), channel_id=1, source_target_pairs={{0,4},{2,6},{4,0},{6,2},{8,12},{10,14},{12,8},{14,10},{16,20},{18,... | collective-permute-start | bytes 1769480 | tf_op jit(solution)/shard_map/ppermute | solution.py:1058
  316.6 23.1 %collective-permute-start.52 = (f32[1,192,768]{2,1,0:T(8,128)S(1)}, f32[1,192,768]{2,1,0:T(8,128)S(1)}, u32[]{:S(2)}, u32[]{:S(2)}) collective-permute-start(f32[1,192,768]{2,1,0:T(8,128)S(1)} %get-tuple-element.534.refs_0_), channel_id=1, source_target_pairs={{0,8},{2,10},{4,12},{6,14},{8,0},{10,2},{12,4},{14,6},{16,24},{18,... | collective-permute-start | bytes 1769480 | tf_op jit(solution)/shard_map/ppermute | solution.py:1058
  324.8 65.8 %collective-permute-start.66 = (f32[512,768]{1,0:T(8,128)S(1)}, f32[512,768]{1,0:T(8,128)S(1)}, u32[]{:S(2)}, u32[]{:S(2)}) collective-permute-start(f32[512,768]{1,0:T(8,128)S(1)} %get-tuple-element.562), channel_id=1, source_target_pairs={{0,1},{1,0},{2,3},{3,2},{4,5},{5,4},{6,7},{7,6},{8,9},{9,8},{10,11... | collective-permute-start | bytes 4718600 | tf_op jit(solution)/shard_map/ppermute | solution.py:1057
  327.7 16.8 %collective-permute-start.51 = (f32[1,192,768]{2,1,0:T(8,128)S(1)}, f32[1,192,768]{2,1,0:T(8,128)S(1)}, u32[]{:S(2)}, u32[]{:S(2)}) collective-permute-start(f32[1,192,768]{2,1,0:T(8,128)S(1)} %get-tuple-element.533), channel_id=1, source_target_pairs={{0,4},{2,6},{4,0},{6,2},{8,12},{10,14},{12,8},{14,10},{16,20},{18,... | collective-permute-start | bytes 1769480 | tf_op jit(solution)/shard_map/ppermute | solution.py:1058
  334.8 27.6 %collective-permute-start.56 = (f32[1,192,768]{2,1,0:T(8,128)S(1)}, f32[1,192,768]{2,1,0:T(8,128)S(1)}, u32[]{:S(2)}, u32[]{:S(2)}) collective-permute-start(f32[1,192,768]{2,1,0:T(8,128)S(1)} %get-tuple-element.543.refs_0_), channel_id=1, source_target_pairs={{0,4},{2,6},{4,0},{6,2},{8,12},{10,14},{12,8},{14,10},{16,20},{18,... | collective-permute-start | bytes 1769480 | tf_op jit(solution)/shard_map/ppermute | solution.py:1058
  345.1 19.9 %collective-permute-start.55 = (f32[1,96,768]{2,1,0:T(8,128)S(1)}, f32[1,96,768]{2,1,0:T(8,128)S(1)}, u32[]{:S(2)}, u32[]{:S(2)}) collective-permute-start(f32[1,96,768]{2,1,0:T(8,128)S(1)} %get-tuple-element.542), channel_id=1, source_target_pairs={{0,8},{2,10},{4,12},{6,14},{8,0},{10,2},{12,4},{14,6},{16,24},{18,... | collective-permute-start | bytes 884744 | tf_op jit(solution)/shard_map/ppermute | solution.py:1058
  369.4 35.7 %collective-permute-start.39 = (f32[512,768]{1,0:T(8,128)S(1)}, f32[512,768]{1,0:T(8,128)S(1)}, u32[]{:S(2)}, u32[]{:S(2)}) collective-permute-start(f32[512,768]{1,0:T(8,128)S(1)} %get-tuple-element.494), channel_id=1, source_target_pairs={{0,1},{1,0},{2,3},{3,2},{4,5},{5,4},{6,7},{7,6},{8,9},{9,8},{10,11... | collective-permute-start | bytes 4718600 | tf_op jit(solution)/shard_map/ppermute | solution.py:1057
  372.8 17.3 %collective-permute-start.64 = (f32[1,96,768]{2,1,0:T(8,128)S(1)}, f32[1,96,768]{2,1,0:T(8,128)S(1)}, u32[]{:S(2)}, u32[]{:S(2)}) collective-permute-start(f32[1,96,768]{2,1,0:T(8,128)S(1)} %get-tuple-element.559.refs_0_), channel_id=1, source_target_pairs={{0,16},{2,18},{4,20},{6,22},{8,24},{10,26},{12,28},{14,30},{16,0},... | collective-permute-start | bytes 884744 | tf_op jit(solution)/shard_map/ppermute | solution.py:1058
  375.3 25.4 %collective-permute-start.63 = (f32[1,192,768]{2,1,0:T(8,128)S(1)}, f32[1,192,768]{2,1,0:T(8,128)S(1)}, u32[]{:S(2)}, u32[]{:S(2)}) collective-permute-start(f32[1,192,768]{2,1,0:T(8,128)S(1)} %get-tuple-element.558.refs_0_), channel_id=1, source_target_pairs={{0,4},{2,6},{4,0},{6,2},{8,12},{10,14},{12,8},{14,10},{16,20},{18,... | collective-permute-start | bytes 1769480 | tf_op jit(solution)/shard_map/ppermute | solution.py:1058
  405.0 17.2 %collective-permute-start.69 = (f32[1,384,768]{2,1,0:T(8,128)S(1)}, f32[1,384,768]{2,1,0:T(8,128)S(1)}, u32[]{:S(2)}, u32[]{:S(2)}) collective-permute-start(f32[1,384,768]{2,1,0:T(8,128)S(1)} %get-tuple-element.575.refs_0_), channel_id=1, source_target_pairs={{0,2},{2,0},{4,6},{6,4},{8,10},{10,8},{12,14},{14,12},{16,18},{18,... | collective-permute-start | bytes 3538952 | tf_op jit(solution)/shard_map/ppermute | solution.py:1058
  405.1 19.1 %collective-permute-start.68 = (f32[1,192,768]{2,1,0:T(8,128)S(1)}, f32[1,192,768]{2,1,0:T(8,128)S(1)}, u32[]{:S(2)}, u32[]{:S(2)}) collective-permute-start(f32[1,192,768]{2,1,0:T(8,128)S(1)} %get-tuple-element.574.refs_0_), channel_id=1, source_target_pairs={{0,4},{2,6},{4,0},{6,2},{8,12},{10,14},{12,8},{14,10},{16,20},{18,... | collective-permute-start | bytes 1769480 | tf_op jit(solution)/shard_map/ppermute | solution.py:1058
  405.4 20.3 %collective-permute-start.75 = (f32[1,192,768]{2,1,0:T(8,128)S(1)}, f32[1,192,768]{2,1,0:T(8,128)S(1)}, u32[]{:S(2)}, u32[]{:S(2)}) collective-permute-start(f32[1,192,768]{2,1,0:T(8,128)S(1)} %get-tuple-element.589.refs_0_), channel_id=1, source_target_pairs={{0,8},{2,10},{4,12},{6,14},{8,0},{10,2},{12,4},{14,6},{16,24},{18,... | collective-permute-start | bytes 1769480 | tf_op jit(solution)/shard_map/ppermute | solution.py:1058
  (123 other events, 907.6 us)

commit v3 on v2

--- a/solution.py
+++ b/solution.py
@@ -41,6 +41,10 @@
 
 def vmem(dims, dtype=f32):
     return pltpu.VMEM(dims, dtype)
+
+
+def hbm(dims, dtype=f32):
+    return pltpu.HBM(dims, dtype)
 
 
 TOKEN = (8, 128)
@@ -161,7 +165,7 @@
         bits,
         [weight],
         [spec],
-        shape(weight.shape, bf16),
+        hbm(weight.shape, bf16),
         spec,
         (steps,),
         dep,
@@ -184,14 +188,17 @@
                 at += rows
 
     total = sum(w.size for w in weights) // parts // STRIP
-    return whole_call(
+    specs = [fixed(w.shape) for w in weights]
+    return call(
         kernel,
         "binarize_pack",
         bits,
-        weights,
-        [shape(w.shape, bf16) for w in weights] + [vmem((total, STRIP))],
-        dep,
-        hold=False,
+        [in_hbm(w) for w in weights],
+        specs,
+        [hbm(w.shape, bf16) for w in weights] + [vmem((total, STRIP))],
+        specs + [IN_VMEM],
+        (1,),
+        dep,
     )
 
 
@@ -432,7 +439,8 @@
     outs = [shape((rows, kept * width), bf16), shape((rows, dim), bf16), shape((rows, dim))]
     out_specs = [block(kept * width), block(dim), block(dim)]
     if student:
-        outs += [shape((rows, width), bf16), shape((rows, dim)), *weights]
+        outs += [shape((rows, width), bf16), hbm((rows, dim))]
+        outs += [hbm(w.shape, bf16) for w in weights]
         out_specs += [block(width), block(dim)] + [fixed(w.shape) for w in weights]
     return call(
         kernel,
@@ -483,7 +491,7 @@
         bits,
         [low, weight, biases],
         [fixed(low.shape), pl.BlockSpec((dim, STRIP), lambda j, b: (0, j)), fixed(biases.shape)],
-        [shape((tokens, hidden), bf16)] * count,
+        [shape((tokens, hidden), bf16), hbm((tokens, hidden), bf16)][:count],
         [pl.BlockSpec((tokens, STRIP), lambda j, b: (0, j))] * count,
         (hidden // STRIP,),
         dep,
@@ -512,7 +520,7 @@
     outs = [shape((tokens, steps * STRIP), bf16)]
     out_specs = [pl.BlockSpec((tokens, STRIP), column)]
     if student:
-        outs += [outs[0], shape((dim, steps * STRIP), bf16)]
+        outs += [hbm((tokens, steps * STRIP), bf16), hbm((dim, steps * STRIP), bf16)]
         out_specs += [out_specs[0], pl.BlockSpec((dim, STRIP), column)]
     return call(
         kernel,
@@ -617,8 +625,8 @@
             shape((tokens, dim)),
             shape((tokens, dim), bf16),
             shape((8, dim)),
-            shape((hidden, dim), bf16),
-            pltpu.HBM((2, tokens, dim), bf16),
+            hbm((hidden, dim), bf16),
+            hbm((2, tokens, dim), bf16),
         ],
         [
             block(dim),
@@ -1146,7 +1154,7 @@
         makers = {
             1: lambda: pack([t_q, t_k, t_v, t_o], names, bits, last),
             2: lambda: touch(v.b_pack, bits, last),
-            3: lambda: pack_tile(t_e, (C,), names[1:], bits, last),
+            3: lambda: pack_tile(in_hbm(t_e), (C,), names[1:], bits, last),
             4: lambda: pack_tile(v.b_e, (C,), names[1:], bits, last),
             5: lambda: pack_tile(v.b_r, names[1:], (C,), bits, last),
         }

time: 442 us -> 435 us (0.984)
  local copies, waits for them, and re-layouts: 30.5 us -> 17.9 us
    unnamed x157 -> x117, local copies, waits for them, and re-layouts: 28.8 us -> 16.3 us
  transfers between devices with their start and end apart: 77 -> 77, of which waited for: 33 -> 34; matrix products, arithmetic and copies ran while one was open for 0% -> 1% of each run, Pallas kernels for 37% -> 39%
where the time goes in v3:
time: 435 us; the launch traced here: 432 us
  Pallas kernels  193 us (44%)
  waiting for transfers between devices  150 us (34%)
  starting transfers between devices  68.2 us (16%)
  local copies, waits for them, and re-layouts  17.9 us (4%)
    pallas_call x95, Pallas kernels, invoke(): pl.pallas_call(body, out_shape=outs + [pltpu.HBM(TOKEN, f32)], input_outp...  180 us
    ppermute x61, waiting for transfers between devices, swap(): lax.ppermute(array, 'wide', [(i, i ^ 1 << bit) for i in range(n_wide)])  102 us
    ppermute x61, starting transfers between devices, swap(): lax.ppermute(array, 'wide', [(i, i ^ 1 << bit) for i in range(n_wide)])  49.6 us
    ppermute x16, waiting for transfers between devices, swap(): return lax.ppermute(array, 'narrow', [(0, 1), (1, 0)])  47.7 us
    ppermute x16, starting transfers between devices, swap(): return lax.ppermute(array, 'narrow', [(0, 1), (1, 0)])  18.6 us
    unnamed x117, local copies, waits for them, and re-layouts  16.3 us
    pallas_call x23, Pallas kernels, touch(): pl.pallas_call(body, in_specs=[pl.BlockSpec(memory_space=pltpu.SMEM)] + [...  12.4 us
  transfers between devices with their start and end apart: 77, of which 34 were waited for; matrix products, arithmetic and copies ran while one was open for 1% of the time, Pallas kernels for 39%

profile of v3, /device:TPU:0, one launch (start us, length us, event | category | flops | bytes accessed | tf_op | source)
XLA Modules:
  0.0 432.0 jit_solution(4822839685646626327)
XLA Ops:
  6.1 4.8 %binarize_pack.1 = (bf16[768,384]{1,0:T(8,128)(2,1)}, bf16[768,384]{1,0:T(8,128)(2,1)}, bf16[768,384]{1,0:T(8,128)(2,1)}, bf16[384,768]{1,0:T(8,128)(2,1)}, f32[384,384]{1,0:T(8,128)S(1)}, /*index=5*/f32[8,128]{1,0:T(8,128)}) custom-call(s32[5]{0:T(128)S(1)} %stack.27.bits_ref, bf16[768,384]{1,0:T(8,128)(2,1)} %refs_0_.7, bf16[768,384]{1,0:T(8,128)(2,1)} %refs_1_.3, ...), custom_call_target="tpu_custom_call" | custom-call | tf_op jit(solution)/shard_map/binarize_pack/pallas_call | solution.py:76
  10.9 8.3 %collective-permute-done.refs_0_ = f32[14,384]{1,0:T(8,128)S(1)} collective-permute-done((f32[14,384]{1,0:T(8,128)S(1)}, f32[14,384]{1,0:T(8,128)S(1)}, u32[]{:S(2)}, u32[]{:S(2)}) %collective-permute-start) | collective-permute-done | bytes 21536 | tf_op jit(solution)/shard_map/ppermute | solution.py:1065
  19.8 3.7 binarize.2
  39.1 4.6 %collective-permute-done.1.refs_0_ = f32[384,384]{1,0:T(8,128)} collective-permute-done((f32[384,384]{1,0:T(8,128)S(1)}, f32[384,384]{1,0:T(8,128)}, u32[]{:S(2)}, u32[]{:S(2)}) %collective-permute-start.1) | collective-permute-done | bytes 589856 | tf_op jit(solution)/shard_map/ppermute | solution.py:1065
  52.2 9.6 %attend_own.1 = (bf16[512,1920]{1,0:T(8,128)(2,1)S(1)}, bf16[512,384]{1,0:T(8,128)(2,1)S(1)}, bf16[512,384]{1,0:T(8,128)(2,1)S(1)}, f32[8,128]{1,0:T(8,128)}) custom-call(s32[5]{0:T(128)S(1)} %stack.27.bits_ref, bf16[512,768]{1,0:T(8,128)(2,1)S(1)} %dynamic-slice_bitcast_fusion.refs_0_.refs_2_, f32[14,384]{1,0:T(8,128)S(1)} %pad_maximum_fusion.refs_1_.refs_2_, ...), custom_call_target="tpu_custom_call" | custom-call | tf_op jit(solution)/shard_map/attend_own/pallas_call | solution.py:76
  77.3 9.8 %collective-permute-done.10.refs_0_ = f32[384,384]{1,0:T(8,128)S(1)} collective-permute-done((f32[384,384]{1,0:T(8,128)S(1)}, f32[384,384]{1,0:T(8,128)S(1)}, u32[]{:S(2)}, u32[]{:S(2)}) %collective-permute-start.10) | collective-permute-done | bytes 589856 | tf_op jit(solution)/shard_map/ppermute | solution.py:1065
  87.6 8.8 %collective-permute-done.9.refs_0_ = f32[384,384]{1,0:T(8,128)S(1)} collective-permute-done((f32[384,384]{1,0:T(8,128)S(1)}, f32[384,384]{1,0:T(8,128)S(1)}, u32[]{:S(2)}, u32[]{:S(2)}) %collective-permute-start.9) | collective-permute-done | bytes 589856 | tf_op jit(solution)/shard_map/ppermute | solution.py:1065
  103.5 6.6 %attend_other.2 = (bf16[512,768]{1,0:T(8,128)(2,1)S(1)}, bf16[512,768]{1,0:T(8,128)(2,1)S(1)}, f32[512,768]{1,0:T(8,128)S(1)}, f32[8,128]{1,0:T(8,128)}) custom-call(s32[5]{0:T(128)S(1)} %stack.27.bits_ref, bf16[512,768]{1,0:T(8,128)(2,1)S(1)} %dynamic-slice_bitcast_fusion.refs_0_.refs_2_, f32[14,384]{1,0:T(8,128)S(1)} %get-tuple-element.312.refs_1_.refs_3_, ...), custom_call_target="tpu_custom_call" | custom-call | tf_op jit(solution)/shard_map/attend_other/pallas_call | solution.py:76
  110.1 5.5 %collective-permute-done.12.refs_1_ = f32[384,384]{1,0:T(8,128)S(1)} collective-permute-done((f32[384,384]{1,0:T(8,128)S(1)}, f32[384,384]{1,0:T(8,128)S(1)}, u32[]{:S(2)}, u32[]{:S(2)}) %collective-permute-start.12) | collective-permute-done | bytes 589856 | tf_op jit(solution)/shard_map/ppermute | solution.py:1066
  119.2 8.2 %attend_other.3 = (bf16[512,1152]{1,0:T(8,128)(2,1)S(1)}, bf16[512,768]{1,0:T(8,128)(2,1)S(1)}, f32[512,768]{1,0:T(8,128)S(1)}, bf16[512,384]{1,0:T(8,128)(2,1)S...) custom-call(s32[5]{0:T(128)S(1)} %stack.27.bits_ref, ...), custom_call_target="tpu_custom_call" | custom-call | tf_op jit(solution)/shard_map/attend_other/pallas_call | solution.py:76
  130.9 3.5 up_other.2
  134.5 5.1 %up_own.3 = (bf16[512,1536]{1,0:T(8,128)(2,1)S(1)}, bf16[512,1536]{1,0:T(8,128)(2,1)}, f32[8,128]{1,0:T(8,128)}) custom-call(s32[5]{0:T(128)S(1)} %stack.27.bits_ref, bf16[512,768]{1,0:T(8,128)(2,1)S(1)} %get-tuple-element.364.refs_0_.refs_2_, bf16[768,1536]{1,0:T(8,128)(2,1)S(1)} %copy-done.2, f32[14,384]{1,0:T(8,128)S(1)} %pad_maximum_fusion.refs_1_.refs_2_, ...), custom_call_target="tpu_custom_call" | custom-call | tf_op jit(solution)/shard_map/up_own/pallas_call | solution.py:76
  145.3 7.2 %collective-permute-done.18.refs_0_ = f32[1536,384]{1,0:T(8,128)S(1)} collective-permute-done((f32[1536,384]{1,0:T(8,128)}, f32[1536,384]{1,0:T(8,128)S(1)}, u32[]{:S(2)}, u32[]{:S(2)}) %collective-permute-start.18) | collective-permute-done | bytes 2359328 | tf_op jit(solution)/shard_map/ppermute | solution.py:1065
  153.6 5.3 %up_other.3 = (bf16[512,1536]{1,0:T(8,128)(2,1)S(1)}, bf16[512,1536]{1,0:T(8,128)(2,1)}, bf16[768,1536]{1,0:T(8,128)(2,1)}, f32[8,128]{1,0:T(8,128)}) custom-call(s32[5]{0:T(128)S(1)} %stack.27.bits_ref, bf16[512,768]{1,0:T(8,128)(2,1)S(1)} %get-tuple-element.364.refs_0_.refs_2_, f32[1536,384]{1,0:T(8,128)S(1)} %get-tuple-element.377.refs_1_, ...), custom_call_target="tpu_custom_call" | custom-call | tf_op jit(solution)/shard_map/up_other/pallas_call | solution.py:76
  161.3 6.3 %down_other.1 = (f32[512,768]{1,0:T(8,128)S(1)}, f32[512,768]{1,0:T(8,128)S(1)}, bf16[512,768]{1,0:T(8,128)(2,1)S(1)}, f32[8,768]{1,0:T(8,128)S(1)}, bf16[1536,7...) custom-call(s32[5]{0:T(128)S(1)} %stack.27.bits_ref, ...), custom_call_target="tpu_custom_call" | custom-call | tf_op jit(solution)/shard_map/down_other/pallas_call | solution.py:76
  170.4 5.2 %up_back.1 = (bf16[512,1536]{1,0:T(8,128)(2,1)S(1)}, bf16[512,1536]{1,0:T(8,128)(2,1)S(1)}, f32[8,1536]{1,0:T(8,128)S(1)}, f32[8,128]{1,0:T(8,128)}) custom-call(s32[5]{0:T(128)S(1)} %stack.27.bits_ref, bf16[512,768]{1,0:T(8,128)(2,1)S(1)} %get-tuple-element.397.refs_0_.refs_1_.refs_3_, bf16[1536,768]{1,0:T(8,128)(2,1)S(1)} %copy-done.4, ...), custom_call_target="tpu_custom_call" | custom-call | tf_op jit(solution)/shard_map/up_back/pallas_call | solution.py:76
  199.0 6.4 %first_back.1 = (f32[512,768]{1,0:T(8,128)S(1)}, bf16[512,768]{1,0:T(8,128)(2,1)S(1)}, bf16[512,384]{1,0:T(8,128)(2,1)S(1)}, bf16[512,384]{1,0:T(8,128)(2,1)S(1)...) custom-call(s32[5]{0:T(128)S(1)} %stack.27.bits_ref, bf16[512,1536]{1,0:T(8,128)(2,1)S(1)} %get-tuple-element.402.refs_1_.refs_0_, ...), custom_call_target="tpu_custom_call" | custom-call | tf_op jit(solution)/shard_map/first_back/pallas_call | solution.py:76
  205.5 11.9 %attend_back.1 = (bf16[512,768]{1,0:T(8,128)(2,1)S(1)}, bf16[512,768]{1,0:T(8,128)(2,1)S(1)}, bf16[512,384]{1,0:T(8,128)(2,1)S(1)}, bf16[512,384]{1,0:T(8,128)(2...) custom-call(s32[5]{0:T(128)S(1)} %stack.27.bits_ref, bf16[512,1920]{1,0:T(8,128)(2,1)S(1)} %copy-done.29, ...), custom_call_target="tpu_custom_call" | custom-call | tf_op jit(solution)/shard_map/attend_back/pallas_call | solution.py:76
  217.4 3.6 outer.10
  235.9 4.7 %token_grad.1 = (f32[512,768]{1,0:T(8,128)S(1)}, f32[2,512,768]{2,1,0:T(8,128)}, f32[8,128]{1,0:T(8,128)}) custom-call(s32[5]{0:T(128)S(1)} %stack.27.bits_ref, f32[512,768]{1,0:T(8,128)S(1)} %get-tuple-element.467.refs_0_, bf16[512,768]{1,0:T(8,128)(2,1)S(1)} %get-tuple-element.444.refs_1_.refs_3_, bf16[768,384]{1,0:T(8,128)(2,1)S(1)} %copy-done.11, ...), custom_call_target="tpu_custom_call" | custom-call | tf_op jit(solution)/shard_map/token_grad/pallas_call | solution.py:76
  251.9 13.2 %collective-permute-done.33.refs_1_ = f32[1,96,768]{2,1,0:T(8,128)S(1)} collective-permute-done((f32[1,96,768]{2,1,0:T(8,128)S(1)}, f32[1,96,768]{2,1,0:T(8,128)S(1)}, u32[]{:S(2)}, u32[]{:S(2)}) %collective-permute-start.33) | collective-permute-done | bytes 294944 | tf_op jit(solution)/shard_map/ppermute | solution.py:1066
  265.1 4.7 %collective-permute-start.35 = (f32[1,96,768]{2,1,0:T(8,128)S(1)}, f32[1,96,768]{2,1,0:T(8,128)S(1)}, u32[]{:S(2)}, u32[]{:S(2)}) collective-permute-start(f32[1,96,768]{2,1,0:T(8,128)S(1)} %get-tuple-element.481), channel_id=1, source_target_pairs={{0,8},{2,10},{4,12},{6,14},{8,0},{10,2},{12,4},{14,6},{16,24},{18,... | collective-permute-start | bytes 884744 | tf_op jit(solution)/shard_map/ppermute | solution.py:1066
  270.3 5.1 %collective-permute-done.35.refs_1_ = f32[1,96,768]{2,1,0:T(8,128)S(1)} collective-permute-done((f32[1,96,768]{2,1,0:T(8,128)S(1)}, f32[1,96,768]{2,1,0:T(8,128)S(1)}, u32[]{:S(2)}, u32[]{:S(2)}) %collective-permute-start.35) | collective-permute-done | bytes 294944 | tf_op jit(solution)/shard_map/ppermute | solution.py:1066
  279.7 10.3 %collective-permute-done.36.refs_1_ = f32[1,96,768]{2,1,0:T(8,128)S(1)} collective-permute-done((f32[1,96,768]{2,1,0:T(8,128)S(1)}, f32[1,96,768]{2,1,0:T(8,128)S(1)}, u32[]{:S(2)}, u32[]{:S(2)}) %collective-permute-start.36) | collective-permute-done | bytes 294944 | tf_op jit(solution)/shard_map/ppermute | solution.py:1066
  293.1 7.5 %collective-permute-done.41.refs_1_ = f32[2,96,768]{2,1,0:T(8,128)S(1)} collective-permute-done((f32[2,96,768]{2,1,0:T(8,128)S(1)}, f32[2,96,768]{2,1,0:T(8,128)S(1)}, u32[]{:S(2)}, u32[]{:S(2)}) %collective-permute-start.41) | collective-permute-done | bytes 589856 | tf_op jit(solution)/shard_map/ppermute | solution.py:1066
  323.7 3.7 collective-permute-done.46.refs_1_
  338.4 7.8 %collective-permute-done.50.refs_1_ = f32[1,96,768]{2,1,0:T(8,128)S(1)} collective-permute-done((f32[1,96,768]{2,1,0:T(8,128)S(1)}, f32[1,96,768]{2,1,0:T(8,128)S(1)}, u32[]{:S(2)}, u32[]{:S(2)}) %collective-permute-start.50) | collective-permute-done | bytes 294944 | tf_op jit(solution)/shard_map/ppermute | solution.py:1066
  350.1 4.2 collective-permute-done.58.refs_1_
  370.0 6.7 %collective-permute-done.59.refs_1_ = f32[1,96,768]{2,1,0:T(8,128)S(1)} collective-permute-done((f32[1,96,768]{2,1,0:T(8,128)S(1)}, f32[1,96,768]{2,1,0:T(8,128)S(1)}, u32[]{:S(2)}, u32[]{:S(2)}) %collective-permute-start.59) | collective-permute-done | bytes 294944 | tf_op jit(solution)/shard_map/ppermute | solution.py:1066
  377.8 5.3 %collective-permute-done.67.refs_1_ = f32[8,4224]{1,0:T(8,128)S(1)} collective-permute-done((f32[8,4224]{1,0:T(8,128)S(1)}, f32[8,4224]{1,0:T(8,128)S(1)}, u32[]{:S(2)}, u32[]{:S(2)}) %collective-permute-start.67) | collective-permute-done | bytes 135200 | tf_op jit(solution)/shard_map/ppermute | solution.py:1066
  387.5 6.5 %collective-permute-done.65.refs_1_ = f32[1,96,768]{2,1,0:T(8,128)S(1)} collective-permute-done((f32[1,96,768]{2,1,0:T(8,128)S(1)}, f32[1,96,768]{2,1,0:T(8,128)S(1)}, u32[]{:S(2)}, u32[]{:S(2)}) %collective-permute-start.65) | collective-permute-done | bytes 294944 | tf_op jit(solution)/shard_map/ppermute | solution.py:1066
  409.0 6.2 %collective-permute-done.70.refs_1_ = f32[8,4224]{1,0:T(8,128)S(1)} collective-permute-done((f32[8,4224]{1,0:T(8,128)S(1)}, f32[8,4224]{1,0:T(8,128)S(1)}, u32[]{:S(2)}, u32[]{:S(2)}) %collective-permute-start.70) | collective-permute-done | bytes 135200 | tf_op jit(solution)/shard_map/ppermute | solution.py:1066
  (373 shorter events, 219.4 us)
Async XLA Ops:
  2.3 26.7 %collective-permute-start.2 = (f32[384,384]{1,0:T(8,128)S(1)}, f32[384,384]{1,0:T(8,128)}, u32[]{:S(2)}, u32[]{:S(2)}) collective-permute-start(f32[384,384]{1,0:T(8,128)S(1)} %get-tuple-element.319), channel_id=1, source_target_pairs={{0,1},{1,0},{2,3},{3,2},{4,5},{5,4},{6,7},{7,6},{8,9},{9,8},{10,11... | collective-permute-start | bytes 1769480 | tf_op jit(solution)/shard_map/ppermute | solution.py:1065
  38.5 28.6 %collective-permute-start.6 = (f32[768,384]{1,0:T(8,128)}, f32[768,384]{1,0:T(8,128)S(1)}, u32[]{:S(2)}, u32[]{:S(2)}) collective-permute-start(f32[768,384]{1,0:T(8,128)} %get-tuple-element.334), channel_id=1, source_target_pairs={{0,1},{1,0},{2,3},{3,2},{4,5},{5,4},{6,7},{7,6},{8,9},{9,8},{10,11... | collective-permute-start | bytes 3538952 | tf_op jit(solution)/shard_map/ppermute | solution.py:1065
  46.4 28.0 %collective-permute-start.8 = (f32[768,384]{1,0:T(8,128)}, f32[768,384]{1,0:T(8,128)}, u32[]{:S(2)}, u32[]{:S(2)}) collective-permute-start(f32[768,384]{1,0:T(8,128)} %get-tuple-element.338.refs_0_), channel_id=1, source_target_pairs={{0,8},{2,10},{4,12},{6,14},{8,0},{10,2},{12,4},{14,6},{16,24},{18,... | collective-permute-start | bytes 3538952 | tf_op jit(solution)/shard_map/ppermute | solution.py:1066
  67.7 29.2 %collective-permute-start.7 = (f32[768,384]{1,0:T(8,128)S(1)}, f32[768,384]{1,0:T(8,128)S(1)}, u32[]{:S(2)}, u32[]{:S(2)}) collective-permute-start(f32[768,384]{1,0:T(8,128)S(1)} %get-tuple-element.336.refs_0_), channel_id=1, source_target_pairs={{0,4},{2,6},{4,0},{6,2},{8,12},{10,14},{12,8},{14,10},{16,20},{18,... | collective-permute-start | bytes 3538952 | tf_op jit(solution)/shard_map/ppermute | solution.py:1066
  69.2 28.5 %collective-permute-start.5 = (f32[768,384]{1,0:T(8,128)S(1)}, f32[768,384]{1,0:T(8,128)S(1)}, u32[]{:S(2)}, u32[]{:S(2)}) collective-permute-start(f32[768,384]{1,0:T(8,128)S(1)} %get-tuple-element.333.refs_0_), channel_id=1, source_target_pairs={{0,8},{2,10},{4,12},{6,14},{8,0},{10,2},{12,4},{14,6},{16,24},{18,... | collective-permute-start | bytes 3538952 | tf_op jit(solution)/shard_map/ppermute | solution.py:1066
  76.8 19.6 %collective-permute-start.9 = (f32[384,384]{1,0:T(8,128)S(1)}, f32[384,384]{1,0:T(8,128)S(1)}, u32[]{:S(2)}, u32[]{:S(2)}) collective-permute-start(f32[384,384]{1,0:T(8,128)S(1)} %get-tuple-element.341), channel_id=1, source_target_pairs={{0,1},{1,0},{2,3},{3,2},{4,5},{5,4},{6,7},{7,6},{8,9},{9,8},{10,11... | collective-permute-start | bytes 1769480 | tf_op jit(solution)/shard_map/ppermute | solution.py:1065
  77.2 23.8 %collective-permute-start.14 = (f32[1536,384]{1,0:T(8,128)S(1)}, f32[1536,384]{1,0:T(8,128)S(1)}, u32[]{:S(2)}, u32[]{:S(2)}) collective-permute-start(f32[1536,384]{1,0:T(8,128)S(1)} %get-tuple-element.350.refs_1_), channel_id=1, source_target_pairs={{0,2},{2,0},{4,6},{6,4},{8,10},{10,8},{12,14},{14,12},{16,18},{18,... | collective-permute-start | bytes 7077896 | tf_op jit(solution)/shard_map/ppermute | solution.py:1066
  98.4 18.2 %collective-permute-start.11 = (f32[1536,384]{1,0:T(8,128)S(1)}, f32[1536,384]{1,0:T(8,128)S(1)}, u32[]{:S(2)}, u32[]{:S(2)}) collective-permute-start(f32[1536,384]{1,0:T(8,128)S(1)} %get-tuple-element.347.refs_4_), channel_id=1, source_target_pairs={{0,2},{2,0},{4,6},{6,4},{8,10},{10,8},{12,14},{14,12},{16,18},{18,... | collective-permute-start | bytes 7077896 | tf_op jit(solution)/shard_map/ppermute | solution.py:1066
  99.0 53.4 %collective-permute-start.18 = (f32[1536,384]{1,0:T(8,128)}, f32[1536,384]{1,0:T(8,128)S(1)}, u32[]{:S(2)}, u32[]{:S(2)}) collective-permute-start(f32[1536,384]{1,0:T(8,128)} %get-tuple-element.378), channel_id=1, source_target_pairs={{0,1},{1,0},{2,3},{3,2},{4,5},{5,4},{6,7},{7,6},{8,9},{9,8},{10,11... | collective-permute-start | bytes 7077896 | tf_op jit(solution)/shard_map/ppermute | solution.py:1065
  116.1 26.9 %collective-permute-start.16 = (f32[768,384]{1,0:T(8,128)S(1)}, f32[768,384]{1,0:T(8,128)S(1)}, u32[]{:S(2)}, u32[]{:S(2)}) collective-permute-start(f32[768,384]{1,0:T(8,128)S(1)} %get-tuple-element.365.refs_0_), channel_id=1, source_target_pairs={{0,8},{2,10},{4,12},{6,14},{8,0},{10,2},{12,4},{14,6},{16,24},{18,... | collective-permute-start | bytes 3538952 | tf_op jit(solution)/shard_map/ppermute | solution.py:1066
  117.9 26.6 %collective-permute-start.19 = (f32[768,384]{1,0:T(8,128)S(1)}, f32[768,384]{1,0:T(8,128)S(1)}, u32[]{:S(2)}, u32[]{:S(2)}) collective-permute-start(f32[768,384]{1,0:T(8,128)S(1)} %get-tuple-element.379.refs_0_), channel_id=1, source_target_pairs={{0,4},{2,6},{4,0},{6,2},{8,12},{10,14},{12,8},{14,10},{16,20},{18,... | collective-permute-start | bytes 3538952 | tf_op jit(solution)/shard_map/ppermute | solution.py:1066
  197.0 28.6 %collective-permute-start.27 = (f32[1,384,768]{2,1,0:T(8,128)}, f32[1,384,768]{2,1,0:T(8,128)S(1)}, u32[]{:S(2)}, u32[]{:S(2)}) collective-permute-start(f32[1,384,768]{2,1,0:T(8,128)} %get-tuple-element.451), channel_id=1, source_target_pairs={{0,1},{1,0},{2,3},{3,2},{4,5},{5,4},{6,7},{7,6},{8,9},{9,8},{10,11... | collective-permute-start | bytes 3538952 | tf_op jit(solution)/shard_map/ppermute | solution.py:1065
  198.5 28.3 %collective-permute-start.26 = (f32[2,192,768]{2,1,0:T(8,128)}, f32[2,192,768]{2,1,0:T(8,128)S(1)}, u32[]{:S(2)}, u32[]{:S(2)}) collective-permute-start(f32[2,192,768]{2,1,0:T(8,128)} %get-tuple-element.449), channel_id=1, source_target_pairs={{0,8},{2,10},{4,12},{6,14},{8,0},{10,2},{12,4},{14,6},{16,24},{18,... | collective-permute-start | bytes 3538952 | tf_op jit(solution)/shard_map/ppermute | solution.py:1066
  233.4 43.3 %collective-permute-start.38 = (f32[2,192,768]{2,1,0:T(8,128)S(1)}, f32[2,192,768]{2,1,0:T(8,128)S(1)}, u32[]{:S(2)}, u32[]{:S(2)}) collective-permute-start(f32[2,192,768]{2,1,0:T(8,128)S(1)} %get-tuple-element.487), channel_id=1, source_target_pairs={{0,8},{2,10},{4,12},{6,14},{8,0},{10,2},{12,4},{14,6},{16,24},{18,... | collective-permute-start | bytes 3538952 | tf_op jit(solution)/shard_map/ppermute | solution.py:1066
  242.2 35.1 %collective-permute-start.37 = (f32[2,192,768]{2,1,0:T(8,128)S(1)}, f32[2,192,768]{2,1,0:T(8,128)S(1)}, u32[]{:S(2)}, u32[]{:S(2)}) collective-permute-start(f32[2,192,768]{2,1,0:T(8,128)S(1)} %get-tuple-element.485), channel_id=1, source_target_pairs={{0,4},{2,6},{4,0},{6,2},{8,12},{10,14},{12,8},{14,10},{16,20},{18,... | collective-permute-start | bytes 3538952 | tf_op jit(solution)/shard_map/ppermute | solution.py:1066
  247.2 17.9 %collective-permute-start.33 = (f32[1,96,768]{2,1,0:T(8,128)S(1)}, f32[1,96,768]{2,1,0:T(8,128)S(1)}, u32[]{:S(2)}, u32[]{:S(2)}) collective-permute-start(f32[1,96,768]{2,1,0:T(8,128)S(1)} %get-tuple-element.477), channel_id=1, source_target_pairs={{0,16},{2,18},{4,20},{6,22},{8,24},{10,26},{12,28},{14,30},{16,0},... | collective-permute-start | bytes 884744 | tf_op jit(solution)/shard_map/ppermute | solution.py:1066
  249.9 42.0 %collective-permute-start.28 = (f32[1,384,768]{2,1,0:T(8,128)S(1)}, f32[1,384,768]{2,1,0:T(8,128)S(1)}, u32[]{:S(2)}, u32[]{:S(2)}) collective-permute-start(f32[1,384,768]{2,1,0:T(8,128)S(1)} %get-tuple-element.458), channel_id=1, source_target_pairs={{0,1},{1,0},{2,3},{3,2},{4,5},{5,4},{6,7},{7,6},{8,9},{9,8},{10,11... | collective-permute-start | bytes 3538952 | tf_op jit(solution)/shard_map/ppermute | solution.py:1065
  251.1 52.9 %collective-permute-start.45 = (f32[1,384,768]{2,1,0:T(8,128)S(1)}, f32[1,384,768]{2,1,0:T(8,128)S(1)}, u32[]{:S(2)}, u32[]{:S(2)}) collective-permute-start(f32[1,384,768]{2,1,0:T(8,128)S(1)} %get-tuple-element.507), channel_id=1, source_target_pairs={{0,1},{1,0},{2,3},{3,2},{4,5},{5,4},{6,7},{7,6},{8,9},{9,8},{10,11... | collective-permute-start | bytes 3538952 | tf_op jit(solution)/shard_map/ppermute | solution.py:1065
  278.0 22.6 %collective-permute-start.41 = (f32[2,96,768]{2,1,0:T(8,128)S(1)}, f32[2,96,768]{2,1,0:T(8,128)S(1)}, u32[]{:S(2)}, u32[]{:S(2)}) collective-permute-start(f32[2,96,768]{2,1,0:T(8,128)S(1)} %get-tuple-element.498), channel_id=1, source_target_pairs={{0,8},{2,10},{4,12},{6,14},{8,0},{10,2},{12,4},{14,6},{16,24},{18,... | collective-permute-start | bytes 1769480 | tf_op jit(solution)/shard_map/ppermute | solution.py:1066
  290.0 17.2 %collective-permute-start.43 = (f32[2,96,768]{2,1,0:T(8,128)S(1)}, f32[2,96,768]{2,1,0:T(8,128)S(1)}, u32[]{:S(2)}, u32[]{:S(2)}) collective-permute-start(f32[2,96,768]{2,1,0:T(8,128)S(1)} %get-tuple-element.503), channel_id=1, source_target_pairs={{0,4},{2,6},{4,0},{6,2},{8,12},{10,14},{12,8},{14,10},{16,20},{18,... | collective-permute-start | bytes 1769480 | tf_op jit(solution)/shard_map/ppermute | solution.py:1066
  308.8 19.1 %collective-permute-start.40 = (f32[1,192,768]{2,1,0:T(8,128)S(1)}, f32[1,192,768]{2,1,0:T(8,128)S(1)}, u32[]{:S(2)}, u32[]{:S(2)}) collective-permute-start(f32[1,192,768]{2,1,0:T(8,128)S(1)} %get-tuple-element.496), channel_id=1, source_target_pairs={{0,4},{2,6},{4,0},{6,2},{8,12},{10,14},{12,8},{14,10},{16,20},{18,... | collective-permute-start | bytes 1769480 | tf_op jit(solution)/shard_map/ppermute | solution.py:1066
  309.7 23.4 %collective-permute-start.52 = (f32[1,192,768]{2,1,0:T(8,128)S(1)}, f32[1,192,768]{2,1,0:T(8,128)S(1)}, u32[]{:S(2)}, u32[]{:S(2)}) collective-permute-start(f32[1,192,768]{2,1,0:T(8,128)S(1)} %get-tuple-element.534.refs_0_), channel_id=1, source_target_pairs={{0,8},{2,10},{4,12},{6,14},{8,0},{10,2},{12,4},{14,6},{16,24},{18,... | collective-permute-start | bytes 1769480 | tf_op jit(solution)/shard_map/ppermute | solution.py:1066
  316.8 67.7 %collective-permute-start.66 = (f32[512,768]{1,0:T(8,128)S(1)}, f32[512,768]{1,0:T(8,128)S(1)}, u32[]{:S(2)}, u32[]{:S(2)}) collective-permute-start(f32[512,768]{1,0:T(8,128)S(1)} %get-tuple-element.562), channel_id=1, source_target_pairs={{0,1},{1,0},{2,3},{3,2},{4,5},{5,4},{6,7},{7,6},{8,9},{9,8},{10,11... | collective-permute-start | bytes 4718600 | tf_op jit(solution)/shard_map/ppermute | solution.py:1065
  319.7 18.0 %collective-permute-start.51 = (f32[1,192,768]{2,1,0:T(8,128)S(1)}, f32[1,192,768]{2,1,0:T(8,128)S(1)}, u32[]{:S(2)}, u32[]{:S(2)}) collective-permute-start(f32[1,192,768]{2,1,0:T(8,128)S(1)} %get-tuple-element.533), channel_id=1, source_target_pairs={{0,4},{2,6},{4,0},{6,2},{8,12},{10,14},{12,8},{14,10},{16,20},{18,... | collective-permute-start | bytes 1769480 | tf_op jit(solution)/shard_map/ppermute | solution.py:1066
  327.9 27.9 %collective-permute-start.56 = (f32[1,192,768]{2,1,0:T(8,128)S(1)}, f32[1,192,768]{2,1,0:T(8,128)S(1)}, u32[]{:S(2)}, u32[]{:S(2)}) collective-permute-start(f32[1,192,768]{2,1,0:T(8,128)S(1)} %get-tuple-element.543.refs_0_), channel_id=1, source_target_pairs={{0,4},{2,6},{4,0},{6,2},{8,12},{10,14},{12,8},{14,10},{16,20},{18,... | collective-permute-start | bytes 1769480 | tf_op jit(solution)/shard_map/ppermute | solution.py:1066
  338.3 20.1 %collective-permute-start.55 = (f32[1,96,768]{2,1,0:T(8,128)S(1)}, f32[1,96,768]{2,1,0:T(8,128)S(1)}, u32[]{:S(2)}, u32[]{:S(2)}) collective-permute-start(f32[1,96,768]{2,1,0:T(8,128)S(1)} %get-tuple-element.542), channel_id=1, source_target_pairs={{0,8},{2,10},{4,12},{6,14},{8,0},{10,2},{12,4},{14,6},{16,24},{18,... | collective-permute-start | bytes 884744 | tf_op jit(solution)/shard_map/ppermute | solution.py:1066
  363.1 34.4 %collective-permute-start.39 = (f32[512,768]{1,0:T(8,128)S(1)}, f32[512,768]{1,0:T(8,128)S(1)}, u32[]{:S(2)}, u32[]{:S(2)}) collective-permute-start(f32[512,768]{1,0:T(8,128)S(1)} %get-tuple-element.494), channel_id=1, source_target_pairs={{0,1},{1,0},{2,3},{3,2},{4,5},{5,4},{6,7},{7,6},{8,9},{9,8},{10,11... | collective-permute-start | bytes 4718600 | tf_op jit(solution)/shard_map/ppermute | solution.py:1065
  366.2 17.7 %collective-permute-start.64 = (f32[1,96,768]{2,1,0:T(8,128)S(1)}, f32[1,96,768]{2,1,0:T(8,128)S(1)}, u32[]{:S(2)}, u32[]{:S(2)}) collective-permute-start(f32[1,96,768]{2,1,0:T(8,128)S(1)} %get-tuple-element.559.refs_0_), channel_id=1, source_target_pairs={{0,16},{2,18},{4,20},{6,22},{8,24},{10,26},{12,28},{14,30},{16,0},... | collective-permute-start | bytes 884744 | tf_op jit(solution)/shard_map/ppermute | solution.py:1066
  369.0 25.5 %collective-permute-start.63 = (f32[1,192,768]{2,1,0:T(8,128)S(1)}, f32[1,192,768]{2,1,0:T(8,128)S(1)}, u32[]{:S(2)}, u32[]{:S(2)}) collective-permute-start(f32[1,192,768]{2,1,0:T(8,128)S(1)} %get-tuple-element.558.refs_0_), channel_id=1, source_target_pairs={{0,4},{2,6},{4,0},{6,2},{8,12},{10,14},{12,8},{14,10},{16,20},{18,... | collective-permute-start | bytes 1769480 | tf_op jit(solution)/shard_map/ppermute | solution.py:1066
  396.6 19.2 %collective-permute-start.69 = (f32[1,384,768]{2,1,0:T(8,128)S(1)}, f32[1,384,768]{2,1,0:T(8,128)S(1)}, u32[]{:S(2)}, u32[]{:S(2)}) collective-permute-start(f32[1,384,768]{2,1,0:T(8,128)S(1)} %get-tuple-element.575.refs_0_), channel_id=1, source_target_pairs={{0,2},{2,0},{4,6},{6,4},{8,10},{10,8},{12,14},{14,12},{16,18},{18,... | collective-permute-start | bytes 3538952 | tf_op jit(solution)/shard_map/ppermute | solution.py:1066
  397.5 20.3 %collective-permute-start.68 = (f32[1,192,768]{2,1,0:T(8,128)S(1)}, f32[1,192,768]{2,1,0:T(8,128)S(1)}, u32[]{:S(2)}, u32[]{:S(2)}) collective-permute-start(f32[1,192,768]{2,1,0:T(8,128)S(1)} %get-tuple-element.574.refs_0_), channel_id=1, source_target_pairs={{0,4},{2,6},{4,0},{6,2},{8,12},{10,14},{12,8},{14,10},{16,20},{18,... | collective-permute-start | bytes 1769480 | tf_op jit(solution)/shard_map/ppermute | solution.py:1066
  398.3 21.1 %collective-permute-start.75 = (f32[1,192,768]{2,1,0:T(8,128)S(1)}, f32[1,192,768]{2,1,0:T(8,128)S(1)}, u32[]{:S(2)}, u32[]{:S(2)}) collective-permute-start(f32[1,192,768]{2,1,0:T(8,128)S(1)} %get-tuple-element.589.refs_0_), channel_id=1, source_target_pairs={{0,8},{2,10},{4,12},{6,14},{8,0},{10,2},{12,4},{14,6},{16,24},{18,... | collective-permute-start | bytes 1769480 | tf_op jit(solution)/shard_map/ppermute | solution.py:1066
  (103 other events, 816.5 us)
